TPU v7x, 256 devices: a whole 4x4x8 slice. The times are simulated.
256 devices in a mesh: dp: 32 (over y_hi, z, core), tensor: 8 (over y_lo, x).
Axes of the slice: x: 4, y: 4 (y_hi: 2, y_lo: 2; y = y_hi * 2 + y_lo), z: 8, core: 2. Of those that a mesh axis runs over, the one named last changes fastest.
Arguments:
- tokens: bfloat16 [8192, 1024], P('dp'), may hold values from -6 to 6
- gain: float32 [1024], replicated, may hold values from 0.1 to 1.9
- w_query: bfloat16 [1024, 8192], P(None, 'tensor'), may hold values from -1 to 1, as said below
- w_key: bfloat16 [1024, 8192], P(None, 'tensor'), may hold values from -1 to 1, as said below
- w_value: bfloat16 [1024, 8192], P(None, 'tensor'), may hold values from -0.1875 to 0.1875
- w_output: bfloat16 [8192, 1024], P('tensor'), may hold values from -0.0625 to 0.0625
- encoder: bfloat16 [1024, 256], replicated, may hold values from -0.1875 to 0.1875
- decoder: bfloat16 [256, 1024], replicated, may hold values from -0.375 to 0.375
- cotangent: bfloat16 [8192, 1024], P('dp'), may hold values from -6 to 6
Outputs:
- output: bfloat16 [8192, 1024], P('dp')
- grad_input: bfloat16 [8192, 1024], P('dp')
- grad_gain: float32 [1024], P(('dp', 'tensor'))
- grad_query: float32 [1024, 8192], P('dp', 'tensor')
- grad_key: float32 [1024, 8192], P('dp', 'tensor')
- grad_value: float32 [1024, 8192], P('dp', 'tensor')
- grad_output: float32 [8192, 1024], P('tensor', 'dp')
- grad_encoder: float32 [1024, 256], P(('dp', 'tensor'))
- grad_decoder: float32 [256, 1024], P('dp')
Inputs may be any that keep to these rules, and one draw needn't show every extreme that they name: `w_query`: independent entries, mean zero. `w_key`: independent entries, mean zero.
All inputs are finite; a program needn't handle non-finite values.
Results may differ from a plain program's by a relative error of at most 0.024.
Values may be sent and summed in bfloat16 or wider, within the bound.
No kernel may reach another device: no remote copies, remote signals or barrier semaphores. Data moves between devices by JAX's collectives and lax.ppermute only.
A program may use at most 128 MiB of HBM per device.

v0:
```python
import jax
import jax.numpy as jnp
from jax import lax
from jax.sharding import PartitionSpec as P

DK = 128
SEQ_LEN = 256


def on_device(tokens, gain, w_query, w_key, w_value, w_output, encoder, decoder, cotangent):
    rows, width = tokens.shape
    seqs_here = rows // SEQ_LEN
    heads_here = w_query.shape[1] // DK
    scale = DK ** (-0.5)
    xfloat = tokens.astype(jnp.float32)
    rms = lax.rsqrt(jnp.mean(xfloat * xfloat, axis=-1, keepdims=True) + 1e-06)
    unit = xfloat * rms
    normed = (unit * gain).astype(jnp.bfloat16)
    query = jnp.dot(normed, w_query, preferred_element_type=jnp.float32).astype(jnp.bfloat16)
    key = jnp.dot(normed, w_key, preferred_element_type=jnp.float32).astype(jnp.bfloat16)
    value = jnp.dot(normed, w_value, preferred_element_type=jnp.float32).astype(jnp.bfloat16)

    def split_heads(a):
        return a.reshape(seqs_here, SEQ_LEN, heads_here, DK)

    query4 = split_heads(query)
    key4 = split_heads(key)
    value4 = split_heads(value)
    scores = jnp.einsum("sqhd,skhd->shqk", query4, key4, preferred_element_type=jnp.float32) * scale
    causal = jnp.arange(SEQ_LEN)[:, None] >= jnp.arange(SEQ_LEN)[None, :]
    masked = jnp.where(causal[None, None], scores, -1e30)
    top = jnp.max(masked, axis=-1, keepdims=True)
    expo = jnp.exp(masked - top)
    probs = expo / jnp.sum(expo, axis=-1, keepdims=True)
    probs_low = probs.astype(jnp.bfloat16)
    context = jnp.einsum("shqk,skhd->sqhd", probs_low, value4, preferred_element_type=jnp.float32)
    context = context.astype(jnp.bfloat16).reshape(rows, heads_here * DK)
    partial_value = jnp.dot(context, w_output, preferred_element_type=jnp.float32).astype(
        jnp.bfloat16
    )
    code_term = jnp.dot(partial_value, encoder, preferred_element_type=jnp.float32)
    code = lax.psum(code_term, "tensor").astype(jnp.bfloat16)
    output = (xfloat + jnp.dot(code, decoder, preferred_element_type=jnp.float32)).astype(
        jnp.bfloat16
    )
    dcode = jnp.dot(cotangent, decoder.T, preferred_element_type=jnp.float32).astype(jnp.bfloat16)
    grad_dec_term = jnp.dot(code.T, cotangent, preferred_element_type=jnp.float32)
    grad_enc_term = jnp.dot(partial_value.T, dcode, preferred_element_type=jnp.float32)
    dpartial = jnp.dot(dcode, encoder.T, preferred_element_type=jnp.float32).astype(jnp.bfloat16)
    grad_out_term = jnp.dot(context.T, dpartial, preferred_element_type=jnp.float32)
    dcontext = jnp.dot(dpartial, w_output.T, preferred_element_type=jnp.float32).astype(
        jnp.bfloat16
    )
    dcontext4 = split_heads(dcontext)
    dprobs = jnp.einsum("sqhd,skhd->shqk", dcontext4, value4, preferred_element_type=jnp.float32)
    dvalue = jnp.einsum(
        "shqk,sqhd->skhd", probs_low, dcontext4, preferred_element_type=jnp.float32
    ).astype(jnp.bfloat16)
    delta = jnp.sum(dprobs * probs, axis=-1, keepdims=True)
    dscores = (probs * (dprobs - delta) * scale).astype(jnp.bfloat16)
    dquery = jnp.einsum(
        "shqk,skhd->sqhd", dscores, key4, preferred_element_type=jnp.float32
    ).astype(jnp.bfloat16)
    dkey = jnp.einsum(
        "shqk,sqhd->skhd", dscores, query4, preferred_element_type=jnp.float32
    ).astype(jnp.bfloat16)
    dquery = dquery.reshape(rows, heads_here * DK)
    dkey = dkey.reshape(rows, heads_here * DK)
    dvalue = dvalue.reshape(rows, heads_here * DK)
    dnormed_term = jnp.dot(dquery, w_query.T, preferred_element_type=jnp.float32)
    dnormed_term = dnormed_term + jnp.dot(dkey, w_key.T, preferred_element_type=jnp.float32)
    dnormed_term = dnormed_term + jnp.dot(dvalue, w_value.T, preferred_element_type=jnp.float32)
    grad_q_term = jnp.dot(normed.T, dquery, preferred_element_type=jnp.float32)
    grad_k_term = jnp.dot(normed.T, dkey, preferred_element_type=jnp.float32)
    grad_v_term = jnp.dot(normed.T, dvalue, preferred_element_type=jnp.float32)
    position = lax.axis_index("tensor")
    block = width // lax.axis_size("tensor")
    dnormed = lax.psum(dnormed_term, "tensor")
    dunit = dnormed * gain
    inner = jnp.sum(dunit * unit, axis=-1, keepdims=True) / width
    grad_input = (cotangent.astype(jnp.float32) + rms * (dunit - unit * inner)).astype(jnp.bfloat16)
    gain_full = jnp.sum(dnormed * unit, axis=0)
    owned = jnp.arange(width) // block == position
    gain_term = jnp.where(owned, gain_full, 0.0)
    grad_gain, grad_encoder = (
        lax.psum_scatter(gain_term, ("dp", "tensor"), scatter_dimension=0, tiled=True),
        lax.psum_scatter(grad_enc_term, ("dp", "tensor"), scatter_dimension=0, tiled=True),
    )
    grad_query, grad_key, grad_value, grad_output, grad_decoder = (
        lax.psum_scatter(
            grad_q_term.astype(jnp.bfloat16), "dp", scatter_dimension=0, tiled=True
        ).astype(jnp.float32),
        lax.psum_scatter(
            grad_k_term.astype(jnp.bfloat16), "dp", scatter_dimension=0, tiled=True
        ).astype(jnp.float32),
        lax.psum_scatter(
            grad_v_term.astype(jnp.bfloat16), "dp", scatter_dimension=0, tiled=True
        ).astype(jnp.float32),
        lax.psum_scatter(
            grad_out_term.astype(jnp.bfloat16), "dp", scatter_dimension=1, tiled=True
        ).astype(jnp.float32),
        lax.psum_scatter(
            grad_dec_term.astype(jnp.bfloat16), "dp", scatter_dimension=0, tiled=True
        ).astype(jnp.float32),
    )
    return (
        output,
        grad_input,
        grad_gain,
        grad_query,
        grad_key,
        grad_value,
        grad_output,
        grad_encoder,
        grad_decoder,
    )


def solution(mesh):
    return jax.shard_map(
        on_device,
        mesh=mesh,
        in_specs=(
            P("dp", None),
            P(),
            P(None, "tensor"),
            P(None, "tensor"),
            P(None, "tensor"),
            P("tensor", None),
            P(),
            P(),
            P("dp", None),
        ),
        out_specs=(
            P("dp", None),
            P("dp", None),
            P(("dp", "tensor")),
            P("dp", "tensor"),
            P("dp", "tensor"),
            P("dp", "tensor"),
            P("tensor", "dp"),
            P(("dp", "tensor"), None),
            P("dp", None),
        ),
        check_vma=False,
    )
```

profile of v0, /device:TPU:1, one launch (start us, length us, event | category | flops | bytes accessed | tf_op | source)
XLA Modules:
  0.0 679.8 jit_solution(13248213682470093382)
XLA Ops:
  8.1 1.4 fusion.31
  9.5 2.6 convolution_convert_fusion.11
  12.1 1.0 copy.46
  13.1 3.1 convolution_convert_fusion.10
  16.2 2.1 copy.47
  18.4 3.2 fusion.23
  21.9 3.4 fusion.65
  25.3 2.1 convolution_convert_fusion.9
  27.5 0.8 copy-done.11
  28.3 0.7 convolution_convert_fusion.8
  29.1 0.8 copy-done.3
  29.9 1.3 fusion.68
  31.3 2.2 fusion.66
  33.5 31.4 %all-reduce.9 = bf16[256,256]{1,0:T(8,128)(2,1)S(1)} all-reduce(f32[256,256]{1,0:T(8,128)} %fusion.66), channel_id=1, replica_groups=mesh['dp'=32,'tensor'=8] {'tensor'}, use_global_device_ids=true, to_apply=%region_3.4 | all-reduce | flops 65536 | bytes 393216 | tf_op jit(solution)/shard_map/psum | solution.py:42
  64.8 1.2 convolution_convert_fusion.4
  66.1 1.4 convolution_convert_fusion.5
  67.5 0.8 copy-done.9
  68.2 1.5 convolution_convert_fusion.7
  69.8 2.1 copy.48
  71.8 2.9 fusion.38
  74.8 5.2 fusion.20
  80.0 5.2 fusion.17
  85.2 2.7 fusion.67
  87.9 0.8 convolution_add_fusion.1
  88.9 0.8 copy-done.13
  89.7 0.5 convolution_convert_fusion.6
  90.2 0.8 copy-done.7
  91.0 0.5 copy-done.5
  91.5 1.7 convolution_add_fusion
  93.3 3.2 convolution_convert_fusion.2
  96.8 3.2 convolution_convert_fusion.3
  100.1 3.2 convolution_convert_fusion.1
  103.4 3.3 convolution_convert_fusion
  106.7 2.1 fusion.16
  108.9 181.8 %all-reduce.8.cloned.1.call-done = f32[1024,256]{1,0:T(8,128)} async-done(((f32[1024,256]{1,0:T(8,128)}), f32[1024,256]{1,0:T(8,128)}) %all-reduce.8.cloned.1.call-update) | async-done | bytes 1048592
  290.6 1.3 constant_dynamic-slice_fusion
  291.9 1.3 convert_element_type.149
  293.3 77.8 %all-reduce.6.cloned.1.call-done = f32[256,1024]{1,0:T(8,128)} async-done(((f32[256,1024]{1,0:T(8,128)}), f32[256,1024]{1,0:T(8,128)}) %all-reduce.6.cloned.1.call-update) | async-done | bytes 1048592 | tf_op jit(solution)/shard_map/psum | solution.py:78
  371.1 1.7 fusion.30
  372.8 80.4 %all-reduce = f32[1024]{0:T(1024)S(1)} all-reduce(f32[1024]{0:T(1024)S(1)} %fusion.52), channel_id=2, replica_groups=mesh['dp'=32,'tensor'=8] {'dp','tensor'}, use_global_device_ids=true, to_apply=%region_8.9.clone | all-reduce | flops 1024 | bytes 8192
  453.2 0.6 dynamic-slice
  453.8 2.4 fusion.29
  456.1 1.5 convert_element_type.143
  457.6 1.5 convert_element_type.141
  459.2 89.7 %reduce-scatter.10.cloned.1.call-done = bf16[32,1024]{1,0:T(8,128)(2,1)} async-done(((bf16[1024,1024]{1,0:T(8,128)(2,1)}), bf16[32,1024]{1,0:T(8,128)(2,1)}) %reduce-scatter.10.cloned.1.call-update) | async-done | bytes 65552 | tf_op jit(solution)/shard_map/reduce_scatter | solution.py:96
  548.9 1.5 convert_element_type.145
  550.4 120.3 %reduce-scatter.12.cloned.1.call-done = bf16[1024,32]{0,1:T(8,128)(2,1)} async-done(((bf16[1024,1024]{0,1:T(8,128)(2,1)}), bf16[1024,32]{0,1:T(8,128)(2,1)}) %reduce-scatter.12.cloned.1.call-update) | async-done | bytes 65552 | tf_op jit(solution)/shard_map/reduce_scatter | solution.py:99
  670.7 1.5 convert_element_type.147
  (44 shorter events, 1.3 us)
Async XLA Ops:
  8.0 20.3 %copy-start = (bf16[1024,1024]{1,0:T(8,128)(2,1)S(1)}, bf16[1024,1024]{1,0:T(8,128)(2,1)}, u32[]{:S(2)}) copy-start(bf16[1024,1024]{1,0:T(8,128)(2,1)} %param.14) | copy-start | bytes 6291460
  8.0 282.6 %all-reduce.8.cloned.1.call-start = ((), (), s32[]{:S(2)}) async-start(), calls=%async_computation.11 | async-start | bytes 2097152
  9.5 3.6 copy-start.1
  9.5 3.6 copy-start.12
  16.2 5.3 copy-start.2
  18.4 3.2 copy-start.6
  27.5 0.8 copy-start.11
  29.1 0.8 copy-start.3
  31.2 260.7 %reduce-scatter.14.cloned.1.call-start = ((), (), s32[]{:S(2)}) async-start(), calls=%async_computation.10 | async-start | bytes 540672 | tf_op jit(solution)/shard_map/reduce_scatter | solution.py:102
  66.0 305.0 %all-reduce.6.cloned.1.call-start = ((), (), s32[]{:S(2)}) async-start(), calls=%async_computation.5 | async-start | bytes 2097152 | tf_op jit(solution)/shard_map/psum | solution.py:78
  67.5 0.8 copy-start.9
  85.2 2.7 copy-start.4
  85.2 2.7 copy-start.8
  87.9 1.0 copy-start.10
  87.9 1.8 copy-start.13
  89.7 1.8 copy-start.5
  90.2 0.8 copy-start.7
  93.3 362.9 %reduce-scatter.8.cloned.1.call-start = ((), (), s32[]{:S(2)}) async-start(), calls=%async_computation.7 | async-start | bytes 2162688 | tf_op jit(solution)/shard_map/reduce_scatter | solution.py:93
  96.6 361.1 %reduce-scatter.6.cloned.1.call-start = ((), (), s32[]{:S(2)}) async-start(), calls=%async_computation.6 | async-start | bytes 2162688 | tf_op jit(solution)/shard_map/reduce_scatter | solution.py:90
  100.0 448.9 %reduce-scatter.10.cloned.1.call-start = ((), (), s32[]{:S(2)}) async-start(), calls=%async_computation.8 | async-start | bytes 2162688 | tf_op jit(solution)/shard_map/reduce_scatter | solution.py:96
  103.3 567.4 %reduce-scatter.12.cloned.1.call-start = ((), (), s32[]{:S(2)}) async-start(), calls=%async_computation.9 | async-start | bytes 2162688 | tf_op jit(solution)/shard_map/reduce_scatter | solution.py:99
Sparse Core Ops, SparseCore 0:
  31.3 259.2 all-reduce.7
  293.5 77.5 all-reduce.5
Sparse Core Ops, SparseCore 1:
  66.1 116.0 reduce-scatter.13
  186.2 117.5 reduce-scatter.7
  308.3 119.8 reduce-scatter.5
  432.3 116.5 reduce-scatter.9
  553.6 117.0 reduce-scatter.11
where the time goes:
time: 686 us; the launch traced here: 680 us
  waiting for transfers between devices  470 us (69%)
  blocking collectives  112 us (16%)
  matrix products  57.3 us (8%)
  between operations  15.9 us (2%)
  other arithmetic  12.8 us (2%)
  local copies, waits for them, and re-layouts  11.8 us (2%)
    unnamed x8, waiting for transfers between devices  182 us
    reduce_scatter x1, waiting for transfers between devices, on_device(): lax.psum_scatter(grad_out_term.astype(jnp.bfloat16), 'dp', scatter_dimens...  120 us
    reduce_scatter x1, waiting for transfers between devices, on_device(): lax.psum_scatter(grad_v_term.astype(jnp.bfloat16), 'dp', scatter_dimensio...  89.7 us
    unnamed x1, blocking collectives  80.4 us
    psum x1, waiting for transfers between devices, on_device(): dnormed = lax.psum(dnormed_term, 'tensor')  77.8 us
    psum x1, blocking collectives, on_device(): code = lax.psum(code_term, 'tensor').astype(jnp.bfloat16)  31.4 us
  transfers between devices with their start and end apart: 7, of which 4 were waited for; matrix products, arithmetic and copies ran while one was open for 8% of the time, Pallas kernels for 0%

commit v1 on v0

v1 whole, which is shorter than its diff:
```python
import jax
import jax.numpy as jnp
import numpy as np
from jax import lax
from jax.experimental import pallas as pl
from jax.experimental.pallas import tpu as pltpu
from jax.sharding import Mesh
from jax.sharding import PartitionSpec as P

DK = 128
SEQ = 256
YH, Z, CORES, YL, X = 2, 8, 2, 2, 4
NT = YL * X
TP = ("yl", "x")
F32 = jnp.float32
BF16 = jnp.bfloat16
SWAP = [(0, 1), (1, 0)]


def dot(a, b, ca=1, cb=0):
    return lax.dot_general(a, b, (((ca,), (cb,)), ((), ())), preferred_element_type=F32)


def forward_kernel(
    core_ref,
    tok_own,
    tok_oth,
    gain,
    wq,
    wk,
    wv,
    wo,
    enc,
    dec,
    cot_own,
    cot_oth,
    buf,
    normed_t,
    q_out,
    k_out,
    ds_out,
    dv_out,
    code_out,
    norm_s,
    dcode_s,
    v_s,
    dctx_s,
    ctx_s,
):
    own = wq.shape[1]
    heads = own // DK
    rows = tok_own.shape[1] // (YH * Z)
    gz = own // 2 // Z
    for s, tok in enumerate((tok_own, tok_oth)):
        x = tok[...].astype(F32)
        rms = lax.rsqrt(jnp.mean(x * x, axis=-1, keepdims=True) + 1e-6)
        norm_s[s * SEQ : (s + 1) * SEQ, :] = (x * rms * gain[...]).astype(BF16)
    dcode_s[0:SEQ, :] = dot(cot_own[...], dec[...], 1, 1).astype(BF16)
    dcode_s[SEQ:, :] = dot(cot_oth[...], dec[...], 1, 1).astype(BF16)
    normed = norm_s[...]
    normed_t[...] = normed.T
    q_out[...] = dot(normed, wq[...]).astype(BF16)
    k_out[...] = dot(normed, wk[...]).astype(BF16)
    v_s[...] = dot(normed, wv[...]).astype(BF16)
    w2 = dot(wo[...], enc[...]).astype(BF16)
    dctx_s[...] = dot(dcode_s[...], w2, 1, 1).astype(BF16)
    scale = DK**-0.5
    row = lax.broadcasted_iota(jnp.int32, (SEQ, SEQ), 0)
    col = lax.broadcasted_iota(jnp.int32, (SEQ, SEQ), 1)
    causal = row >= col
    for s in range(2):
        for h in range(heads):
            at = (slice(s * SEQ, (s + 1) * SEQ), slice(h * DK, (h + 1) * DK))
            q, k, v, dctx = q_out[at], k_out[at], v_s[at], dctx_s[at]
            scores = jnp.where(causal, dot(q, k, 1, 1) * scale, -1e30)
            top = jnp.max(scores, axis=-1, keepdims=True)
            expo = jnp.exp(scores - top)
            probs = expo * (1.0 / jnp.sum(expo, axis=-1, keepdims=True))
            low = probs.astype(BF16)
            ctx_s[at] = dot(low, v).astype(BF16)
            dprobs = dot(dctx, v, 1, 1)
            dv_out[at] = dot(low, dctx, 0, 0).astype(BF16)
            delta = jnp.sum(dprobs * probs, axis=-1, keepdims=True)
            ds_out[s * heads + h] = (probs * (dprobs - delta) * scale).astype(BF16)
    code_out[...] = dot(ctx_s[...], w2)
    gv = dot(normed_t[...], dv_out[...]).astype(BF16)
    g = dot(ctx_s[...], dcode_s[...], 0, 0).astype(BF16)
    code = g.shape[1]
    for z in range(Z):
        for y in range(YH):
            at = (y * Z + z) * rows
            buf[z, y * rows : (y + 1) * rows, :] = gv[at : at + rows, :]
        buf[z, YH * rows :, 0:code] = g[z * gz : (z + 1) * gz, :]
        buf[z, YH * rows :, code:] = g[own // 2 + z * gz : own // 2 + (z + 1) * gz, :]


def backward_kernel(
    core_ref, normed_t, q_in, k_in, ds_in, dv, code, wq, wk, wv, buf, keep, send, dq_s, dk_s
):
    width = wq.shape[0]
    own = wq.shape[1]
    heads = own // DK
    rows = width // (YH * Z)
    for s in range(2):
        for h in range(heads):
            at = (slice(s * SEQ, (s + 1) * SEQ), slice(h * DK, (h + 1) * DK))
            ds = ds_in[s * heads + h]
            dq_s[at] = dot(ds, k_in[at]).astype(BF16)
            dk_s[at] = dot(ds, q_in[at], 0, 0).astype(BF16)
    for i, g_s in enumerate((dq_s, dk_s)):
        g = dot(normed_t[...], g_s[...]).astype(BF16)
        for z in range(Z):
            for y in range(YH):
                at = (y * Z + z) * rows
                buf[z, y * rows : (y + 1) * rows, i * own : (i + 1) * own] = g[at : at + rows, :]
    for s, out in enumerate((keep, send)):
        at = slice(s * SEQ, (s + 1) * SEQ)
        dn = dot(dq_s[at, :], wq[...], 1, 1)
        dn = dn + dot(dk_s[at, :], wk[...], 1, 1)
        dn = dn + dot(dv[at, :], wv[...], 1, 1)
        out[:, 0:width] = dn.astype(out.dtype)
        out[:, width:] = code[at, :].astype(out.dtype)


def whole(shape):
    return pl.BlockSpec(shape, lambda i, core: (0,) * len(shape))


def run_kernel(body, core, args, blocks, outs, scratch, flops):
    specs = [whole(a.shape) if b is None else b for a, b in zip(args, blocks, strict=True)]
    moved = sum(a.size * a.dtype.itemsize for a in (*args, *outs))
    return pl.pallas_call(
        body,
        grid_spec=pltpu.PrefetchScalarGridSpec(
            num_scalar_prefetch=1,
            grid=(1,),
            in_specs=specs,
            out_specs=[whole(o.shape) for o in outs],
            scratch_shapes=scratch,
        ),
        out_shape=outs,
        compiler_params=pltpu.CompilerParams(vmem_limit_bytes=56 * 1024 * 1024),
        cost_estimate=pl.CostEstimate(flops=flops, bytes_accessed=moved, transcendentals=0),
    )(core, *args)


def on_device(tokens, gain, w_query, w_key, w_value, w_output, encoder, decoder, cotangent):
    rows, width = tokens.shape
    own = w_query.shape[1] // CORES
    heads = own // DK
    code_w = encoder.shape[1]
    yh, z, c = lax.axis_index("yh"), lax.axis_index("z"), lax.axis_index("c")
    t = lax.axis_index("yl") * X + lax.axis_index("x")
    dp = (yh * Z + z) * CORES + c
    part = width // (YH * Z)
    fine = part // CORES
    sds = jax.ShapeDtypeStruct
    core = jnp.reshape(c, (1,)).astype(jnp.int32)

    tok_oth = lax.ppermute(tokens, "c", SWAP)
    cot_oth = lax.ppermute(cotangent, "c", SWAP)

    by_col = pl.BlockSpec((width, own), lambda i, core: (0, core[0]))
    by_row = pl.BlockSpec((own, width), lambda i, core: (core[0], 0))
    gz = own // 2 // Z
    buf_a, normed_t, query, key, dscores, dvalue, code_p = run_kernel(
        forward_kernel,
        core,
        (
            tokens,
            tok_oth,
            gain.reshape(1, width),
            w_query,
            w_key,
            w_value,
            w_output,
            encoder,
            decoder,
            cotangent,
            cot_oth,
        ),
        (None, None, None, by_col, by_col, by_col, by_row, None, None, None, None),
        (
            sds((Z, YH * part + gz, own), BF16),
            sds((width, 2 * SEQ), BF16),
            sds((2 * SEQ, own), BF16),
            sds((2 * SEQ, own), BF16),
            sds((2 * heads, SEQ, SEQ), BF16),
            sds((2 * SEQ, own), BF16),
            sds((2 * SEQ, code_w), F32),
        ),
        (
            pltpu.VMEM((2 * SEQ, width), BF16),
            pltpu.VMEM((2 * SEQ, code_w), BF16),
            pltpu.VMEM((2 * SEQ, own), BF16),
            pltpu.VMEM((2 * SEQ, own), BF16),
            pltpu.VMEM((2 * SEQ, own), BF16),
        ),
        5_000_000_000,
    )
    red_a = lax.psum_scatter(buf_a, "z", scatter_dimension=0, tiled=True)[0]

    buf_b, keep, send = run_kernel(
        backward_kernel,
        core,
        (normed_t, query, key, dscores, dvalue, code_p, w_query, w_key, w_value),
        (None, None, None, None, None, None, by_col, by_col, by_col),
        (
            sds((Z, YH * part, 2 * own), BF16),
            sds((SEQ, width + code_w), F32),
            sds((SEQ, width + code_w), BF16),
        ),
        (pltpu.VMEM((2 * SEQ, own), BF16), pltpu.VMEM((2 * SEQ, own), BF16)),
        3_000_000_000,
    )
    red_b = lax.psum_scatter(buf_b, "z", scatter_dimension=0, tiled=True)[0]

    both = (keep + lax.ppermute(send, "c", SWAP).astype(F32)).astype(BF16)
    piece = rows // NT
    got = lax.all_to_all(both.reshape(NT, piece, width + code_w), TP, 0, 0, tiled=True)
    total = jnp.sum(got.astype(F32), axis=0)
    dnormed = total[:, :width]
    x = lax.dynamic_slice_in_dim(tokens, t * piece, piece, 0).astype(F32)
    cot = lax.dynamic_slice_in_dim(cotangent, t * piece, piece, 0).astype(F32)
    rms = lax.rsqrt(jnp.mean(x * x, axis=-1, keepdims=True) + 1e-6)
    unit = x * rms
    dunit = dnormed * gain
    inner = jnp.sum(dunit * unit, axis=-1, keepdims=True) / width
    grad_rows = cot + rms * (dunit - unit * inner)
    gain_row = jnp.sum(dnormed * unit, axis=0)
    gain_by_t = gain_row.reshape(YH * Z * CORES, NT, width // (YH * Z * CORES * NT))
    gain_by_t = gain_by_t.transpose(1, 0, 2).reshape(NT, 1, -1)
    gain_w = gain_by_t.shape[2]
    first = jnp.concatenate([grad_rows, total[:, width:]], axis=1).astype(BF16)
    out_w = width + code_w
    second = jnp.pad(gain_by_t, ((0, 0), (0, 15), (0, out_w - gain_w))).astype(BF16)
    packed = jnp.concatenate(
        [jnp.broadcast_to(first[None], (NT, piece, out_w)), second], axis=1
    )
    got = lax.all_to_all(packed, TP, 0, 0, tiled=True)
    whole_rows = got[:, :piece].reshape(rows, out_w)
    grad_input = whole_rows[:, :width]
    code = whole_rows[:, width:]
    output = (tokens.astype(F32) + dot(code, decoder)).astype(BF16)
    gain_sum = jnp.sum(got[:, piece, :gain_w].astype(F32), axis=0).reshape(YH * Z, CORES, -1)
    gain_keep = lax.dynamic_index_in_dim(gain_sum, c, 1, keepdims=False)
    gain_send = lax.dynamic_index_in_dim(gain_sum, 1 - c, 1, keepdims=False)
    gain_keep = gain_keep + lax.ppermute(gain_send, "c", SWAP)

    code_oth = lax.ppermute(code, "c", SWAP)
    cols = width // NT
    cot_own_c = lax.dynamic_slice_in_dim(cotangent, t * cols, cols, 1)
    cot_oth_c = lax.dynamic_slice_in_dim(cot_oth, t * cols, cols, 1)
    dec_p = dot(code, cot_own_c, 0, 0) + dot(code_oth, cot_oth_c, 0, 0)
    dec_rows = code_w // (YH * Z * CORES)
    dec_p = dec_p.reshape(YH * Z, CORES, dec_rows, cols)
    dec_p = lax.dynamic_index_in_dim(dec_p, c, 1, keepdims=False)

    swap_rows = jnp.where(yh == 0, red_a[part : 2 * part], red_a[0:part])
    from_yh = lax.ppermute(jnp.concatenate([swap_rows, red_a[2 * part :]], axis=0), "yh", SWAP)
    mine = jnp.where(yh == 0, red_a[0:part], red_a[part : 2 * part])
    gv = (mine.astype(F32) + from_yh[:part].astype(F32)).astype(BF16)
    g = (red_a[2 * part :].astype(F32) + from_yh[part:].astype(F32)).astype(BF16)
    g = jnp.where(yh == 0, g[:, :code_w], g[:, code_w:])

    n_yz = YH * Z
    flat = jnp.concatenate(
        [
            jnp.broadcast_to(g.reshape(1, -1), (n_yz, gz * code_w)),
            dec_p.astype(BF16).reshape(n_yz, -1),
            jnp.pad(gain_keep, ((0, 0), (0, 128 - gain_keep.shape[1]))).astype(BF16),
        ],
        axis=1,
    )
    got = lax.all_to_all(flat, ("yh", "z"), 0, 0, tiled=True)
    g_size, d_size = gz * code_w, dec_rows * cols
    g_own = got[:, :g_size].reshape(own, code_w)
    tail = jnp.sum(got[:, g_size:].astype(F32), axis=0)
    dec_sum = tail[:d_size].reshape(dec_rows, cols)
    grad_gain = tail[d_size : d_size + gain_keep.shape[1]]
    g_oth = lax.ppermute(g_own, "c", SWAP)
    g_all = jnp.concatenate(
        [jnp.where(c == 0, g_own, g_oth), jnp.where(c == 0, g_oth, g_own)], axis=0
    )
    enc_rows = lax.dynamic_slice_in_dim(encoder, dp * fine, fine, 0)
    grad_output = dot(g_all, enc_rows, 1, 1)
    wo_cols = lax.dynamic_slice_in_dim(w_output, dp * fine, fine, 1)
    enc_p = dot(wo_cols, g_all, 0, 0)

    flat = jnp.concatenate(
        [
            jnp.broadcast_to(dec_sum.reshape(1, -1), (NT, d_size)),
            enc_p.reshape(NT, -1),
        ],
        axis=1,
    )
    got = lax.all_to_all(flat, TP, 0, 0, tiled=True)
    grad_decoder = got[:, :d_size].reshape(NT, dec_rows, cols).transpose(1, 0, 2)
    grad_decoder = grad_decoder.reshape(dec_rows, width)
    grad_encoder = jnp.sum(got[:, d_size:], axis=0).reshape(-1, code_w)

    swap_rows = jnp.where(yh == 0, red_b[part:], red_b[:part])
    mine = jnp.where(yh == 0, red_b[:part], red_b[part:])
    gqk = (mine.astype(F32) + lax.ppermute(swap_rows, "yh", SWAP).astype(F32)).astype(BF16)

    def over_cores(a):
        kept = jnp.where(c == 0, a[:fine], a[fine:])
        other = lax.ppermute(jnp.where(c == 0, a[fine:], a[:fine]), "c", SWAP)
        low = jnp.where(c == 0, kept, other).astype(F32)
        high = jnp.where(c == 0, other, kept).astype(F32)
        return low, high

    low, high = over_cores(gv)
    grad_value = jnp.concatenate([low, high], axis=1)
    low, high = over_cores(gqk)
    grad_query = jnp.concatenate([low[:, :own], high[:, :own]], axis=1)
    grad_key = jnp.concatenate([low[:, own:], high[:, own:]], axis=1)
    return (
        output,
        grad_input,
        grad_gain,
        grad_query,
        grad_key,
        grad_value,
        grad_output,
        grad_encoder,
        grad_decoder,
    )


def solution(mesh):
    devices = np.asarray(mesh.devices).reshape(YH, Z, CORES, YL, X)
    fine = Mesh(devices, ("yh", "z", "c", "yl", "x"))
    dp = ("yh", "z", "c")
    every = (*dp, *TP)
    return jax.shard_map(
        on_device,
        mesh=fine,
        in_specs=(
            P(dp, None),
            P(),
            P(None, TP),
            P(None, TP),
            P(None, TP),
            P(TP, None),
            P(),
            P(),
            P(dp, None),
        ),
        out_specs=(
            P(dp, None),
            P(dp, None),
            P(every),
            P(dp, TP),
            P(dp, TP),
            P(dp, TP),
            P(TP, dp),
            P(every, None),
            P(dp, None),
        ),
        check_vma=False,
    )
```

time: 686 us -> 161 us (0.23)
  waiting for transfers between devices: 470 us -> 53.2 us
  blocking collectives: 112 us -> 0 us
  matrix products: 57.3 us -> 6.15 us
  starting transfers between devices: 0.48 us -> 49 us
  Pallas kernels: 0 us -> 18.5 us
    reduce_scatter x5 -> x2, waiting for transfers between devices: 210 us -> 11.6 us  [the longest x1 7 us: on_device(): red_b = lax.psum_scatter(buf_b, 'z', scatter_dimension=0, tiled=True)[0]]
    unnamed x8 -> x2, waiting for transfers between devices: 182 us -> 1.36 us
    unnamed x1 -> x0, blocking collectives: 80.4 us -> none
    psum x1 -> x0, waiting for transfers between devices: 77.8 us -> none  [on_device(): dnormed = lax.psum(dnormed_term, 'tensor')]
    dot_general x23 -> x5, matrix products: 53.9 us -> 6.15 us  [dot(): lax.dot_general(a, b, (((ca,), (cb,)), ((), ())), preferred_element_type=...]
    all_to_all x0 -> x4, waiting for transfers between devices: none -> 33.7 us  [the longest x1 14.3 us: on_device(): got = lax.all_to_all(packed, TP, 0, 0, tiled=True)]
    psum x1 -> x0, blocking collectives: 31.4 us -> none  [on_device(): code = lax.psum(code_term, 'tensor').astype(jnp.bfloat16)]
    ppermute x0 -> x10, starting transfers between devices: none -> 30.7 us  [the longest x2 11.3 us: over_cores(): other = lax.ppermute(jnp.where(c == 0, a[fine:], a[:fine]), 'c', SWAP)]
  transfers between devices with their start and end apart: 7 -> 16, of which waited for: 4 -> 10; matrix products, arithmetic and copies ran while one was open for 8% -> 12% of each run, Pallas kernels for 0% -> 0%
where the time goes in v1:
time: 161 us; the launch traced here: 160 us
  waiting for transfers between devices  53.2 us (33%)
  starting transfers between devices  49 us (30%)
  Pallas kernels  18.5 us (11%)
  between operations  14.4 us (9%)
  other arithmetic  10.5 us (7%)
  local copies, waits for them, and re-layouts  8.2 us (5%)
  matrix products  6.15 us (4%)
    pallas_call x2, Pallas kernels, run_kernel(): pl.pallas_call(body, grid_spec=pltpu.PrefetchScalarGridSpec(num_scalar_pr...  18.5 us
    all_to_all x1, waiting for transfers between devices, on_device(): got = lax.all_to_all(packed, TP, 0, 0, tiled=True)  14.3 us
    ppermute x2, starting transfers between devices, over_cores(): other = lax.ppermute(jnp.where(c == 0, a[fine:], a[:fine]), 'c', SWAP)  11.3 us
    all_to_all x1, waiting for transfers between devices, on_device(): lax.all_to_all(both.reshape(NT, piece, width + code_w), TP, 0, 0, tiled=T...  10.7 us
    ppermute x1, starting transfers between devices, on_device(): g_oth = lax.ppermute(g_own, 'c', SWAP)  7.78 us
    reduce_scatter x1, waiting for transfers between devices, on_device(): red_b = lax.psum_scatter(buf_b, 'z', scatter_dimension=0, tiled=True)[0]  7 us
    all_to_all x1, starting transfers between devices, on_device(): got = lax.all_to_all(flat, ('yh', 'z'), 0, 0, tiled=True)  6.99 us
    dot_general x5, matrix products, dot(): lax.dot_general(a, b, (((ca,), (cb,)), ((), ())), preferred_element_type=...  6.15 us
  transfers between devices with their start and end apart: 16, of which 10 were waited for; matrix products, arithmetic and copies ran while one was open for 12% of the time, Pallas kernels for 0%

profile of v1, /device:TPU:1, one launch (start us, length us, event | category | flops | bytes accessed | tf_op | source)
XLA Modules:
  0.0 160.0 jit_solution(14587136696962367927)
XLA Ops:
  7.2 3.3 %collective-permute-start.1 = (bf16[256,1024]{1,0:T(8,128)(2,1)}, bf16[256,1024]{1,0:T(8,128)(2,1)S(1)}, u32[]{:S(2)}, u32[]{:S(2)}) collective-permute-start(bf16[256,1024]{1,0:T(8,128)(2,1)} %cot_own.1), channel_id=1, source_target_pairs={{0,8},{8,0},{1,9},{9,1},{2,10},{10,2},{3,11},{11,3},{4,12},{12,4},... | collective-permute-start | bytes 1572872 | tf_op jit(solution)/shard_map/ppermute | solution.py:161
  10.6 1.6 %collective-permute-done.1.cot_oth = bf16[256,1024]{1,0:T(8,128)(2,1)S(1)} collective-permute-done((bf16[256,1024]{1,0:T(8,128)(2,1)}, bf16[256,1024]{1,0:T(8,128)(2,1)S(1)}, u32[]{:S(2)}, u32[]{:S(2)}) %collective-permute-start.1) | collective-permute-done | bytes 524320 | tf_op jit(solution)/shard_map/ppermute | solution.py:161
  12.3 0.7 collective-permute-done.tok_oth
  13.0 0.7 copy-done.6
  13.8 10.6 %shard_map.160 = (bf16[8,160,512]{2,1,0:T(8,128)(2,1)}, bf16[1024,512]{1,0:T(8,128)(2,1)}, bf16[512,512]{1,0:T(8,128)(2,1)}, bf16[512,512]{1,0:T(8,128)(2,1)}, b...) custom-call(s32[1]{0:T(128)} %bitcast.core_ref, bf16[256,1024]{1,0:T(8,128)(2,1)} %tok_own.1, ...), custom_call_target="tpu_custom_call" | custom-call | flops 5000000000 | bytes 17043456 | tf_op jit(solution)/shard_map/pallas_call | solution.py:132
  24.4 7.8 %shard_map.161 = (bf16[8,128,1024]{2,1,0:T(8,128)(2,1)}, f32[256,1280]{1,0:T(8,128)}, bf16[256,1280]{1,0:T(8,128)(2,1)}) custom-call(s32[1]{0:T(128)} %bitcast.core_ref, bf16[1024,512]{1,0:T(8,128)(2,1)} %get-tuple-element.19.normed_t, bf16[512,512]{1,0:T(8,128)(2,1)} %get-tuple-element.20.q_in, bf16[512,512]{1,0:T(8,128)(2,1)} %get-tuple-element.21.k_in, ...), custom_call_target="tpu_custom_call" | custom-call | flops 3000000000 | bytes 14548992 | tf_op jit(solution)/shard_map/pallas_call | solution.py:132
  32.7 1.9 %collective-permute-done.2 = bf16[256,1280]{1,0:T(8,128)(2,1)S(1)} collective-permute-done((bf16[256,1280]{1,0:T(8,128)(2,1)}, bf16[256,1280]{1,0:T(8,128)(2,1)S(1)}, u32[]{:S(2)}, u32[]{:S(2)}) %collective-permute-start.2) | collective-permute-done | bytes 655392 | tf_op jit(solution)/shard_map/ppermute | solution.py:218
  34.6 2.3 %add_convert_fusion = bf16[256,1280]{1,0:T(8,128)(2,1)} fusion(f32[256,1280]{1,0:T(8,128)} %get-tuple-element.25, bf16[256,1280]{1,0:T(8,128)(2,1)S(1)} %collective-permute-done.2), kind=kLoop, calls=%fused_computation.4 | loop fusion | flops 983040 | bytes 2621440 | tf_op jit(solution)/shard_map/convert_element_type | solution.py:218
  36.9 3.7 %all-to-all-start = ((bf16[8,32,1280]{2,1,0:T(8,128)(2,1)}), bf16[8,32,1280]{2,1,0:T(8,128)(2,1)S(1)}, u32[]{:S(2)}, u32[]{:S(2)}) async-start(bf16[8,32,1280]{2,1,0:T(8,128)(2,1)} %bitcast.2), calls=%async_computation | async-start | bytes 1310720 | tf_op jit(solution)/shard_map/all_to_all | solution.py:220
  40.6 0.7 reduce-scatter.3.cloned.1.call-update
  41.5 10.7 %all-to-all-done = bf16[8,32,1280]{2,1,0:T(8,128)(2,1)S(1)} async-done(((bf16[8,32,1280]{2,1,0:T(8,128)(2,1)}), bf16[8,32,1280]{2,1,0:T(8,128)(2,1)S(1)}, u32[]{:S(2)}, u32[]{:S(2)}) %all-to-all-start) | async-done | bytes 655392 | tf_op jit(solution)/shard_map/all_to_all | solution.py:220
  53.0 1.0 fusion.17
  54.1 1.0 fusion.2
  55.1 3.6 %all-to-all-start.1 = ((bf16[8,48,1280]{2,1,0:T(8,128)(2,1)}), bf16[8,48,1280]{2,1,0:T(8,128)(2,1)S(1)}, u32[]{:S(2)}, u32[]{:S(2)}) async-start(bf16[8,48,1280]{2,1,0:T(8,128)(2,1)} %fusion.2), calls=%async_computation.1 | async-start | bytes 1966080 | tf_op jit(solution)/shard_map/all_to_all | solution.py:240
  58.7 0.7 reduce-scatter.5.cloned.1.call-update
  59.4 14.3 %all-to-all-done.1 = bf16[8,48,1280]{2,1,0:T(8,128)(2,1)S(1)} async-done(((bf16[8,48,1280]{2,1,0:T(8,128)(2,1)}), bf16[8,48,1280]{2,1,0:T(8,128)(2,1)S(1)}, u32[]{:S(2)}, u32[]{:S(2)}) %all-to-all-start.1) | async-done | bytes 983072 | tf_op jit(solution)/shard_map/all_to_all | solution.py:240
  73.8 0.9 collective-permute-start.4
  75.2 1.1 fusion.22
  76.4 1.1 convolution_add_fusion.1
  77.5 4.6 %reduce-scatter.3.cloned.1.call-done = bf16[1,160,512]{2,1,0:T(8,128)(2,1)} async-done(((bf16[8,160,512]{2,1,0:T(8,128)(2,1)}), bf16[1,160,512]{2,1,0:T(8,128)(2,1)}) %reduce-scatter.3.cloned.1.call-update) | async-done | bytes 163856 | tf_op jit(solution)/shard_map/reduce_scatter | solution.py:201
  82.1 0.8 slice_bitcast_fusion.1
  83.0 0.9 select_bitcast_fusion.1
  83.9 2.8 %collective-permute-start.3 = (bf16[96,512]{1,0:T(8,128)(2,1)S(1)}, bf16[96,512]{1,0:T(8,128)(2,1)S(1)}, u32[]{:S(2)}, u32[]{:S(2)}) collective-permute-start(bf16[96,512]{1,0:T(8,128)(2,1)S(1)} %pad_maximum_fusion.5), channel_id=1, source_target_pairs={{0,128},{128,0},{1,129},{129,1},{2,130},{130,2},{3,131},{131,3},{4... | collective-permute-start | bytes 294920 | tf_op jit(solution)/shard_map/ppermute | solution.py:260
  86.7 2.2 %collective-permute-done.3 = bf16[96,512]{1,0:T(8,128)(2,1)S(1)} collective-permute-done((bf16[96,512]{1,0:T(8,128)(2,1)S(1)}, bf16[96,512]{1,0:T(8,128)(2,1)S(1)}, u32[]{:S(2)}, u32[]{:S(2)}) %collective-permute-start.3) | collective-permute-done | bytes 98336 | tf_op jit(solution)/shard_map/ppermute | solution.py:260
  88.9 0.8 add_convert_fusion.1
  89.8 0.5 broadcast.47
  90.3 0.8 reduce.1
  91.1 1.0 reshape.132
  92.2 7.0 %all-to-all-start.2 = ((bf16[16,2,4672]{2,1,0:T(2,128)(2,1)}), bf16[16,2,4672]{2,1,0:T(2,128)(2,1)S(1)}, u32[]{:S(2)}, u32[]{:S(2)}) async-start(bf16[16,2,4672]{2,1,0:T(2,128)(2,1)} %reshape.132), calls=%async_computation.3 | async-start | bytes 606208 | tf_op jit(solution)/shard_map/all_to_all | solution.py:275
  99.2 6.0 %collective-permute-start.8 = (bf16[32,512]{1,0:T(8,128)(2,1)S(1)}, bf16[32,512]{1,0:T(8,128)(2,1)S(1)}, u32[]{:S(2)}, u32[]{:S(2)}) collective-permute-start(bf16[32,512]{1,0:T(8,128)(2,1)S(1)} %broadcast_select_fusion.6), channel_id=1, source_target_pairs={{0,8},{8,0},{1,9},{9,1},{2,10},{10,2},{3,11},{11,3},{4,12},{12,4},... | collective-permute-start | bytes 98312 | tf_op jit(solution)/shard_map/ppermute | solution.py:308
  105.2 1.1 fusion.1
  106.3 0.9 slice.138
  107.2 5.0 %all-to-all-done.2 = bf16[16,2,4672]{2,1,0:T(2,128)(2,1)S(1)} async-done(((bf16[16,2,4672]{2,1,0:T(2,128)(2,1)}), bf16[16,2,4672]{2,1,0:T(2,128)(2,1)S(1)}, u32[]{:S(2)}, u32[]{:S(2)}) %all-to-all-start.2) | async-done | bytes 299040 | tf_op jit(solution)/shard_map/all_to_all | solution.py:275
  112.9 7.8 %collective-permute-start.9 = (bf16[512,256]{1,0:T(8,128)(2,1)S(1)}, bf16[512,256]{1,0:T(8,128)(2,1)S(1)}, u32[]{:S(2)}, u32[]{:S(2)}) collective-permute-start(bf16[512,256]{1,0:T(8,128)(2,1)S(1)} %reshape.123), channel_id=1, source_target_pairs={{0,8},{8,0},{1,9},{9,1},{2,10},{10,2},{3,11},{11,3},{4,12},{12,4},... | collective-permute-start | bytes 786440 | tf_op jit(solution)/shard_map/ppermute | solution.py:281
  120.7 0.7 maximum_convert_fusion
  121.9 1.3 fusion.4
  123.2 7.0 %reduce-scatter.5.cloned.1.call-done = bf16[1,128,1024]{2,1,0:T(8,128)(2,1)} async-done(((bf16[8,128,1024]{2,1,0:T(8,128)(2,1)}), bf16[1,128,1024]{2,1,0:T(8,128)(2,1)}) %reduce-scatter.5.cloned.1.call-update) | async-done | bytes 262160 | tf_op jit(solution)/shard_map/reduce_scatter | solution.py:216
  130.2 1.0 select_bitcast_fusion
  131.3 3.8 %collective-permute-start.6 = (bf16[64,1024]{1,0:T(8,128)(2,1)S(1)}, bf16[64,1024]{1,0:T(8,128)(2,1)S(1)}, u32[]{:S(2)}, u32[]{:S(2)}) collective-permute-start(bf16[64,1024]{1,0:T(8,128)(2,1)S(1)} %select_bitcast_fusion), channel_id=1, source_target_pairs={{0,128},{128,0},{1,129},{129,1},{2,130},{130,2},{3,131},{131,3},{4... | collective-permute-start | bytes 393224 | tf_op jit(solution)/shard_map/ppermute | solution.py:304
  135.1 0.7 all_to_all.27
  135.8 4.0 %all-to-all-start.3 = ((f32[8,1,2048]{2,1,0:T(1,128)}), f32[8,1,2048]{2,1,0:T(1,128)S(1)}, u32[]{:S(2)}, u32[]{:S(2)}) async-start(f32[8,1,2048]{2,1,0:T(1,128)} %all_to_all.27), calls=%async_computation.5 | async-start | bytes 131072 | tf_op jit(solution)/shard_map/all_to_all | solution.py:297
  139.8 1.6 %fusion.5 = f32[1024,32]{0,1:T(8,128)} fusion(bf16[512,256]{1,0:T(8,128)(2,1)S(1)} %get-tuple-element.32, bf16[512,256]{1,0:T(8,128)(2,1)S(1)} %get-tuple-element.31, bf16[1024,256]{1,0:T(8,128)(2,1)} %enc.1, s32[]{:T(128)S(6)} %select_n.140), kind=kOutput, calls=%fused_computation.12 | convolution fusion | flops 17825792 | bytes 671748 | tf_op jit(solution)/shard_map/dot_general | solution.py:21
  141.5 3.6 %all-to-all-done.3 = f32[8,1,2048]{2,1,0:T(1,128)S(1)} async-done(((f32[8,1,2048]{2,1,0:T(1,128)}), f32[8,1,2048]{2,1,0:T(1,128)S(1)}, u32[]{:S(2)}, u32[]{:S(2)}) %all-to-all-start.3) | async-done | bytes 65568 | tf_op jit(solution)/shard_map/all_to_all | solution.py:297
  145.1 5.4 %collective-permute-start.7 = (bf16[32,1024]{1,0:T(8,128)(2,1)S(1)}, bf16[32,1024]{1,0:T(8,128)(2,1)S(1)}, u32[]{:S(2)}, u32[]{:S(2)}) collective-permute-start(bf16[32,1024]{1,0:T(8,128)(2,1)S(1)} %broadcast_select_fusion.2), channel_id=1, source_target_pairs={{0,8},{8,0},{1,9},{9,1},{2,10},{10,2},{3,11},{11,3},{4,12},{12,4},... | collective-permute-start | bytes 196616 | tf_op jit(solution)/shard_map/ppermute | solution.py:308
  150.5 0.6 copy.52
  151.2 0.6 reshape.125
  151.8 0.7 pad_maximum_fusion.4
  152.5 0.7 pad_maximum_fusion.3
  (71 shorter events, 3.9 us)
Async XLA Ops:
  7.2 5.1 %collective-permute-start.1 = (bf16[256,1024]{1,0:T(8,128)(2,1)}, bf16[256,1024]{1,0:T(8,128)(2,1)S(1)}, u32[]{:S(2)}, u32[]{:S(2)}) collective-permute-start(bf16[256,1024]{1,0:T(8,128)(2,1)} %cot_own.1), channel_id=1, source_target_pairs={{0,8},{8,0},{1,9},{9,1},{2,10},{10,2},{3,11},{11,3},{4,12},{12,4},... | collective-permute-start | bytes 1572872 | tf_op jit(solution)/shard_map/ppermute | solution.py:161
  10.5 2.5 %collective-permute-start = (bf16[256,1024]{1,0:T(8,128)(2,1)}, bf16[256,1024]{1,0:T(8,128)(2,1)S(1)}, u32[]{:S(2)}, u32[]{:S(2)}) collective-permute-start(bf16[256,1024]{1,0:T(8,128)(2,1)} %tok_own.1), channel_id=1, source_target_pairs={{0,8},{8,0},{1,9},{9,1},{2,10},{10,2},{3,11},{11,3},{4,12},{12,4},... | collective-permute-start | bytes 1572872 | tf_op jit(solution)/shard_map/ppermute | solution.py:160
  12.3 0.8 copy-start.5
  13.0 0.8 copy-start.6
  32.3 2.3 %collective-permute-start.2 = (bf16[256,1280]{1,0:T(8,128)(2,1)}, bf16[256,1280]{1,0:T(8,128)(2,1)S(1)}, u32[]{:S(2)}, u32[]{:S(2)}) collective-permute-start(bf16[256,1280]{1,0:T(8,128)(2,1)} %get-tuple-element.26), channel_id=1, source_target_pairs={{0,8},{8,0},{1,9},{9,1},{2,10},{10,2},{3,11},{11,3},{4,12},{12,4},... | collective-permute-start | bytes 1966088 | tf_op jit(solution)/shard_map/ppermute | solution.py:218
  36.9 4.4 %copy-start.1 = (bf16[256,1024]{1,0:T(8,128)(2,1)S(1)}, bf16[256,1024]{1,0:T(8,128)(2,1)}, u32[]{:S(2)}) copy-start(bf16[256,1024]{1,0:T(8,128)(2,1)} %tok_own.1) | copy-start | bytes 1572868
  36.9 15.4 %copy-start.4 = (f32[1024]{0:T(1024)S(1)}, f32[1024]{0:T(1024)}, u32[]{:S(2)}) copy-start(f32[1024]{0:T(1024)} %param.10) | copy-start | bytes 12292
  36.9 15.3 %all-to-all-start = ((bf16[8,32,1280]{2,1,0:T(8,128)(2,1)}), bf16[8,32,1280]{2,1,0:T(8,128)(2,1)S(1)}, u32[]{:S(2)}, u32[]{:S(2)}) async-start(bf16[8,32,1280]{2,1,0:T(8,128)(2,1)} %bitcast.2), calls=%async_computation | async-start | bytes 1310720 | tf_op jit(solution)/shard_map/all_to_all | solution.py:220
  40.6 41.5 %reduce-scatter.3.cloned.1.call-start = ((), (), s32[]{:S(2)}) async-start(), calls=%async_computation.6 | async-start | bytes 1474560 | tf_op jit(solution)/shard_map/reduce_scatter | solution.py:201
  55.1 18.6 %all-to-all-start.1 = ((bf16[8,48,1280]{2,1,0:T(8,128)(2,1)}), bf16[8,48,1280]{2,1,0:T(8,128)(2,1)S(1)}, u32[]{:S(2)}, u32[]{:S(2)}) async-start(bf16[8,48,1280]{2,1,0:T(8,128)(2,1)} %fusion.2), calls=%async_computation.1 | async-start | bytes 1966080 | tf_op jit(solution)/shard_map/all_to_all | solution.py:240
  58.6 71.6 %reduce-scatter.5.cloned.1.call-start = ((), (), s32[]{:S(2)}) async-start(), calls=%async_computation.7 | async-start | bytes 2359296 | tf_op jit(solution)/shard_map/reduce_scatter | solution.py:216
  73.8 2.6 %collective-permute-start.4 = (bf16[256,256]{1,0:T(8,128)(2,1)S(1)}, bf16[256,256]{1,0:T(8,128)(2,1)S(1)}, u32[]{:S(2)}, u32[]{:S(2)}) collective-permute-start(bf16[256,256]{1,0:T(8,128)(2,1)S(1)} %slice.137), channel_id=1, source_target_pairs={{0,8},{8,0},{1,9},{9,1},{2,10},{10,2},{3,11},{11,3},{4,12},{12,4},... | collective-permute-start | bytes 393224 | tf_op jit(solution)/shard_map/ppermute | solution.py:250
  74.9 30.3 %copy-start.3 = (bf16[256,1024]{1,0:T(8,128)(2,1)S(1)}, bf16[256,1024]{1,0:T(8,128)(2,1)}, u32[]{:S(2)}) copy-start(bf16[256,1024]{1,0:T(8,128)(2,1)} %dec.1) | copy-start | bytes 1572868
  74.9 1.4 collective-permute-start.5
  82.1 17.1 %copy-start.2 = (bf16[1,160,512]{2,1,0:T(8,128)(2,1)S(1)}, bf16[1,160,512]{2,1,0:T(8,128)(2,1)}, u32[]{:S(2)}) copy-start(bf16[1,160,512]{2,1,0:T(8,128)(2,1)} %reduce-scatter.3.cloned.1.call-done) | copy-start | bytes 491524
  83.9 5.1 %collective-permute-start.3 = (bf16[96,512]{1,0:T(8,128)(2,1)S(1)}, bf16[96,512]{1,0:T(8,128)(2,1)S(1)}, u32[]{:S(2)}, u32[]{:S(2)}) collective-permute-start(bf16[96,512]{1,0:T(8,128)(2,1)S(1)} %pad_maximum_fusion.5), channel_id=1, source_target_pairs={{0,128},{128,0},{1,129},{129,1},{2,130},{130,2},{3,131},{131,3},{4... | collective-permute-start | bytes 294920 | tf_op jit(solution)/shard_map/ppermute | solution.py:260
  92.2 20.0 %all-to-all-start.2 = ((bf16[16,2,4672]{2,1,0:T(2,128)(2,1)}), bf16[16,2,4672]{2,1,0:T(2,128)(2,1)S(1)}, u32[]{:S(2)}, u32[]{:S(2)}) async-start(bf16[16,2,4672]{2,1,0:T(2,128)(2,1)} %reshape.132), calls=%async_computation.3 | async-start | bytes 606208 | tf_op jit(solution)/shard_map/all_to_all | solution.py:275
  99.2 21.4 %collective-permute-start.8 = (bf16[32,512]{1,0:T(8,128)(2,1)S(1)}, bf16[32,512]{1,0:T(8,128)(2,1)S(1)}, u32[]{:S(2)}, u32[]{:S(2)}) collective-permute-start(bf16[32,512]{1,0:T(8,128)(2,1)S(1)} %broadcast_select_fusion.6), channel_id=1, source_target_pairs={{0,8},{8,0},{1,9},{9,1},{2,10},{10,2},{3,11},{11,3},{4,12},{12,4},... | collective-permute-start | bytes 98312 | tf_op jit(solution)/shard_map/ppermute | solution.py:308
  112.9 9.0 %collective-permute-start.9 = (bf16[512,256]{1,0:T(8,128)(2,1)S(1)}, bf16[512,256]{1,0:T(8,128)(2,1)S(1)}, u32[]{:S(2)}, u32[]{:S(2)}) collective-permute-start(bf16[512,256]{1,0:T(8,128)(2,1)S(1)} %reshape.123), channel_id=1, source_target_pairs={{0,8},{8,0},{1,9},{9,1},{2,10},{10,2},{3,11},{11,3},{4,12},{12,4},... | collective-permute-start | bytes 786440 | tf_op jit(solution)/shard_map/ppermute | solution.py:281
  130.2 14.8 %copy-start = (bf16[1,128,1024]{2,1,0:T(8,128)(2,1)S(1)}, bf16[1,128,1024]{2,1,0:T(8,128)(2,1)}, u32[]{:S(2)}) copy-start(bf16[1,128,1024]{2,1,0:T(8,128)(2,1)} %reduce-scatter.5.cloned.1.call-done) | copy-start | bytes 786436
  131.3 13.8 %collective-permute-start.6 = (bf16[64,1024]{1,0:T(8,128)(2,1)S(1)}, bf16[64,1024]{1,0:T(8,128)(2,1)S(1)}, u32[]{:S(2)}, u32[]{:S(2)}) collective-permute-start(bf16[64,1024]{1,0:T(8,128)(2,1)S(1)} %select_bitcast_fusion), channel_id=1, source_target_pairs={{0,128},{128,0},{1,129},{129,1},{2,130},{130,2},{3,131},{131,3},{4... | collective-permute-start | bytes 393224 | tf_op jit(solution)/shard_map/ppermute | solution.py:304
  135.8 9.2 %all-to-all-start.3 = ((f32[8,1,2048]{2,1,0:T(1,128)}), f32[8,1,2048]{2,1,0:T(1,128)S(1)}, u32[]{:S(2)}, u32[]{:S(2)}) async-start(f32[8,1,2048]{2,1,0:T(1,128)} %all_to_all.27), calls=%async_computation.5 | async-start | bytes 131072 | tf_op jit(solution)/shard_map/all_to_all | solution.py:297
  145.1 6.6 %collective-permute-start.7 = (bf16[32,1024]{1,0:T(8,128)(2,1)S(1)}, bf16[32,1024]{1,0:T(8,128)(2,1)S(1)}, u32[]{:S(2)}, u32[]{:S(2)}) collective-permute-start(bf16[32,1024]{1,0:T(8,128)(2,1)S(1)} %broadcast_select_fusion.2), channel_id=1, source_target_pairs={{0,8},{8,0},{1,9},{9,1},{2,10},{10,2},{3,11},{11,3},{4,12},{12,4},... | collective-permute-start | bytes 196616 | tf_op jit(solution)/shard_map/ppermute | solution.py:308
Sparse Core Ops, SparseCore 0:
  44.0 38.1 reduce-scatter.2
  84.7 45.5 reduce-scatter.4

commit v2 on v1

v2 whole, which is shorter than its diff:
```python
import jax
import jax.numpy as jnp
import numpy as np
from jax import lax
from jax.experimental import pallas as pl
from jax.experimental.pallas import tpu as pltpu
from jax.sharding import Mesh
from jax.sharding import PartitionSpec as P

DK = 128
SEQ = 256
YH, Z, CORES, YL, X = 2, 8, 2, 2, 4
NT = YL * X
TP = ("yl", "x")
F32 = jnp.float32
BF16 = jnp.bfloat16
SWAP = [(0, 1), (1, 0)]


def dot(a, b, ca=1, cb=0):
    return lax.dot_general(a, b, (((ca,), (cb,)), ((), ())), preferred_element_type=F32)


def block_kernel(
    core_ref,
    gain,
    tok_own_h,
    tok_oth_h,
    wq_h,
    cot_own_h,
    cot_oth_h,
    dec_h,
    wo_h,
    enc_h,
    wk_h,
    wv_h,
    buf_h,
    send,
    keep,
    enc_out,
    tok,
    cot,
    wq,
    wk,
    wv,
    wo,
    enc,
    dec,
    norm_s,
    norm_t,
    dcode_s,
    q_s,
    k_s,
    v_s,
    dctx_s,
    ctx_s,
    dq_s,
    dk_s,
    dv_s,
    stage,
    in_sem,
    out_sem,
):
    width, own = wq.shape
    heads = own // DK
    code = enc.shape[1]
    part = width // (YH * Z)
    core = core_ref[0]
    mine = pl.ds(pl.multiple_of(core * own, own), own)
    pairs = (
        (tok_own_h, tok.at[pl.ds(0, SEQ)]),
        (tok_oth_h, tok.at[pl.ds(SEQ, SEQ)]),
        (wq_h.at[:, mine], wq),
        (wk_h.at[:, mine], wk),
        (wv_h.at[:, mine], wv),
        (cot_own_h, cot.at[pl.ds(0, SEQ)]),
        (cot_oth_h, cot.at[pl.ds(SEQ, SEQ)]),
        (dec_h, dec),
        (wo_h.at[mine, :], wo),
        (enc_h, enc),
    )
    copies = [pltpu.make_async_copy(a, b, in_sem.at[i]) for i, (a, b) in enumerate(pairs)]
    for copy in copies:
        copy.start()

    for s in range(2):
        at = slice(s * SEQ, (s + 1) * SEQ)
        copies[s].wait()
        x = tok[at, :].astype(F32)
        rms = lax.rsqrt(jnp.mean(x * x, axis=-1, keepdims=True) + 1e-6)
        norm_s[at, :] = (x * rms * gain[...]).astype(BF16)
    normed = norm_s[...]
    copies[2].wait()
    q_s[...] = dot(normed, wq[...]).astype(BF16)
    norm_t[...] = normed.T
    copies[3].wait()
    k_s[...] = dot(normed, wk[...]).astype(BF16)
    copies[4].wait()
    v_s[...] = dot(normed, wv[...]).astype(BF16)
    for copy in copies[5:]:
        copy.wait()
    dcode_s[...] = dot(cot[...], dec[...], 1, 1).astype(BF16)
    w2 = dot(wo[...], enc[...]).astype(BF16)
    dctx_s[...] = dot(dcode_s[...], w2, 1, 1).astype(BF16)
    scale = DK**-0.5
    row = lax.broadcasted_iota(jnp.int32, (SEQ, SEQ), 0)
    col = lax.broadcasted_iota(jnp.int32, (SEQ, SEQ), 1)
    causal = row >= col
    for s in range(2):
        for h in range(heads):
            at = (slice(s * SEQ, (s + 1) * SEQ), slice(h * DK, (h + 1) * DK))
            q, k, v, dctx = q_s[at], k_s[at], v_s[at], dctx_s[at]
            scores = jnp.where(causal, dot(q, k, 1, 1) * scale, -1e30)
            top = jnp.max(scores, axis=-1, keepdims=True)
            expo = jnp.exp(scores - top)
            probs = expo * (1.0 / jnp.sum(expo, axis=-1, keepdims=True))
            low = probs.astype(BF16)
            ctx_s[at] = dot(low, v).astype(BF16)
            dprobs = dot(dctx, v, 1, 1)
            dv_s[at] = dot(low, dctx, 0, 0).astype(BF16)
            delta = jnp.sum(dprobs * probs, axis=-1, keepdims=True)
            ds = (probs * (dprobs - delta) * scale).astype(BF16)
            dq_s[at] = dot(ds, k).astype(BF16)
            dk_s[at] = dot(ds, q, 0, 0).astype(BF16)

    def put(i, g):
        lanes = slice(i * own, (i + 1) * own)
        for z in range(Z):
            for y in range(YH):
                at = (y * Z + z) * part
                stage[z, y * part : (y + 1) * part, lanes] = g[at : at + part, :].astype(BF16)
        there = buf_h.at[:, :, pl.ds(i * own, own)]
        copy = pltpu.make_async_copy(stage.at[:, :, pl.ds(i * own, own)], there, out_sem.at[i])
        copy.start()
        return copy

    g = dot(ctx_s[...], dcode_s[...], 0, 0).astype(BF16)
    out = [put(3, dot(enc[...], g, 1, 1))]
    out.append(put(2, dot(norm_t[...], dv_s[...])))
    out.append(put(0, dot(norm_t[...], dq_s[...])))
    out.append(put(1, dot(norm_t[...], dk_s[...])))
    for s, ref in enumerate((keep, send)):
        at = slice(s * SEQ, (s + 1) * SEQ)
        dn = dot(dq_s[at, :], wq[...], 1, 1)
        dn = dn + dot(dk_s[at, :], wk[...], 1, 1)
        dn = dn + dot(dv_s[at, :], wv[...], 1, 1)
        ref[:, 0:width] = dn.astype(BF16)
        ref[:, width : width + code] = dot(ctx_s[at, :], w2).astype(BF16)
    enc_out[...] = dot(wo[...], g, 0, 0).astype(BF16)
    for copy in out:
        copy.wait()


def run_block(core, gain, *args):
    tokens, wq, enc = args[0], args[2], args[7]
    width, own = wq.shape[0], wq.shape[1] // CORES
    code = enc.shape[1]
    part = width // (YH * Z)
    sds = jax.ShapeDtypeStruct
    outs = (
        sds((Z, YH * part, 4 * own), BF16),
        sds((SEQ, width + code), BF16),
        sds((SEQ, width + code), BF16),
        sds((width, code), BF16),
    )
    vmem = pl.BlockSpec(memory_space=pltpu.VMEM)
    hbm = pl.BlockSpec(memory_space=pl.ANY)
    two = 2 * SEQ
    shapes = (
        (two, width),
        (two, width),
        (width, own),
        (width, own),
        (width, own),
        (own, width),
        (width, code),
        (code, width),
        (two, width),
        (width, two),
        (two, code),
        *(((two, own),) * 8),
        (Z, YH * part, 4 * own),
    )
    return pl.pallas_call(
        block_kernel,
        in_specs=[pl.BlockSpec(memory_space=pltpu.SMEM), vmem, *([hbm] * len(args))],
        out_specs=[hbm, vmem, vmem, vmem],
        out_shape=outs,
        scratch_shapes=[
            *(pltpu.VMEM(shape, BF16) for shape in shapes),
            pltpu.SemaphoreType.DMA((10,)),
            pltpu.SemaphoreType.DMA((4,)),
        ],
        compiler_params=pltpu.CompilerParams(vmem_limit_bytes=56 * 1024 * 1024),
        cost_estimate=pl.CostEstimate(
            flops=7_500_000_000, bytes_accessed=14_000_000, transcendentals=600_000
        ),
    )(core, gain, *args)


def on_device(tokens, gain, w_query, w_key, w_value, w_output, encoder, decoder, cotangent):
    rows, width = tokens.shape
    own = w_query.shape[1] // CORES
    code_w = encoder.shape[1]
    yh, z, c = lax.axis_index("yh"), lax.axis_index("z"), lax.axis_index("c")
    t = lax.axis_index("yl") * X + lax.axis_index("x")
    n_yz = YH * Z
    n_dp = n_yz * CORES
    fine = width // n_dp
    tiny = fine // NT
    core = jnp.reshape(c, (1,)).astype(jnp.int32)

    tok_oth = lax.ppermute(tokens, "c", SWAP)
    cot_oth = lax.ppermute(cotangent, "c", SWAP)
    buf, send, keep, enc_p = run_block(
        core,
        gain.reshape(1, width),
        tokens,
        tok_oth,
        w_query,
        cotangent,
        cot_oth,
        decoder,
        w_output,
        encoder,
        w_key,
        w_value,
    )
    red = lax.psum_scatter(buf, "z", scatter_dimension=0, tiled=True)

    both = (keep.astype(F32) + lax.ppermute(send, "c", SWAP).astype(F32)).astype(BF16)
    piece = rows // NT
    got = lax.all_to_all(both.reshape(NT, piece, width + code_w), TP, 0, 0, tiled=True)
    total = jnp.sum(got.astype(F32), axis=0)
    dnormed = total[:, :width]
    x = lax.dynamic_slice_in_dim(tokens, t * piece, piece, 0).astype(F32)
    cot = lax.dynamic_slice_in_dim(cotangent, t * piece, piece, 0).astype(F32)
    rms = lax.rsqrt(jnp.mean(x * x, axis=-1, keepdims=True) + 1e-6)
    unit = x * rms
    dunit = dnormed * gain
    inner = jnp.sum(dunit * unit, axis=-1, keepdims=True) / width
    grad_rows = cot + rms * (dunit - unit * inner)
    gain_row = jnp.sum(dnormed * unit, axis=0)
    gain_by_t = gain_row.reshape(n_dp, NT, tiny).transpose(1, 0, 2).reshape(NT, 1, -1)
    gain_w = n_dp * tiny

    enc_p = enc_p.reshape(n_yz, CORES, fine, code_w)
    enc_keep = lax.dynamic_index_in_dim(enc_p, c, 1, keepdims=False)
    enc_send = lax.dynamic_index_in_dim(enc_p, 1 - c, 1, keepdims=False)
    enc_c = enc_keep.astype(F32) + lax.ppermute(enc_send, "c", SWAP).astype(F32)
    enc_c = enc_c.astype(BF16).reshape(n_yz, NT, tiny, code_w).transpose(1, 0, 2, 3)
    enc_c = enc_c.reshape(NT, n_yz * tiny, code_w)

    first = jnp.concatenate([grad_rows, total[:, width:]], axis=1).astype(BF16)
    out_w = width + code_w
    half = n_yz * tiny // 2
    enc_c = jnp.concatenate([enc_c[:, :half], enc_c[:, half:]], axis=2)
    enc_c = jnp.pad(enc_c, ((0, 0), (0, piece - half), (0, 0)))
    gain_b = jnp.pad(gain_by_t, ((0, 0), (0, piece - 1), (0, -gain_w % 128))).astype(BF16)
    packed = jnp.concatenate(
        [jnp.broadcast_to(first[None], (NT, piece, out_w)), enc_c, gain_b], axis=2
    )
    got = lax.all_to_all(packed, TP, 0, 0, tiled=True)
    whole_rows = got[:, :, :out_w].reshape(rows, out_w)
    grad_input = whole_rows[:, :width]
    code = whole_rows[:, width:]
    code_oth = lax.ppermute(code, "c", SWAP)
    sums = jnp.sum(got[:, :, out_w:].astype(F32), axis=0)
    enc_t = jnp.concatenate(
        [sums[:half, :code_w], sums[:half, code_w : 2 * code_w]], axis=0
    ).reshape(n_yz, -1)
    gain_sum = sums[0, 2 * code_w : 2 * code_w + gain_w].reshape(n_yz, CORES, tiny)
    gain_keep = lax.dynamic_index_in_dim(gain_sum, c, 1, keepdims=False)
    gain_send = lax.dynamic_index_in_dim(gain_sum, 1 - c, 1, keepdims=False)
    gain_keep = gain_keep + lax.ppermute(gain_send, "c", SWAP)

    cols = width // NT
    cot_own_c = lax.dynamic_slice_in_dim(cotangent, t * cols, cols, 1)
    cot_oth_c = lax.dynamic_slice_in_dim(cot_oth, t * cols, cols, 1)
    dec_p = dot(code, cot_own_c, 0, 0) + dot(code_oth, cot_oth_c, 0, 0)
    dec_rows = code_w // n_dp
    dec_p = dec_p.reshape(n_yz, CORES, dec_rows, cols)
    dec_p = lax.dynamic_index_in_dim(dec_p, c, 1, keepdims=False)

    flat = jnp.concatenate(
        [
            dec_p.reshape(n_yz, -1),
            enc_t,
            jnp.pad(gain_keep, ((0, 0), (0, 128 - tiny))),
        ],
        axis=1,
    ).astype(BF16)
    got = lax.all_to_all(flat, ("yh", "z"), 0, 0, tiled=True)
    tail = jnp.sum(got.astype(F32), axis=0)
    d_size, e_size = dec_rows * cols, tiny * code_w
    grad_encoder = tail[d_size : d_size + e_size].reshape(tiny, code_w)
    grad_gain = tail[d_size + e_size : d_size + e_size + tiny]
    dec_sum = jnp.broadcast_to(tail[:d_size].reshape(1, dec_rows, cols), (NT, dec_rows, cols))
    got = lax.all_to_all(dec_sum, TP, 0, 0, tiled=True)
    grad_decoder = got.transpose(1, 0, 2).reshape(dec_rows, width)
    output = (tokens.astype(F32) + dot(code, decoder)).astype(BF16)

    got = lax.all_to_all(
        red.reshape(YH * CORES, fine, 4 * own), ("yh", "c"), 0, 0, tiled=True
    )
    got = got.reshape(YH, CORES, fine, 4, own).astype(F32)
    grads = got[0] + got[1]
    grads = [
        jnp.concatenate([grads[0, :, i], grads[1, :, i]], axis=1) for i in range(4)
    ]
    return (
        output,
        grad_input,
        grad_gain,
        grads[0],
        grads[1],
        grads[2],
        grads[3].T,
        grad_encoder,
        grad_decoder,
    )


def solution(mesh):
    devices = np.asarray(mesh.devices).reshape(YH, Z, CORES, YL, X)
    fine = Mesh(devices, ("yh", "z", "c", "yl", "x"))
    dp = ("yh", "z", "c")
    every = (*dp, *TP)
    return jax.shard_map(
        on_device,
        mesh=fine,
        in_specs=(
            P(dp, None),
            P(),
            P(None, TP),
            P(None, TP),
            P(None, TP),
            P(TP, None),
            P(),
            P(),
            P(dp, None),
        ),
        out_specs=(
            P(dp, None),
            P(dp, None),
            P(every),
            P(dp, TP),
            P(dp, TP),
            P(dp, TP),
            P(TP, dp),
            P(every, None),
            P(dp, None),
        ),
        check_vma=False,
    )
```

time: 161 us -> 130 us (0.81)
  starting transfers between devices: 49 us -> 18.6 us
  blocking collectives: 0 us -> 26.6 us
  waiting for transfers between devices: 53.2 us -> 37.5 us
  Pallas kernels: 18.5 us -> 15.1 us
  other arithmetic: 10.5 us -> 7.18 us
  matrix products: 6.15 us -> 3.24 us
    all_to_all x0 -> x2, blocking collectives: none -> 26.6 us  [the longest x1 19.1 us: on_device(): got = lax.all_to_all(flat, ('yh', 'z'), 0, 0, tiled=True)]
    ppermute x6 -> x2, starting transfers between devices: 26.2 us -> 0.81 us  [the longest x1 0.44 us: on_device(): enc_c = enc_keep.astype(F32) + lax.ppermute(enc_send, 'c', SWAP).astype(F32)]
    reduce_scatter x2 -> x1, waiting for transfers between devices: 11.6 us -> 0.01 us  [on_device(): red = lax.psum_scatter(buf, 'z', scatter_dimension=0, tiled=True)]
    all_to_all x2 -> x1, starting transfers between devices: 11 us -> 6.18 us  [on_device(): lax.all_to_all(red.reshape(YH * CORES, fine, 4 * own), ('yh', 'c'), 0, 0,...]
    pallas_call x2 -> x1, Pallas kernels: 18.5 us -> 15.1 us  [run_block(): pl.pallas_call(block_kernel, in_specs=[pl.BlockSpec(memory_space=pltpu.SM...]
    ppermute x6 -> x2, waiting for transfers between devices: 4.19 us -> 1.13 us  [the longest x1 1.13 us: on_device(): lax.ppermute(send, 'c', SWAP).astype(F32)]
    dot_general x5 -> x3, matrix products: 6.15 us -> 3.24 us  [dot(): lax.dot_general(a, b, (((ca,), (cb,)), ((), ())), preferred_element_type=...]
    all_to_all x2 -> x1, waiting for transfers between devices: 8.61 us -> 6.41 us  [on_device(): lax.all_to_all(red.reshape(YH * CORES, fine, 4 * own), ('yh', 'c'), 0, 0,...]
  transfers between devices with their start and end apart: 16 -> 10, of which waited for: 10 -> 7; matrix products, arithmetic and copies ran while one was open for 12% -> 9% of each run, Pallas kernels for 0% -> 0%
where the time goes in v2:
time: 130 us
  waiting for transfers between devices  37.5 us (29%)
  blocking collectives  26.6 us (20%)
  starting transfers between devices  18.6 us (14%)
  Pallas kernels  15.1 us (12%)
  between operations  14.4 us (11%)
  other arithmetic  7.18 us (6%)
  local copies, waits for them, and re-layouts  7.05 us (5%)
  matrix products  3.24 us (2%)
    all_to_all x1, blocking collectives, on_device(): got = lax.all_to_all(flat, ('yh', 'z'), 0, 0, tiled=True)  19.1 us
    pallas_call x1, Pallas kernels, run_block(): pl.pallas_call(block_kernel, in_specs=[pl.BlockSpec(memory_space=pltpu.SM...  15.1 us
    all_to_all x1, waiting for transfers between devices, on_device(): got = lax.all_to_all(packed, TP, 0, 0, tiled=True)  15.1 us
    all_to_all x1, waiting for transfers between devices, on_device(): lax.all_to_all(both.reshape(NT, piece, width + code_w), TP, 0, 0, tiled=T...  11.2 us
    all_to_all x1, blocking collectives, on_device(): got = lax.all_to_all(dec_sum, TP, 0, 0, tiled=True)  7.48 us
    all_to_all x1, waiting for transfers between devices, on_device(): lax.all_to_all(red.reshape(YH * CORES, fine, 4 * own), ('yh', 'c'), 0, 0,...  6.41 us
    all_to_all x1, starting transfers between devices, on_device(): lax.all_to_all(red.reshape(YH * CORES, fine, 4 * own), ('yh', 'c'), 0, 0,...  6.18 us
    all_to_all x1, starting transfers between devices, on_device(): got = lax.all_to_all(packed, TP, 0, 0, tiled=True)  3.56 us
  transfers between devices with their start and end apart: 10, of which 7 were waited for; matrix products, arithmetic and copies ran while one was open for 9% of the time, Pallas kernels for 0%

profile of v2, /device:TPU:1, one launch (start us, length us, event | category | flops | bytes accessed | tf_op | source)
XLA Modules:
  0.0 129.7 jit_solution(13118455524943081523)
XLA Ops:
  7.2 3.3 %collective-permute-start.1 = (bf16[256,1024]{1,0:T(8,128)(2,1)}, bf16[256,1024]{1,0:T(8,128)(2,1)S(1)}, u32[]{:S(2)}, u32[]{:S(2)}) collective-permute-start(bf16[256,1024]{1,0:T(8,128)(2,1)} %cot_own_h.1), channel_id=1, source_target_pairs={{0,8},{8,0},{1,9},{9,1},{2,10},{10,2},{3,11},{11,3},{4,12},{12,4},... | collective-permute-start | bytes 1572872 | tf_op jit(solution)/shard_map/ppermute | solution.py:214
  10.6 0.1 collective-permute-start
  10.7 1.6 %collective-permute-done.1.cot_oth_h = bf16[256,1024]{1,0:T(8,128)(2,1)S(1)} collective-permute-done((bf16[256,1024]{1,0:T(8,128)(2,1)}, bf16[256,1024]{1,0:T(8,128)(2,1)S(1)}, u32[]{:S(2)}, u32[]{:S(2)}) %collective-permute-start.1) | collective-permute-done | bytes 524320 | tf_op jit(solution)/shard_map/ppermute | solution.py:214
  12.3 0.7 collective-permute-done.tok_oth_h
  13.1 0.7 copy-done.7
  13.8 15.1 %shard_map.160 = (bf16[8,128,2048]{2,1,0:T(8,128)(2,1)}, bf16[256,1280]{1,0:T(8,128)(2,1)}, bf16[256,1280]{1,0:T(8,128)(2,1)}, bf16[1024,256]{1,0:T(8,128)(2,1)}) custom-call(s32[1]{0:T(128)} %bitcast.core_ref, f32[1,1024]{1,0:T(1,128)} %bitcast.63, bf16[256,1024]{1,0:T(8,128)(2,1)} %tok_own_h.1, bf16[256,1024]{1,0:T(8,128)(2,1)} %copy-done.7, ...), custom_call_target="tpu_custom_call" | custom-call | flops 7500000256 | bytes 14000000 | tf_op jit(solution)/shard_map/pallas_call | solution.py:184
  29.1 1.0 copy-done.6
  30.1 0.4 collective-permute-start.2
  30.5 0.1 fusion.13
  30.6 0.4 collective-permute-start.3
  31.1 1.1 collective-permute-done.2
  32.2 1.0 add_convert_fusion
  33.2 3.5 %all-to-all-start = ((bf16[8,32,1280]{2,1,0:T(8,128)(2,1)}), bf16[8,32,1280]{2,1,0:T(8,128)(2,1)S(1)}, u32[]{:S(2)}, u32[]{:S(2)}) async-start(bf16[8,32,1280]{2,1,0:T(8,128)(2,1)} %bitcast.2), calls=%async_computation | async-start | bytes 1310720 | tf_op jit(solution)/shard_map/all_to_all | solution.py:233
  37.1 11.2 %all-to-all-done = bf16[8,32,1280]{2,1,0:T(8,128)(2,1)S(1)} async-done(((bf16[8,32,1280]{2,1,0:T(8,128)(2,1)}), bf16[8,32,1280]{2,1,0:T(8,128)(2,1)S(1)}, u32[]{:S(2)}, u32[]{:S(2)}) %all-to-all-start) | async-done | bytes 655392 | tf_op jit(solution)/shard_map/all_to_all | solution.py:233
  48.4 0.2 fusion.7
  48.7 0.2 reshape.163
  48.8 0.3 copy.43
  49.2 1.0 fusion.11
  50.2 1.0 fusion.2
  51.2 3.6 %all-to-all-start.1 = ((bf16[8,32,1920]{2,1,0:T(8,128)(2,1)}), bf16[8,32,1920]{2,1,0:T(8,128)(2,1)S(1)}, u32[]{:S(2)}, u32[]{:S(2)}) async-start(bf16[8,32,1920]{2,1,0:T(8,128)(2,1)} %fusion.2), calls=%async_computation.1 | async-start | bytes 1966080 | tf_op jit(solution)/shard_map/all_to_all | solution.py:263
  54.8 15.1 %all-to-all-done.1 = bf16[8,32,1920]{2,1,0:T(8,128)(2,1)S(1)} async-done(((bf16[8,32,1920]{2,1,0:T(8,128)(2,1)}), bf16[8,32,1920]{2,1,0:T(8,128)(2,1)S(1)}, u32[]{:S(2)}, u32[]{:S(2)}) %all-to-all-start.1) | async-done | bytes 983072 | tf_op jit(solution)/shard_map/all_to_all | solution.py:263
  69.9 0.1 reshape_squeeze.3
  70.1 0.9 collective-permute-start.5
  71.1 1.1 fusion.15
  72.2 0.1 collective-permute-start.4
  72.4 1.3 %collective-permute-done.4 = bf16[256,256]{1,0:T(8,128)(2,1)S(1)} collective-permute-done((bf16[256,256]{1,0:T(8,128)(2,1)S(1)}, bf16[256,256]{1,0:T(8,128)(2,1)S(1)}, u32[]{:S(2)}, u32[]{:S(2)}) %collective-permute-start.4) | collective-permute-done | bytes 131104 | tf_op jit(solution)/shard_map/ppermute | solution.py:267
  73.7 1.1 convolution_add_fusion.1
  74.8 0.5 broadcast.35
  75.3 0.7 reduce.5
  76.0 0.1 reshape.178
  76.1 19.1 %all_to_all.26 = bf16[16,2,1088]{2,1,0:T(2,128)(2,1)S(1)} all-to-all(bf16[16,2,1088]{2,1,0:T(2,128)(2,1)S(1)} %reshape.178), channel_id=1, replica_groups=mesh['yh'=2,'z'=8,'c'=2,'yl'=2,'x'=4] {'yh','z'}, dimensions={0} | all-to-all | bytes 139264 | tf_op jit(solution)/shard_map/all_to_all | solution.py:293
  95.2 0.1 reshape.179
  95.3 0.1 convert_reduce_fusion.2
  95.5 7.5 %all_to_all.27 = f32[8,8,128]{2,1,0:T(8,128)S(1)} all-to-all(f32[8,8,128]{2,1,0:T(8,128)S(1)} %broadcast_in_dim.5), channel_id=1, replica_groups=mesh['yh'=2,'z'=8,'c'=2,'yl'=2,'x'=4] {'yl','x'}, dimensions={0} | all-to-all | bytes 65536 | tf_op jit(solution)/shard_map/all_to_all | solution.py:299
  103.0 6.2 %all-to-all-start.3 = ((bf16[4,32,2048]{2,1,0:T(8,128)(2,1)}), bf16[4,32,2048]{2,1,0:T(8,128)(2,1)S(1)}, u32[]{:S(2)}, u32[]{:S(2)}) async-start(bf16[4,32,2048]{2,1,0:T(8,128)(2,1)} %bitcast.55), calls=%async_computation.4 | async-start | bytes 1048576 | tf_op jit(solution)/shard_map/all_to_all | solution.py:303
  109.2 0.9 slice.116
  110.0 1.1 fusion.1
  111.1 0.5 slice.121
  111.6 0.6 reshape.168
  112.2 6.4 %all-to-all-done.3 = bf16[4,32,2048]{2,1,0:T(8,128)(2,1)S(1)} async-done(((bf16[4,32,2048]{2,1,0:T(8,128)(2,1)}), bf16[4,32,2048]{2,1,0:T(8,128)(2,1)S(1)}, u32[]{:S(2)}, u32[]{:S(2)}) %all-to-all-start.3) | async-done | bytes 524320 | tf_op jit(solution)/shard_map/all_to_all | solution.py:303
  118.6 0.1 convert_element_type.79
  118.8 0.4 add.80
  119.2 0.4 fusion.21
  119.6 0.7 maximum_bitcast_fusion
  120.3 0.7 pad_maximum_fusion.2
  120.9 0.7 pad_maximum_fusion.1
  121.6 0.7 pad_maximum_fusion
  122.3 0.6 copy.77
  (53 shorter events, 1.1 us)
Async XLA Ops:
  7.2 95.8 %reduce-scatter.2.cloned.1.call-start = ((), (), s32[]{:S(2)}) async-start(), calls=%async_computation.6 | async-start | bytes 4718592 | tf_op jit(solution)/shard_map/reduce_scatter | solution.py:229
  7.2 5.1 %collective-permute-start.1 = (bf16[256,1024]{1,0:T(8,128)(2,1)}, bf16[256,1024]{1,0:T(8,128)(2,1)S(1)}, u32[]{:S(2)}, u32[]{:S(2)}) collective-permute-start(bf16[256,1024]{1,0:T(8,128)(2,1)} %cot_own_h.1), channel_id=1, source_target_pairs={{0,8},{8,0},{1,9},{9,1},{2,10},{10,2},{3,11},{11,3},{4,12},{12,4},... | collective-permute-start | bytes 1572872 | tf_op jit(solution)/shard_map/ppermute | solution.py:214
  10.6 2.5 %collective-permute-start = (bf16[256,1024]{1,0:T(8,128)(2,1)}, bf16[256,1024]{1,0:T(8,128)(2,1)S(1)}, u32[]{:S(2)}, u32[]{:S(2)}) collective-permute-start(bf16[256,1024]{1,0:T(8,128)(2,1)} %tok_own_h.1), channel_id=1, source_target_pairs={{0,8},{8,0},{1,9},{9,1},{2,10},{10,2},{3,11},{11,3},{4,12},{12,4},... | collective-permute-start | bytes 1572872 | tf_op jit(solution)/shard_map/ppermute | solution.py:213
  12.3 0.8 copy-start.5
  13.0 0.8 copy-start.7
  29.0 1.1 copy-start.6
  29.0 1.5 %copy-start = (bf16[256,1024]{1,0:T(8,128)(2,1)S(1)}, bf16[256,1024]{1,0:T(8,128)(2,1)}, u32[]{:S(2)}) copy-start(bf16[256,1024]{1,0:T(8,128)(2,1)} %tok_own_h.1) | copy-start | bytes 1572868
  29.0 1.6 %copy-start.3 = (bf16[1024,256]{1,0:T(8,128)(2,1)S(1)}, bf16[1024,256]{1,0:T(8,128)(2,1)}, u32[]{:S(2)}) copy-start(bf16[1024,256]{1,0:T(8,128)(2,1)} %get-tuple-element.15) | copy-start | bytes 1572868
  29.0 3.2 %copy-start.1 = (bf16[256,1280]{1,0:T(8,128)(2,1)S(1)}, bf16[256,1280]{1,0:T(8,128)(2,1)}, u32[]{:S(2)}) copy-start(bf16[256,1280]{1,0:T(8,128)(2,1)} %get-tuple-element.13) | copy-start | bytes 1966084
  30.1 2.1 %collective-permute-start.2 = (bf16[256,1280]{1,0:T(8,128)(2,1)S(1)}, bf16[256,1280]{1,0:T(8,128)(2,1)S(1)}, u32[]{:S(2)}, u32[]{:S(2)}) collective-permute-start(bf16[256,1280]{1,0:T(8,128)(2,1)S(1)} %copy-done.6), channel_id=1, source_target_pairs={{0,8},{8,0},{1,9},{9,1},{2,10},{10,2},{3,11},{11,3},{4,12},{12,4},... | collective-permute-start | bytes 1966088 | tf_op jit(solution)/shard_map/ppermute | solution.py:231
  30.6 6.1 %collective-permute-start.3 = (bf16[16,32,256]{2,1,0:T(8,128)(2,1)S(1)}, bf16[16,32,256]{2,1,0:T(8,128)(2,1)S(1)}, u32[]{:S(2)}, u32[]{:S(2)}) collective-permute-start(bf16[16,32,256]{2,1,0:T(8,128)(2,1)S(1)} %dynamic-slice_bitcast_fusion), channel_id=1, source_target_pairs={{0,8},{8,0},{1,9},{9,1},{2,10},{10,2},{3,11},{11,3},{4,12},{12,4},... | collective-permute-start | bytes 786440 | tf_op jit(solution)/shard_map/ppermute | solution.py:250
  33.2 15.2 %all-to-all-start = ((bf16[8,32,1280]{2,1,0:T(8,128)(2,1)}), bf16[8,32,1280]{2,1,0:T(8,128)(2,1)S(1)}, u32[]{:S(2)}, u32[]{:S(2)}) async-start(bf16[8,32,1280]{2,1,0:T(8,128)(2,1)} %bitcast.2), calls=%async_computation | async-start | bytes 1310720 | tf_op jit(solution)/shard_map/all_to_all | solution.py:233
  36.7 11.7 %copy-start.4 = (f32[1024]{0:T(1024)S(1)}, f32[1024]{0:T(1024)}, u32[]{:S(2)}) copy-start(f32[1024]{0:T(1024)} %param.10) | copy-start | bytes 12292
  51.2 18.6 %all-to-all-start.1 = ((bf16[8,32,1920]{2,1,0:T(8,128)(2,1)}), bf16[8,32,1920]{2,1,0:T(8,128)(2,1)S(1)}, u32[]{:S(2)}, u32[]{:S(2)}) async-start(bf16[8,32,1920]{2,1,0:T(8,128)(2,1)} %fusion.2), calls=%async_computation.1 | async-start | bytes 1966080 | tf_op jit(solution)/shard_map/all_to_all | solution.py:263
  70.1 2.2 %collective-permute-start.5 = (f32[16,4]{1,0:T(8,128)S(1)}, f32[16,4]{1,0:T(8,128)S(1)}, u32[]{:S(2)}, u32[]{:S(2)}) collective-permute-start(f32[16,4]{1,0:T(8,128)S(1)} %bitcast.64), channel_id=1, source_target_pairs={{0,8},{8,0},{1,9},{9,1},{2,10},{10,2},{3,11},{11,3},{4,12},{12,4},... | collective-permute-start | bytes 776 | tf_op jit(solution)/shard_map/ppermute | solution.py:275
  72.1 37.9 %copy-start.2 = (bf16[256,1024]{1,0:T(8,128)(2,1)S(1)}, bf16[256,1024]{1,0:T(8,128)(2,1)}, u32[]{:S(2)}) copy-start(bf16[256,1024]{1,0:T(8,128)(2,1)} %dec_h.1) | copy-start | bytes 1572868
  72.2 1.4 %collective-permute-start.4 = (bf16[256,256]{1,0:T(8,128)(2,1)S(1)}, bf16[256,256]{1,0:T(8,128)(2,1)S(1)}, u32[]{:S(2)}, u32[]{:S(2)}) collective-permute-start(bf16[256,256]{1,0:T(8,128)(2,1)S(1)} %slice.115), channel_id=1, source_target_pairs={{0,8},{8,0},{1,9},{9,1},{2,10},{10,2},{3,11},{11,3},{4,12},{12,4},... | collective-permute-start | bytes 393224 | tf_op jit(solution)/shard_map/ppermute | solution.py:267
  103.0 15.7 %all-to-all-start.3 = ((bf16[4,32,2048]{2,1,0:T(8,128)(2,1)}), bf16[4,32,2048]{2,1,0:T(8,128)(2,1)S(1)}, u32[]{:S(2)}, u32[]{:S(2)}) async-start(bf16[4,32,2048]{2,1,0:T(8,128)(2,1)} %bitcast.55), calls=%async_computation.4 | async-start | bytes 1048576 | tf_op jit(solution)/shard_map/all_to_all | solution.py:303
Sparse Core Ops, SparseCore 0:
  29.2 56.2 reduce-scatter.1

commit v3 on v2

--- a/solution.py
+++ b/solution.py
@@ -1,3 +1,5 @@
+import functools
+
 import jax
 import jax.numpy as jnp
 import numpy as np
@@ -35,9 +37,9 @@
     wk_h,
     wv_h,
     buf_h,
+    keep,
     send,
-    keep,
-    enc_out,
+    first,
     tok,
     cot,
     wq,
@@ -57,7 +59,11 @@
     dq_s,
     dk_s,
     dv_s,
+    code_s,
     stage,
+    rms_s,
+    enc_s,
+    small_s,
     in_sem,
     out_sem,
 ):
@@ -66,6 +72,7 @@
     code = enc.shape[1]
     part = width // (YH * Z)
     core = core_ref[0]
+    far = lax.rem(core_ref[1] + Z // 2, Z)
     mine = pl.ds(pl.multiple_of(core * own, own), own)
     pairs = (
         (tok_own_h, tok.at[pl.ds(0, SEQ)]),
@@ -88,6 +95,7 @@
         copies[s].wait()
         x = tok[at, :].astype(F32)
         rms = lax.rsqrt(jnp.mean(x * x, axis=-1, keepdims=True) + 1e-6)
+        rms_s[at, :] = jnp.broadcast_to(rms, (SEQ, 128))
         norm_s[at, :] = (x * rms * gain[...]).astype(BF16)
     normed = norm_s[...]
     copies[2].wait()
@@ -139,14 +147,61 @@
     out.append(put(2, dot(norm_t[...], dv_s[...])))
     out.append(put(0, dot(norm_t[...], dq_s[...])))
     out.append(put(1, dot(norm_t[...], dk_s[...])))
-    for s, ref in enumerate((keep, send)):
+    for i in range(2):
+        half = YH * part // 2
+        first[i] = stage[far, i * half : (i + 1) * half, :]
+    piece = SEQ // NT
+    code_s[...] = dot(ctx_s[...], w2).astype(BF16)
+    gain_p = jnp.zeros((1, width), F32)
+    for s in range(2):
         at = slice(s * SEQ, (s + 1) * SEQ)
         dn = dot(dq_s[at, :], wq[...], 1, 1)
         dn = dn + dot(dk_s[at, :], wk[...], 1, 1)
         dn = dn + dot(dv_s[at, :], wv[...], 1, 1)
-        ref[:, 0:width] = dn.astype(BF16)
-        ref[:, width : width + code] = dot(ctx_s[at, :], w2).astype(BF16)
-    enc_out[...] = dot(wo[...], g, 0, 0).astype(BF16)
+        unit = tok[at, :].astype(F32) * rms_s[at, 0:1]
+        gain_p = gain_p + jnp.sum(dn * unit, axis=0, keepdims=True)
+        low = dn.astype(BF16)
+        for t in range(NT):
+            here = slice(t * piece, (t + 1) * piece)
+            there = slice(s * SEQ + t * piece, s * SEQ + (t + 1) * piece)
+            ref = (keep, send)[s]
+            ref[t, :, 0:width] = low[here, :]
+            ref[t, :, width : width + code] = code_s[there, :]
+    enc_s[...] = dot(wo[...], g, 0, 0)
+    dec_p = dot(code_s[...], cot[...], 0, 0).astype(BF16)
+    n_yz = YH * Z
+    fine = part // CORES
+    tiny = fine // NT
+    rows = code // n_yz // CORES
+    cols = width // NT
+    blocks = n_yz * rows // piece
+    each = piece // rows
+    base = width + code
+    for cc in range(CORES):
+        small = small_s.at[jnp.where(core == cc, 0, 1)]
+        for t in range(NT):
+            for j in range(blocks):
+                dec_at = j * 2 * cols
+                dec_b, enc_b = [], []
+                for yz in range(j * each, (j + 1) * each):
+                    r = (yz * CORES + cc) * rows
+                    dec_b.append(dec_p[r : r + rows, t * cols : (t + 1) * cols])
+                    e = (yz * CORES + cc) * fine + t * tiny
+                    enc_b.append(enc_s[e : e + tiny, 0:cols])
+                    enc_b.append(enc_s[e : e + tiny, cols : 2 * cols])
+                small[t, :, dec_at : dec_at + cols] = jnp.concatenate(dec_b, axis=0)
+                enc_v = jnp.concatenate(enc_b, axis=0).astype(BF16)
+                small[t, :, dec_at + cols : dec_at + 2 * cols] = enc_v
+    gain_v = jnp.concatenate(
+        [gain_p[:, i * 128 : (i + 1) * 128] for i in range(width // 128)]
+        + [jnp.zeros((piece - width // 128, 128), F32)],
+        axis=0,
+    ).astype(BF16)
+    end = base + blocks * 2 * cols
+    for s, ref in enumerate((keep, send)):
+        ref[:, :, base:end] = small_s[s]
+        for t in range(NT):
+            ref[t, :, end:] = gain_v
     for copy in out:
         copy.wait()
 
@@ -157,11 +212,13 @@
     code = enc.shape[1]
     part = width // (YH * Z)
     sds = jax.ShapeDtypeStruct
+    piece = SEQ // NT
+    lanes = width + code + width + 128
     outs = (
         sds((Z, YH * part, 4 * own), BF16),
-        sds((SEQ, width + code), BF16),
-        sds((SEQ, width + code), BF16),
-        sds((width, code), BF16),
+        sds((NT, piece, lanes), BF16),
+        sds((NT, piece, lanes), BF16),
+        sds((2, YH * part // 2, 4 * own), BF16),
     )
     vmem = pl.BlockSpec(memory_space=pltpu.VMEM)
     hbm = pl.BlockSpec(memory_space=pl.ANY)
@@ -179,6 +236,7 @@
         (width, two),
         (two, code),
         *(((two, own),) * 8),
+        (two, code),
         (Z, YH * part, 4 * own),
     )
     return pl.pallas_call(
@@ -188,6 +246,9 @@
         out_shape=outs,
         scratch_shapes=[
             *(pltpu.VMEM(shape, BF16) for shape in shapes),
+            pltpu.VMEM((two, 128), F32),
+            pltpu.VMEM((width, code), F32),
+            pltpu.VMEM((2, NT, piece, width), BF16),
             pltpu.SemaphoreType.DMA((10,)),
             pltpu.SemaphoreType.DMA((4,)),
         ],
@@ -198,21 +259,55 @@
     )(core, gain, *args)
 
 
+def ring_chunk(buf, z, c, k, sign):
+    turn = k * sign * (1 - 2 * c)
+    return lax.dynamic_index_in_dim(buf, lax.rem(z + turn + Z, Z), 0, keepdims=False)
+
+
+def ring_send(held):
+    return [
+        lax.ppermute(
+            a,
+            ("z", "c"),
+            [
+                (at * CORES + core, (at + sign * (1 - 2 * core)) % Z * CORES + core)
+                for at in range(Z)
+                for core in range(CORES)
+            ],
+        )
+        for a, sign in zip(held, (1, -1), strict=True)
+    ]
+
+
+def ring_add(chunk, k, got):
+    out = []
+    for a, sign in zip(got, (1, -1), strict=True):
+        local = chunk(k, sign)
+        half = local.shape[0] // 2
+        if k < Z // 2 - 1:
+            out.append((local.astype(F32) + a.astype(F32)).astype(BF16))
+            continue
+        rows = slice(0, half) if sign == 1 else slice(half, 2 * half)
+        added = (local[rows].astype(F32) + a.astype(F32)).astype(BF16)
+        parts = [added, local[half:]] if sign == 1 else [local[:half], added]
+        out.append(jnp.concatenate(parts, axis=0))
+    return out
+
+
 def on_device(tokens, gain, w_query, w_key, w_value, w_output, encoder, decoder, cotangent):
     rows, width = tokens.shape
     own = w_query.shape[1] // CORES
     code_w = encoder.shape[1]
     yh, z, c = lax.axis_index("yh"), lax.axis_index("z"), lax.axis_index("c")
     t = lax.axis_index("yl") * X + lax.axis_index("x")
-    n_yz = YH * Z
-    n_dp = n_yz * CORES
+    n_dp = YH * Z * CORES
     fine = width // n_dp
     tiny = fine // NT
-    core = jnp.reshape(c, (1,)).astype(jnp.int32)
+    core = jnp.stack([c, z]).astype(jnp.int32)
 
     tok_oth = lax.ppermute(tokens, "c", SWAP)
     cot_oth = lax.ppermute(cotangent, "c", SWAP)
-    buf, send, keep, enc_p = run_block(
+    buf, keep, send, first = run_block(
         core,
         gain.reshape(1, width),
         tokens,
@@ -226,12 +321,31 @@
         w_key,
         w_value,
     )
-    red = lax.psum_scatter(buf, "z", scatter_dimension=0, tiled=True)
-
+    chunk = functools.partial(ring_chunk, buf, z, c)
+    got = ring_send([first[0], first[1]])
     both = (keep.astype(F32) + lax.ppermute(send, "c", SWAP).astype(F32)).astype(BF16)
+    *got, both = lax.optimization_barrier((*got, both))
+
+    over_t = lax.all_to_all(both, TP, 0, 0, tiled=True)
+    got = ring_send(ring_add(chunk, 3, got))
+    *got, over_t = lax.optimization_barrier((*got, over_t))
+
+    total = jnp.sum(over_t.astype(F32), axis=0)
     piece = rows // NT
-    got = lax.all_to_all(both.reshape(NT, piece, width + code_w), TP, 0, 0, tiled=True)
-    total = jnp.sum(got.astype(F32), axis=0)
+    out_w = width + code_w
+    cols = width // NT
+    dec_rows = code_w // n_dp
+    small = total[:, out_w : out_w + width]
+    small = jnp.concatenate(
+        [small[:, i * 2 * cols : (i + 1) * 2 * cols] for i in range(width // (2 * cols))], axis=0
+    ).reshape(YH * Z, dec_rows, 2 * cols)
+    gain_v = total[: width // 128, out_w + width :]
+    small = jnp.concatenate(
+        [small, jnp.broadcast_to(gain_v[None], (YH * Z, *gain_v.shape))], axis=2
+    ).astype(BF16)
+    small = lax.all_to_all(small, ("yh", "z"), 0, 0, tiled=True)
+    got = ring_send(ring_add(chunk, 2, got))
+
     dnormed = total[:, :width]
     x = lax.dynamic_slice_in_dim(tokens, t * piece, piece, 0).astype(F32)
     cot = lax.dynamic_slice_in_dim(cotangent, t * piece, piece, 0).astype(F32)
@@ -240,73 +354,44 @@
     dunit = dnormed * gain
     inner = jnp.sum(dunit * unit, axis=-1, keepdims=True) / width
     grad_rows = cot + rms * (dunit - unit * inner)
-    gain_row = jnp.sum(dnormed * unit, axis=0)
-    gain_by_t = gain_row.reshape(n_dp, NT, tiny).transpose(1, 0, 2).reshape(NT, 1, -1)
-    gain_w = n_dp * tiny
-
-    enc_p = enc_p.reshape(n_yz, CORES, fine, code_w)
-    enc_keep = lax.dynamic_index_in_dim(enc_p, c, 1, keepdims=False)
-    enc_send = lax.dynamic_index_in_dim(enc_p, 1 - c, 1, keepdims=False)
-    enc_c = enc_keep.astype(F32) + lax.ppermute(enc_send, "c", SWAP).astype(F32)
-    enc_c = enc_c.astype(BF16).reshape(n_yz, NT, tiny, code_w).transpose(1, 0, 2, 3)
-    enc_c = enc_c.reshape(NT, n_yz * tiny, code_w)
-
-    first = jnp.concatenate([grad_rows, total[:, width:]], axis=1).astype(BF16)
-    out_w = width + code_w
-    half = n_yz * tiny // 2
-    enc_c = jnp.concatenate([enc_c[:, :half], enc_c[:, half:]], axis=2)
-    enc_c = jnp.pad(enc_c, ((0, 0), (0, piece - half), (0, 0)))
-    gain_b = jnp.pad(gain_by_t, ((0, 0), (0, piece - 1), (0, -gain_w % 128))).astype(BF16)
-    packed = jnp.concatenate(
-        [jnp.broadcast_to(first[None], (NT, piece, out_w)), enc_c, gain_b], axis=2
-    )
-    got = lax.all_to_all(packed, TP, 0, 0, tiled=True)
-    whole_rows = got[:, :, :out_w].reshape(rows, out_w)
+    mine = jnp.concatenate([grad_rows, total[:, width:out_w]], axis=1).astype(BF16)
+    *got, small, mine = lax.optimization_barrier((*got, small, mine))
+
+    small = jnp.sum(small.astype(F32), axis=0)
+    enc_v = small[:, cols : 2 * cols]
+    grad_encoder = jnp.concatenate([enc_v[:tiny], enc_v[tiny:]], axis=1)
+    at = (((yh * Z + z) * CORES + c) * NT + t) * tiny
+    grad_gain = lax.dynamic_slice(small, (at // 128, 2 * cols + at % 128), (1, tiny))[0]
+
+    dec_b = jnp.pad(small[:, :cols].astype(BF16), ((0, piece - dec_rows), (0, 0)))
+    mine = jnp.concatenate([mine, dec_b], axis=1)
+    over_t = lax.all_to_all(
+        jnp.broadcast_to(mine[None], (NT, *mine.shape)), TP, 0, 0, tiled=True
+    )
+    got = ring_send(ring_add(chunk, 1, got))
+    red = chunk(0, 1).astype(F32) + got[0].astype(F32) + got[1].astype(F32)
+    red = red.astype(BF16)
+    whole_rows = over_t[:, :, :out_w].reshape(rows, out_w)
     grad_input = whole_rows[:, :width]
-    code = whole_rows[:, width:]
-    code_oth = lax.ppermute(code, "c", SWAP)
-    sums = jnp.sum(got[:, :, out_w:].astype(F32), axis=0)
-    enc_t = jnp.concatenate(
-        [sums[:half, :code_w], sums[:half, code_w : 2 * code_w]], axis=0
-    ).reshape(n_yz, -1)
-    gain_sum = sums[0, 2 * code_w : 2 * code_w + gain_w].reshape(n_yz, CORES, tiny)
-    gain_keep = lax.dynamic_index_in_dim(gain_sum, c, 1, keepdims=False)
-    gain_send = lax.dynamic_index_in_dim(gain_sum, 1 - c, 1, keepdims=False)
-    gain_keep = gain_keep + lax.ppermute(gain_send, "c", SWAP)
-
-    cols = width // NT
-    cot_own_c = lax.dynamic_slice_in_dim(cotangent, t * cols, cols, 1)
-    cot_oth_c = lax.dynamic_slice_in_dim(cot_oth, t * cols, cols, 1)
-    dec_p = dot(code, cot_own_c, 0, 0) + dot(code_oth, cot_oth_c, 0, 0)
-    dec_rows = code_w // n_dp
-    dec_p = dec_p.reshape(n_yz, CORES, dec_rows, cols)
-    dec_p = lax.dynamic_index_in_dim(dec_p, c, 1, keepdims=False)
-
-    flat = jnp.concatenate(
-        [
-            dec_p.reshape(n_yz, -1),
-            enc_t,
-            jnp.pad(gain_keep, ((0, 0), (0, 128 - tiny))),
-        ],
-        axis=1,
-    ).astype(BF16)
-    got = lax.all_to_all(flat, ("yh", "z"), 0, 0, tiled=True)
-    tail = jnp.sum(got.astype(F32), axis=0)
-    d_size, e_size = dec_rows * cols, tiny * code_w
-    grad_encoder = tail[d_size : d_size + e_size].reshape(tiny, code_w)
-    grad_gain = tail[d_size + e_size : d_size + e_size + tiny]
-    dec_sum = jnp.broadcast_to(tail[:d_size].reshape(1, dec_rows, cols), (NT, dec_rows, cols))
-    got = lax.all_to_all(dec_sum, TP, 0, 0, tiled=True)
-    grad_decoder = got.transpose(1, 0, 2).reshape(dec_rows, width)
-    output = (tokens.astype(F32) + dot(code, decoder)).astype(BF16)
-
-    got = lax.all_to_all(
-        red.reshape(YH * CORES, fine, 4 * own), ("yh", "c"), 0, 0, tiled=True
-    )
-    got = got.reshape(YH, CORES, fine, 4, own).astype(F32)
-    grads = got[0] + got[1]
+    output = (tokens.astype(F32) + dot(whole_rows[:, width:], decoder)).astype(BF16)
+    grad_decoder = over_t[:, :dec_rows, out_w:].astype(F32)
+    grad_decoder = grad_decoder.transpose(1, 0, 2).reshape(dec_rows, width)
+
+    red = red.reshape(YH, CORES * fine, 4 * own)
+    away = lax.dynamic_index_in_dim(red, 1 - yh, 0, keepdims=False)
+    here = lax.dynamic_index_in_dim(red, yh, 0, keepdims=False)
+    both = here.astype(F32) + lax.ppermute(away, "yh", SWAP).astype(F32)
+    both = both.astype(BF16).reshape(CORES, fine, 4 * own)
+    here = lax.dynamic_index_in_dim(both, c, 0, keepdims=False)
+    away = lax.dynamic_index_in_dim(both, 1 - c, 0, keepdims=False)
+    away = lax.ppermute(away, "c", SWAP)
+    low = jnp.where(c == 0, here, away).astype(F32)
+    high = jnp.where(c == 0, away, here).astype(F32)
     grads = [
-        jnp.concatenate([grads[0, :, i], grads[1, :, i]], axis=1) for i in range(4)
+        jnp.concatenate(
+            [low[:, i * own : (i + 1) * own], high[:, i * own : (i + 1) * own]], axis=1
+        )
+        for i in range(4)
     ]
     return (
         output,

time: 130 us -> 114 us (0.88)
  blocking collectives: 26.6 us -> 0 us
  starting transfers between devices: 18.6 us -> 33.6 us
  between operations: 14.4 us -> 0.86 us
  other arithmetic: 7.18 us -> 15.6 us
  waiting for transfers between devices: 37.5 us -> 41.1 us
  matrix products: 3.24 us -> 1.1 us
  local copies, waits for them, and re-layouts: 7.05 us -> 5.45 us
    all_to_all x2 -> x0, blocking collectives: 26.6 us -> none  [the longest x1 19.1 us: on_device(): got = lax.all_to_all(flat, ('yh', 'z'), 0, 0, tiled=True)]
    ppermute x3 -> x10, waiting for transfers between devices: 1.3 us -> 25 us  [the longest x8 21.7 us: ring_send(): lax.ppermute(a, ('z', 'c'), [(at * CORES + core, (at + sign * (1 - 2 * co...]
    all_to_all x3, waiting for transfers between devices: 32.7 us -> 14.3 us  [the longest x1 9.12 us: on_device(): small = lax.all_to_all(small, ('yh', 'z'), 0, 0, tiled=True)]
    ppermute x3 -> x10, starting transfers between devices: 1.44 us -> 14.1 us  [the longest x8 11.6 us: ring_send(): lax.ppermute(a, ('z', 'c'), [(at * CORES + core, (at + sign * (1 - 2 * co...]
    convert_element_type x2 -> x6, other arithmetic: 0.18 us -> 6.74 us  [the longest x2 4.14 us: ring_add(): out.append((local.astype(F32) + a.astype(F32)).astype(BF16))]
    ppermute x1, starting transfers between devices: 3.33 us -> 0.1 us  [on_device(): cot_oth = lax.ppermute(cotangent, 'c', SWAP)]
    ppermute x1, starting transfers between devices: 0.1 us -> 3.33 us  [on_device(): tok_oth = lax.ppermute(tokens, 'c', SWAP)]
    all_to_all x3, starting transfers between devices: 13.3 us -> 15.4 us  [the longest x1 6.4 us: on_device(): small = lax.all_to_all(small, ('yh', 'z'), 0, 0, tiled=True)]
  transfers between devices with their start and end apart: 10 -> 16, of which waited for: 7 -> 13; matrix products, arithmetic and copies ran while one was open for 9% -> 12% of each run, Pallas kernels for 0% -> 0%
where the time goes in v3:
time: 114 us
  waiting for transfers between devices  41.1 us (36%)
  starting transfers between devices  33.6 us (29%)
  Pallas kernels  16 us (14%)
  other arithmetic  15.6 us (14%)
  local copies, waits for them, and re-layouts  5.45 us (5%)
    ppermute x8, waiting for transfers between devices, ring_send(): lax.ppermute(a, ('z', 'c'), [(at * CORES + core, (at + sign * (1 - 2 * co...  21.7 us
    pallas_call x1, Pallas kernels, run_block(): pl.pallas_call(block_kernel, in_specs=[pl.BlockSpec(memory_space=pltpu.SM...  16 us
    ppermute x8, starting transfers between devices, ring_send(): lax.ppermute(a, ('z', 'c'), [(at * CORES + core, (at + sign * (1 - 2 * co...  11.6 us
    all_to_all x1, waiting for transfers between devices, on_device(): small = lax.all_to_all(small, ('yh', 'z'), 0, 0, tiled=True)  9.12 us
    all_to_all x1, starting transfers between devices, on_device(): small = lax.all_to_all(small, ('yh', 'z'), 0, 0, tiled=True)  6.4 us
    all_to_all x1, starting transfers between devices, on_device(): over_t = lax.all_to_all(both, TP, 0, 0, tiled=True)  5.03 us
    convert_element_type x2, other arithmetic, ring_add(): out.append((local.astype(F32) + a.astype(F32)).astype(BF16))  4.14 us
    all_to_all x1, starting transfers between devices, on_device(): lax.all_to_all(jnp.broadcast_to(mine[None], (NT, *mine.shape)), TP, 0, 0,...  4.02 us
  transfers between devices with their start and end apart: 16, of which 13 were waited for; matrix products, arithmetic and copies ran while one was open for 12% of the time, Pallas kernels for 0%

profile of v3, /device:TPU:1, one launch (start us, length us, event | category | flops | bytes accessed | tf_op | source)
XLA Modules:
  0.0 113.7 jit_solution(4637619637625451778)
XLA Ops:
  0.6 3.3 %collective-permute-start = (bf16[256,1024]{1,0:T(8,128)(2,1)}, bf16[256,1024]{1,0:T(8,128)(2,1)S(1)}, u32[]{:S(2)}, u32[]{:S(2)}) collective-permute-start(bf16[256,1024]{1,0:T(8,128)(2,1)} %tok_own_h.1), channel_id=1, source_target_pairs={{0,8},{8,0},{1,9},{9,1},{2,10},{10,2},{3,11},{11,3},{4,12},{12,4},... | collective-permute-start | bytes 1572872 | tf_op jit(solution)/shard_map/ppermute | solution.py:308
  4.1 0.6 pad_add_fusion.core_ref
  4.7 1.1 collective-permute-done.tok_oth_h
  5.7 0.7 collective-permute-done.1.cot_oth_h
  6.5 0.7 copy-done.5
  7.3 16.0 %shard_map.160 = (bf16[8,128,2048]{2,1,0:T(8,128)(2,1)}, bf16[8,32,2432]{2,1,0:T(8,128)(2,1)}, bf16[8,32,2432]{2,1,0:T(8,128)(2,1)}, bf16[2,64,2048]{2,1,0:T(8,128)(2,1)}) custom-call(s32[2]{0:T(128)} %pad_add_fusion.core_ref, f32[1,1024]{1,0:T(1,128)} %bitcast.70, bf16[256,1024]{1,0:T(8,128)(2,1)} %tok_own_h.1, bf16[256,1024]{1,0:T(8,128)(2,1)} %copy-done.4, ...), custom_call_target="tpu_custom_call" | custom-call | flops 7500000256 | bytes 14000000 | tf_op jit(solution)/shard_map/pallas_call | solution.py:242
  23.3 0.6 collective-permute-start.4
  23.9 1.1 slice_bitcast_fusion
  25.0 3.9 %collective-permute-start.2 = (bf16[64,2048]{1,0:T(8,128)(2,1)S(1)}, bf16[64,2048]{1,0:T(8,128)(2,1)S(1)}, u32[]{:S(2)}, u32[]{:S(2)}) collective-permute-start(bf16[64,2048]{1,0:T(8,128)(2,1)S(1)} %get-tuple-element.46), channel_id=1, source_target_pairs={{0,16},{8,120},{16,32},{24,8},{32,48},{40,24},{48,64},{56,40},{64,... | collective-permute-start | bytes 786440 | tf_op jit(solution)/shard_map/ppermute | solution.py:269
  28.9 1.1 dynamic-slice_bitcast_fusion.1
  30.0 1.4 %add_convert_fusion = bf16[8,32,2432]{2,1,0:T(8,128)(2,1)} fusion(bf16[8,32,2432]{2,1,0:T(8,128)(2,1)S(1)} %collective-permute-done.4, bf16[8,32,2432]{2,1,0:T(8,128)(2,1)S(1)} %copy-done), kind=kLoop, calls=%fused_computation.1 | loop fusion | flops 2490368 | bytes 3735552 | tf_op jit(solution)/shard_map/convert_element_type | solution.py:326
  31.4 3.0 %collective-permute-done.2 = bf16[64,2048]{1,0:T(8,128)(2,1)S(1)} collective-permute-done((bf16[64,2048]{1,0:T(8,128)(2,1)S(1)}, bf16[64,2048]{1,0:T(8,128)(2,1)S(1)}, u32[]{:S(2)}, u32[]{:S(2)}) %collective-permute-start.2) | collective-permute-done | bytes 262176 | tf_op jit(solution)/shard_map/ppermute | solution.py:269
  34.4 1.4 %collective-permute-done.3 = bf16[64,2048]{1,0:T(8,128)(2,1)S(1)} collective-permute-done((bf16[64,2048]{1,0:T(8,128)(2,1)S(1)}, bf16[64,2048]{1,0:T(8,128)(2,1)S(1)}, u32[]{:S(2)}, u32[]{:S(2)}) %collective-permute-start.3) | collective-permute-done | bytes 262176 | tf_op jit(solution)/shard_map/ppermute | solution.py:269
  35.8 5.0 %all-to-all-start = ((bf16[8,32,2432]{2,1,0:T(8,128)(2,1)}), bf16[8,32,2432]{2,1,0:T(8,128)(2,1)S(1)}, u32[]{:S(2)}, u32[]{:S(2)}) async-start(bf16[8,32,2432]{2,1,0:T(8,128)(2,1)} %add_convert_fusion), calls=%async_computation | async-start | bytes 2490368 | tf_op jit(solution)/shard_map/all_to_all | solution.py:329
  40.8 1.2 %fusion.8 = (bf16[64,2048]{1,0:T(8,128)(2,1)S(1)}, bf16[64,2048]{1,0:T(8,128)(2,1)S(1)}) fusion(bf16[64,2048]{1,0:T(8,128)(2,1)S(1)} %collective-permute-done.3, bf16[8,128,2048]{2,1,0:T(8,128)(2,1)} %get-tuple-element.23, s32[]{:T(128)S(6)} %select_n.71, s32[]{:T(128)S(6)} %add.206, bf16[64,2048]{1,0:T(8,128)(2,1)S(1)} %collective-permute-done.2, ...), kind=kLoop, calls=%fused_computation.20 | loop fusion | flops 1048576 | bytes 1572876 | tf_op jit(solution)/shard_map/convert_element_type | solution.py:291
  42.2 0.8 pad_maximum_fusion
  43.0 2.7 %collective-permute-start.5 = (bf16[128,2048]{1,0:T(8,128)(2,1)}, bf16[128,2048]{1,0:T(8,128)(2,1)S(1)}, u32[]{:S(2)}, u32[]{:S(2)}) collective-permute-start(bf16[128,2048]{1,0:T(8,128)(2,1)} %pad_maximum_fusion), channel_id=1, source_target_pairs={{0,16},{8,120},{16,32},{24,8},{32,48},{40,24},{48,64},{56,40},{64,... | collective-permute-start | bytes 1572872 | tf_op jit(solution)/shard_map/ppermute | solution.py:269
  45.8 6.4 %collective-permute-done.6 = bf16[128,2048]{1,0:T(8,128)(2,1)} collective-permute-done((bf16[128,2048]{1,0:T(8,128)(2,1)S(1)}, bf16[128,2048]{1,0:T(8,128)(2,1)}, u32[]{:S(2)}, u32[]{:S(2)}) %collective-permute-start.6) | collective-permute-done | bytes 524320 | tf_op jit(solution)/shard_map/ppermute | solution.py:269
  52.2 5.5 %collective-permute-done.5 = bf16[128,2048]{1,0:T(8,128)(2,1)S(1)} collective-permute-done((bf16[128,2048]{1,0:T(8,128)(2,1)}, bf16[128,2048]{1,0:T(8,128)(2,1)S(1)}, u32[]{:S(2)}, u32[]{:S(2)}) %collective-permute-start.5) | collective-permute-done | bytes 524320 | tf_op jit(solution)/shard_map/ppermute | solution.py:269
  57.7 1.2 %all-to-all-done = bf16[8,32,2432]{2,1,0:T(8,128)(2,1)S(1)} async-done(((bf16[8,32,2432]{2,1,0:T(8,128)(2,1)}), bf16[8,32,2432]{2,1,0:T(8,128)(2,1)S(1)}, u32[]{:S(2)}, u32[]{:S(2)}) %all-to-all-start) | async-done | bytes 1245216 | tf_op jit(solution)/shard_map/all_to_all | solution.py:329
  59.4 1.7 %fusion.5 = (bf16[128,2048]{1,0:T(8,128)(2,1)S(1)}, bf16[128,2048]{1,0:T(8,128)(2,1)S(1)}) fusion(bf16[128,2048]{1,0:T(8,128)(2,1)} %collective-permute-done.6, bf16[8,128,2048]{2,1,0:T(8,128)(2,1)} %get-tuple-element.23, s32[]{:T(128)S(6)} %select_n.72, bf16[128,2048]{1,0:T(8,128)(2,1)S(1)} %collective-permute-done.5, s32[]{:T(128)S(6)} %select_n.69), kind=kLoop, calls=%fused_computation.12 | loop fusion | flops 2097152 | bytes 3145736 | tf_op jit(solution)/shard_map/convert_element_type | solution.py:288
  61.1 2.3 %collective-permute-start.7 = (bf16[128,2048]{1,0:T(8,128)(2,1)S(1)}, bf16[128,2048]{1,0:T(8,128)(2,1)S(1)}, u32[]{:S(2)}, u32[]{:S(2)}) collective-permute-start(bf16[128,2048]{1,0:T(8,128)(2,1)S(1)} %get-tuple-element.40), channel_id=1, source_target_pairs={{0,16},{8,120},{16,32},{24,8},{32,48},{40,24},{48,64},{56,40},{64,... | collective-permute-start | bytes 1572872 | tf_op jit(solution)/shard_map/ppermute | solution.py:269
  63.4 0.7 pad_maximum_fusion.5
  64.1 6.4 %all-to-all-start.1 = ((bf16[16,8,384]{2,1,0:T(8,128)(2,1)}), bf16[16,8,384]{2,1,0:T(8,128)(2,1)S(1)}, u32[]{:S(2)}, u32[]{:S(2)}) async-start(bf16[16,8,384]{2,1,0:T(8,128)(2,1)} %pad_maximum_fusion.5), calls=%async_computation.1 | async-start | bytes 196608 | tf_op jit(solution)/shard_map/all_to_all | solution.py:346
  70.5 0.9 fusion.17
  71.4 9.1 %all-to-all-done.1 = bf16[16,8,384]{2,1,0:T(8,128)(2,1)S(1)} async-done(((bf16[16,8,384]{2,1,0:T(8,128)(2,1)}), bf16[16,8,384]{2,1,0:T(8,128)(2,1)S(1)}, u32[]{:S(2)}, u32[]{:S(2)}) %all-to-all-start.1) | async-done | bytes 98336 | tf_op jit(solution)/shard_map/all_to_all | solution.py:346
  80.6 2.4 %fusion.2 = (bf16[128,2048]{1,0:T(8,128)(2,1)S(1)}, bf16[128,2048]{1,0:T(8,128)(2,1)}) fusion(bf16[128,2048]{1,0:T(8,128)(2,1)S(1)} %collective-permute-done.7, bf16[8,128,2048]{2,1,0:T(8,128)(2,1)} %get-tuple-element.23, s32[]{:T(128)S(6)} %select_n.80, bf16[128,2048]{1,0:T(8,128)(2,1)S(1)} %collective-permute-done.8, s32[]{:T(128)S(6)} %select_n.81), kind=kLoop, calls=%fused_computation.7 | loop fusion | flops 2097152 | bytes 3145736 | tf_op jit(solution)/shard_map/convert_element_type | solution.py:288
  83.0 2.0 %collective-permute-start.10 = (bf16[128,2048]{1,0:T(8,128)(2,1)}, bf16[128,2048]{1,0:T(8,128)(2,1)S(1)}, u32[]{:S(2)}, u32[]{:S(2)}) collective-permute-start(bf16[128,2048]{1,0:T(8,128)(2,1)} %get-tuple-element.38), channel_id=1, source_target_pairs={{0,112},{8,24},{16,0},{24,40},{32,16},{40,56},{48,32},{56,72},{64,... | collective-permute-start | bytes 1572872 | tf_op jit(solution)/shard_map/ppermute | solution.py:269
  84.9 0.7 collective-permute-start.9
  85.7 0.9 broadcast_in_dim.5
  86.6 4.0 %all-to-all-start.2 = ((bf16[8,32,1408]{2,1,0:T(8,128)(2,1)}), bf16[8,32,1408]{2,1,0:T(8,128)(2,1)S(1)}, u32[]{:S(2)}, u32[]{:S(2)}) async-start(bf16[8,32,1408]{2,1,0:T(8,128)(2,1)} %broadcast_in_dim.5), calls=%async_computation.2 | async-start | bytes 1441792 | tf_op jit(solution)/shard_map/all_to_all | solution.py:368
  90.6 0.6 dynamic-slice_bitcast_fusion.6
  91.2 0.6 pad_maximum_fusion.7
  91.8 2.2 %collective-permute-done.10 = bf16[128,2048]{1,0:T(8,128)(2,1)S(1)} collective-permute-done((bf16[128,2048]{1,0:T(8,128)(2,1)}, bf16[128,2048]{1,0:T(8,128)(2,1)S(1)}, u32[]{:S(2)}, u32[]{:S(2)}) %collective-permute-start.10) | collective-permute-done | bytes 524320 | tf_op jit(solution)/shard_map/ppermute | solution.py:269
  94.0 3.2 %collective-permute-done.9 = bf16[128,2048]{1,0:T(8,128)(2,1)S(1)} collective-permute-done((bf16[128,2048]{1,0:T(8,128)(2,1)S(1)}, bf16[128,2048]{1,0:T(8,128)(2,1)S(1)}, u32[]{:S(2)}, u32[]{:S(2)}) %collective-permute-start.9) | collective-permute-done | bytes 524320 | tf_op jit(solution)/shard_map/ppermute | solution.py:269
  97.2 1.3 %fusion.4 = bf16[128,2048]{1,0:T(8,128)(2,1)S(1)} fusion(bf16[128,2048]{1,0:T(8,128)(2,1)S(1)} %collective-permute-done.10, bf16[128,2048]{1,0:T(8,128)(2,1)S(1)} %collective-permute-done.9, bf16[8,128,2048]{2,1,0:T(8,128)(2,1)} %get-tuple-element.23, s32[]{:T(128)S(6)} %select_n.79), kind=kLoop, calls=%fused_computation.10 | loop fusion | flops 1572864 | bytes 2097156 | tf_op jit(solution)/shard_map/convert_element_type | solution.py:373
  98.5 0.4 collective-permute-start.11
  99.0 3.9 %all-to-all-done.2 = bf16[8,32,1408]{2,1,0:T(8,128)(2,1)S(1)} async-done(((bf16[8,32,1408]{2,1,0:T(8,128)(2,1)}), bf16[8,32,1408]{2,1,0:T(8,128)(2,1)S(1)}, u32[]{:S(2)}, u32[]{:S(2)}) %all-to-all-start.2) | async-done | bytes 720928 | tf_op jit(solution)/shard_map/all_to_all | solution.py:368
  102.9 0.9 slice.146
  103.8 1.1 fusion
  104.9 2.9 %collective-permute-done.11 = bf16[64,2048]{1,0:T(8,128)(2,1)S(1)} collective-permute-done((bf16[64,2048]{1,0:T(8,128)(2,1)S(1)}, bf16[64,2048]{1,0:T(8,128)(2,1)S(1)}, u32[]{:S(2)}, u32[]{:S(2)}) %collective-permute-start.11) | collective-permute-done | bytes 262176 | tf_op jit(solution)/shard_map/ppermute | solution.py:383
  107.9 2.1 %collective-permute-start.12 = (bf16[32,2048]{1,0:T(8,128)(2,1)S(1)}, bf16[32,2048]{1,0:T(8,128)(2,1)S(1)}, u32[]{:S(2)}, u32[]{:S(2)}) collective-permute-start(bf16[32,2048]{1,0:T(8,128)(2,1)S(1)} %dynamic-slice_bitcast_fusion.5), channel_id=1, source_target_pairs={{0,8},{8,0},{1,9},{9,1},{2,10},{10,2},{3,11},{11,3},{4,12},{12,4},... | collective-permute-start | bytes 393224 | tf_op jit(solution)/shard_map/ppermute | solution.py:387
  110.0 0.6 convert_bitcast_fusion
  110.6 0.4 collective-permute-done.12
  111.1 0.7 maximum_bitcast_fusion
  111.7 0.7 pad_maximum_fusion.4
  112.4 0.7 pad_maximum_fusion.3
  113.1 0.7 pad_maximum_fusion.2
  (40 shorter events, 1.1 us)
Async XLA Ops:
  0.6 5.1 %collective-permute-start = (bf16[256,1024]{1,0:T(8,128)(2,1)}, bf16[256,1024]{1,0:T(8,128)(2,1)S(1)}, u32[]{:S(2)}, u32[]{:S(2)}) collective-permute-start(bf16[256,1024]{1,0:T(8,128)(2,1)} %tok_own_h.1), channel_id=1, source_target_pairs={{0,8},{8,0},{1,9},{9,1},{2,10},{10,2},{3,11},{11,3},{4,12},{12,4},... | collective-permute-start | bytes 1572872 | tf_op jit(solution)/shard_map/ppermute | solution.py:308
  4.0 2.5 %collective-permute-start.1 = (bf16[256,1024]{1,0:T(8,128)(2,1)}, bf16[256,1024]{1,0:T(8,128)(2,1)S(1)}, u32[]{:S(2)}, u32[]{:S(2)}) collective-permute-start(bf16[256,1024]{1,0:T(8,128)(2,1)} %cot_own_h.1), channel_id=1, source_target_pairs={{0,8},{8,0},{1,9},{9,1},{2,10},{10,2},{3,11},{11,3},{4,12},{12,4},... | collective-permute-start | bytes 1572872 | tf_op jit(solution)/shard_map/ppermute | solution.py:309
  5.7 0.8 copy-start.4
  6.5 0.8 copy-start.5
  23.3 6.7 %copy-start = (bf16[8,32,2432]{2,1,0:T(8,128)(2,1)S(1)}, bf16[8,32,2432]{2,1,0:T(8,128)(2,1)}, u32[]{:S(2)}) copy-start(bf16[8,32,2432]{2,1,0:T(8,128)(2,1)} %get-tuple-element.25) | copy-start | bytes 3735556
  23.3 6.7 %collective-permute-start.4 = (bf16[8,32,2432]{2,1,0:T(8,128)(2,1)}, bf16[8,32,2432]{2,1,0:T(8,128)(2,1)S(1)}, u32[]{:S(2)}, u32[]{:S(2)}) collective-permute-start(bf16[8,32,2432]{2,1,0:T(8,128)(2,1)} %get-tuple-element.26), channel_id=1, source_target_pairs={{0,8},{8,0},{1,9},{9,1},{2,10},{10,2},{3,11},{11,3},{4,12},{12,4},... | collective-permute-start | bytes 3735560 | tf_op jit(solution)/shard_map/ppermute | solution.py:326
  25.0 9.4 %collective-permute-start.2 = (bf16[64,2048]{1,0:T(8,128)(2,1)S(1)}, bf16[64,2048]{1,0:T(8,128)(2,1)S(1)}, u32[]{:S(2)}, u32[]{:S(2)}) collective-permute-start(bf16[64,2048]{1,0:T(8,128)(2,1)S(1)} %get-tuple-element.46), channel_id=1, source_target_pairs={{0,16},{8,120},{16,32},{24,8},{32,48},{40,24},{48,64},{56,40},{64,... | collective-permute-start | bytes 786440 | tf_op jit(solution)/shard_map/ppermute | solution.py:269
  28.9 6.9 %collective-permute-start.3 = (bf16[64,2048]{1,0:T(8,128)(2,1)S(1)}, bf16[64,2048]{1,0:T(8,128)(2,1)S(1)}, u32[]{:S(2)}, u32[]{:S(2)}) collective-permute-start(bf16[64,2048]{1,0:T(8,128)(2,1)S(1)} %get-tuple-element.45), channel_id=1, source_target_pairs={{0,112},{8,24},{16,0},{24,40},{32,16},{40,56},{48,32},{56,72},{64,... | collective-permute-start | bytes 786440 | tf_op jit(solution)/shard_map/ppermute | solution.py:269
  35.8 23.1 %all-to-all-start = ((bf16[8,32,2432]{2,1,0:T(8,128)(2,1)}), bf16[8,32,2432]{2,1,0:T(8,128)(2,1)S(1)}, u32[]{:S(2)}, u32[]{:S(2)}) async-start(bf16[8,32,2432]{2,1,0:T(8,128)(2,1)} %add_convert_fusion), calls=%async_computation | async-start | bytes 2490368 | tf_op jit(solution)/shard_map/all_to_all | solution.py:329
  40.8 4.9 %copy-start.1 = (bf16[256,1024]{1,0:T(8,128)(2,1)S(1)}, bf16[256,1024]{1,0:T(8,128)(2,1)}, u32[]{:S(2)}) copy-start(bf16[256,1024]{1,0:T(8,128)(2,1)} %tok_own_h.1) | copy-start | bytes 1572868
  42.1 17.1 %copy-start.3 = (f32[1024]{0:T(1024)S(1)}, f32[1024]{0:T(1024)}, u32[]{:S(2)}) copy-start(f32[1024]{0:T(1024)} %param.10) | copy-start | bytes 12292
  42.1 10.1 %collective-permute-start.6 = (bf16[128,2048]{1,0:T(8,128)(2,1)S(1)}, bf16[128,2048]{1,0:T(8,128)(2,1)}, u32[]{:S(2)}, u32[]{:S(2)}) collective-permute-start(bf16[128,2048]{1,0:T(8,128)(2,1)S(1)} %pad_maximum_fusion.1), channel_id=1, source_target_pairs={{0,112},{8,24},{16,0},{24,40},{32,16},{40,56},{48,32},{56,72},{64,... | collective-permute-start | bytes 1572872 | tf_op jit(solution)/shard_map/ppermute | solution.py:269
  43.0 14.7 %collective-permute-start.5 = (bf16[128,2048]{1,0:T(8,128)(2,1)}, bf16[128,2048]{1,0:T(8,128)(2,1)S(1)}, u32[]{:S(2)}, u32[]{:S(2)}) collective-permute-start(bf16[128,2048]{1,0:T(8,128)(2,1)} %pad_maximum_fusion), channel_id=1, source_target_pairs={{0,16},{8,120},{16,32},{24,8},{32,48},{40,24},{48,64},{56,40},{64,... | collective-permute-start | bytes 1572872 | tf_op jit(solution)/shard_map/ppermute | solution.py:269
  61.1 19.4 %collective-permute-start.7 = (bf16[128,2048]{1,0:T(8,128)(2,1)S(1)}, bf16[128,2048]{1,0:T(8,128)(2,1)S(1)}, u32[]{:S(2)}, u32[]{:S(2)}) collective-permute-start(bf16[128,2048]{1,0:T(8,128)(2,1)S(1)} %get-tuple-element.40), channel_id=1, source_target_pairs={{0,16},{8,120},{16,32},{24,8},{32,48},{40,24},{48,64},{56,40},{64,... | collective-permute-start | bytes 1572872 | tf_op jit(solution)/shard_map/ppermute | solution.py:269
  63.4 17.2 %collective-permute-start.8 = (bf16[128,2048]{1,0:T(8,128)(2,1)S(1)}, bf16[128,2048]{1,0:T(8,128)(2,1)S(1)}, u32[]{:S(2)}, u32[]{:S(2)}) collective-permute-start(bf16[128,2048]{1,0:T(8,128)(2,1)S(1)} %get-tuple-element.39), channel_id=1, source_target_pairs={{0,112},{8,24},{16,0},{24,40},{32,16},{40,56},{48,32},{56,72},{64,... | collective-permute-start | bytes 1572872 | tf_op jit(solution)/shard_map/ppermute | solution.py:269
  64.1 16.5 %all-to-all-start.1 = ((bf16[16,8,384]{2,1,0:T(8,128)(2,1)}), bf16[16,8,384]{2,1,0:T(8,128)(2,1)S(1)}, u32[]{:S(2)}, u32[]{:S(2)}) async-start(bf16[16,8,384]{2,1,0:T(8,128)(2,1)} %pad_maximum_fusion.5), calls=%async_computation.1 | async-start | bytes 196608 | tf_op jit(solution)/shard_map/all_to_all | solution.py:346
  83.0 11.0 %collective-permute-start.10 = (bf16[128,2048]{1,0:T(8,128)(2,1)}, bf16[128,2048]{1,0:T(8,128)(2,1)S(1)}, u32[]{:S(2)}, u32[]{:S(2)}) collective-permute-start(bf16[128,2048]{1,0:T(8,128)(2,1)} %get-tuple-element.38), channel_id=1, source_target_pairs={{0,112},{8,24},{16,0},{24,40},{32,16},{40,56},{48,32},{56,72},{64,... | collective-permute-start | bytes 1572872 | tf_op jit(solution)/shard_map/ppermute | solution.py:269
  84.9 12.3 %collective-permute-start.9 = (bf16[128,2048]{1,0:T(8,128)(2,1)S(1)}, bf16[128,2048]{1,0:T(8,128)(2,1)S(1)}, u32[]{:S(2)}, u32[]{:S(2)}) collective-permute-start(bf16[128,2048]{1,0:T(8,128)(2,1)S(1)} %get-tuple-element.37), channel_id=1, source_target_pairs={{0,16},{8,120},{16,32},{24,8},{32,48},{40,24},{48,64},{56,40},{64,... | collective-permute-start | bytes 1572872 | tf_op jit(solution)/shard_map/ppermute | solution.py:269
  86.6 16.3 %all-to-all-start.2 = ((bf16[8,32,1408]{2,1,0:T(8,128)(2,1)}), bf16[8,32,1408]{2,1,0:T(8,128)(2,1)S(1)}, u32[]{:S(2)}, u32[]{:S(2)}) async-start(bf16[8,32,1408]{2,1,0:T(8,128)(2,1)} %broadcast_in_dim.5), calls=%async_computation.2 | async-start | bytes 1441792 | tf_op jit(solution)/shard_map/all_to_all | solution.py:368
  91.8 12.0 %copy-start.2 = (bf16[256,1024]{1,0:T(8,128)(2,1)S(1)}, bf16[256,1024]{1,0:T(8,128)(2,1)}, u32[]{:S(2)}) copy-start(bf16[256,1024]{1,0:T(8,128)(2,1)} %dec_h.1) | copy-start | bytes 1572868
  98.5 9.3 %collective-permute-start.11 = (bf16[64,2048]{1,0:T(8,128)(2,1)S(1)}, bf16[64,2048]{1,0:T(8,128)(2,1)S(1)}, u32[]{:S(2)}, u32[]{:S(2)}) collective-permute-start(bf16[64,2048]{1,0:T(8,128)(2,1)S(1)} %dynamic-slice_bitcast_fusion.4), channel_id=1, source_target_pairs={{0,128},{128,0},{1,129},{129,1},{2,130},{130,2},{3,131},{131,3},{4... | collective-permute-start | bytes 786440 | tf_op jit(solution)/shard_map/ppermute | solution.py:383
  107.9 3.1 %collective-permute-start.12 = (bf16[32,2048]{1,0:T(8,128)(2,1)S(1)}, bf16[32,2048]{1,0:T(8,128)(2,1)S(1)}, u32[]{:S(2)}, u32[]{:S(2)}) collective-permute-start(bf16[32,2048]{1,0:T(8,128)(2,1)S(1)} %dynamic-slice_bitcast_fusion.5), channel_id=1, source_target_pairs={{0,8},{8,0},{1,9},{9,1},{2,10},{10,2},{3,11},{11,3},{4,12},{12,4},... | collective-permute-start | bytes 393224 | tf_op jit(solution)/shard_map/ppermute | solution.py:387

commit v4 on v3

--- a/solution.py
+++ b/solution.py
@@ -39,7 +39,8 @@
     buf_h,
     keep,
     send,
-    first,
+    first_up,
+    first_down,
     tok,
     cot,
     wq,
@@ -113,23 +114,24 @@
     scale = DK**-0.5
     row = lax.broadcasted_iota(jnp.int32, (SEQ, SEQ), 0)
     col = lax.broadcasted_iota(jnp.int32, (SEQ, SEQ), 1)
-    causal = row >= col
+    causal = row <= col
+    log2 = scale * 1.4426950408889634
     for s in range(2):
         for h in range(heads):
             at = (slice(s * SEQ, (s + 1) * SEQ), slice(h * DK, (h + 1) * DK))
             q, k, v, dctx = q_s[at], k_s[at], v_s[at], dctx_s[at]
-            scores = jnp.where(causal, dot(q, k, 1, 1) * scale, -1e30)
-            top = jnp.max(scores, axis=-1, keepdims=True)
-            expo = jnp.exp(scores - top)
-            probs = expo * (1.0 / jnp.sum(expo, axis=-1, keepdims=True))
+            scores = jnp.where(causal, dot(k, q, 1, 1), -1e30)
+            top = jnp.max(scores, axis=0, keepdims=True)
+            expo = jnp.exp2((scores - top) * log2)
+            probs = expo * (1.0 / jnp.sum(expo, axis=0, keepdims=True))
             low = probs.astype(BF16)
-            ctx_s[at] = dot(low, v).astype(BF16)
-            dprobs = dot(dctx, v, 1, 1)
-            dv_s[at] = dot(low, dctx, 0, 0).astype(BF16)
-            delta = jnp.sum(dprobs * probs, axis=-1, keepdims=True)
+            ctx_s[at] = dot(low, v, 0, 0).astype(BF16)
+            dprobs = dot(v, dctx, 1, 1)
+            dv_s[at] = dot(low, dctx).astype(BF16)
+            delta = jnp.sum(dprobs * probs, axis=0, keepdims=True)
             ds = (probs * (dprobs - delta) * scale).astype(BF16)
-            dq_s[at] = dot(ds, k).astype(BF16)
-            dk_s[at] = dot(ds, q, 0, 0).astype(BF16)
+            dq_s[at] = dot(ds, k, 0, 0).astype(BF16)
+            dk_s[at] = dot(ds, q).astype(BF16)
 
     def put(i, g):
         lanes = slice(i * own, (i + 1) * own)
@@ -149,7 +151,7 @@
     out.append(put(1, dot(norm_t[...], dk_s[...])))
     for i in range(2):
         half = YH * part // 2
-        first[i] = stage[far, i * half : (i + 1) * half, :]
+        (first_up, first_down)[i][...] = stage[far, i * half : (i + 1) * half, :]
     piece = SEQ // NT
     code_s[...] = dot(ctx_s[...], w2).astype(BF16)
     gain_p = jnp.zeros((1, width), F32)
@@ -218,7 +220,8 @@
         sds((Z, YH * part, 4 * own), BF16),
         sds((NT, piece, lanes), BF16),
         sds((NT, piece, lanes), BF16),
-        sds((2, YH * part // 2, 4 * own), BF16),
+        sds((YH * part // 2, 4 * own), BF16),
+        sds((YH * part // 2, 4 * own), BF16),
     )
     vmem = pl.BlockSpec(memory_space=pltpu.VMEM)
     hbm = pl.BlockSpec(memory_space=pl.ANY)
@@ -242,7 +245,7 @@
     return pl.pallas_call(
         block_kernel,
         in_specs=[pl.BlockSpec(memory_space=pltpu.SMEM), vmem, *([hbm] * len(args))],
-        out_specs=[hbm, vmem, vmem, vmem],
+        out_specs=[hbm, vmem, vmem, vmem, vmem],
         out_shape=outs,
         scratch_shapes=[
             *(pltpu.VMEM(shape, BF16) for shape in shapes),
@@ -264,34 +267,48 @@
     return lax.dynamic_index_in_dim(buf, lax.rem(z + turn + Z, Z), 0, keepdims=False)
 
 
-def ring_send(held):
-    return [
-        lax.ppermute(
-            a,
-            ("z", "c"),
-            [
-                (at * CORES + core, (at + sign * (1 - 2 * core)) % Z * CORES + core)
-                for at in range(Z)
-                for core in range(CORES)
-            ],
-        )
-        for a, sign in zip(held, (1, -1), strict=True)
+def ring_send(a, sign):
+    pairs = [
+        (at * CORES + core, (at + sign * (1 - 2 * core)) % Z * CORES + core)
+        for at in range(Z)
+        for core in range(CORES)
     ]
-
-
-def ring_add(chunk, k, got):
-    out = []
-    for a, sign in zip(got, (1, -1), strict=True):
-        local = chunk(k, sign)
-        half = local.shape[0] // 2
-        if k < Z // 2 - 1:
-            out.append((local.astype(F32) + a.astype(F32)).astype(BF16))
-            continue
-        rows = slice(0, half) if sign == 1 else slice(half, 2 * half)
-        added = (local[rows].astype(F32) + a.astype(F32)).astype(BF16)
-        parts = [added, local[half:]] if sign == 1 else [local[:half], added]
-        out.append(jnp.concatenate(parts, axis=0))
-    return out
+    return lax.ppermute(a, ("z", "c"), pairs)
+
+
+def ring_add(local, a, sign):
+    half = local.shape[0] // 2
+    if a.shape[0] == local.shape[0]:
+        return (local.astype(F32) + a.astype(F32)).astype(BF16)
+    rows = slice(0, half) if sign == 1 else slice(half, 2 * half)
+    added = (local[rows].astype(F32) + a.astype(F32)).astype(BF16)
+    parts = [added, local[half:]] if sign == 1 else [local[:half], added]
+    return jnp.concatenate(parts, axis=0)
+
+
+def tie(*arrays):
+    return lax.optimization_barrier(arrays)
+
+
+def spread_kernel(core_ref, here, away, *outs):
+    own = outs[0].shape[1] // CORES
+    core = core_ref[0]
+    for ref, at in ((here, core), (away, 1 - core)):
+        lanes = pl.ds(pl.multiple_of(at * own, own), own)
+        for i, out in enumerate(outs):
+            out[:, lanes] = ref[:, i * own : (i + 1) * own].astype(F32)
+
+
+def spread(core, here, away):
+    rows, own = here.shape[0], here.shape[1] // 4
+    vmem = pl.BlockSpec(memory_space=pltpu.VMEM)
+    return pl.pallas_call(
+        spread_kernel,
+        in_specs=[pl.BlockSpec(memory_space=pltpu.SMEM), vmem, vmem],
+        out_specs=[vmem] * 4,
+        out_shape=[jax.ShapeDtypeStruct((rows, CORES * own), F32)] * 4,
+        compiler_params=pltpu.CompilerParams(vmem_limit_bytes=16 * 1024 * 1024),
+    )(core, here, away)
 
 
 def on_device(tokens, gain, w_query, w_key, w_value, w_output, encoder, decoder, cotangent):
@@ -307,7 +324,7 @@
 
     tok_oth = lax.ppermute(tokens, "c", SWAP)
     cot_oth = lax.ppermute(cotangent, "c", SWAP)
-    buf, keep, send, first = run_block(
+    buf, keep, send, first_up, first_down = run_block(
         core,
         gain.reshape(1, width),
         tokens,
@@ -322,14 +339,18 @@
         w_value,
     )
     chunk = functools.partial(ring_chunk, buf, z, c)
-    got = ring_send([first[0], first[1]])
+    up = ring_send(first_up, 1)
+    down = ring_send(first_down, -1)
     both = (keep.astype(F32) + lax.ppermute(send, "c", SWAP).astype(F32)).astype(BF16)
-    *got, both = lax.optimization_barrier((*got, both))
-
+    up, both = tie(up, both)
+    up = ring_add(chunk(3, 1), up, 1)
+    up, down, both = tie(up, down, both)
     over_t = lax.all_to_all(both, TP, 0, 0, tiled=True)
-    got = ring_send(ring_add(chunk, 3, got))
-    *got, over_t = lax.optimization_barrier((*got, over_t))
-
+    up = ring_send(up, 1)
+    down = ring_send(ring_add(chunk(3, -1), down, -1), -1)
+    up = ring_add(chunk(2, 1), up, 1)
+    up, down = tie(up, down)
+    up = ring_send(up, 1)
     total = jnp.sum(over_t.astype(F32), axis=0)
     piece = rows // NT
     out_w = width + code_w
@@ -343,8 +364,12 @@
     small = jnp.concatenate(
         [small, jnp.broadcast_to(gain_v[None], (YH * Z, *gain_v.shape))], axis=2
     ).astype(BF16)
+    small, down = tie(small, down)
     small = lax.all_to_all(small, ("yh", "z"), 0, 0, tiled=True)
-    got = ring_send(ring_add(chunk, 2, got))
+    down = ring_send(ring_add(chunk(2, -1), down, -1), -1)
+    up = ring_add(chunk(1, 1), up, 1)
+    up, down = tie(up, down)
+    up = ring_send(up, 1)
 
     dnormed = total[:, :width]
     x = lax.dynamic_slice_in_dim(tokens, t * piece, piece, 0).astype(F32)
@@ -355,7 +380,6 @@
     inner = jnp.sum(dunit * unit, axis=-1, keepdims=True) / width
     grad_rows = cot + rms * (dunit - unit * inner)
     mine = jnp.concatenate([grad_rows, total[:, width:out_w]], axis=1).astype(BF16)
-    *got, small, mine = lax.optimization_barrier((*got, small, mine))
 
     small = jnp.sum(small.astype(F32), axis=0)
     enc_v = small[:, cols : 2 * cols]
@@ -365,12 +389,12 @@
 
     dec_b = jnp.pad(small[:, :cols].astype(BF16), ((0, piece - dec_rows), (0, 0)))
     mine = jnp.concatenate([mine, dec_b], axis=1)
+    mine, down = tie(mine, down)
     over_t = lax.all_to_all(
         jnp.broadcast_to(mine[None], (NT, *mine.shape)), TP, 0, 0, tiled=True
     )
-    got = ring_send(ring_add(chunk, 1, got))
-    red = chunk(0, 1).astype(F32) + got[0].astype(F32) + got[1].astype(F32)
-    red = red.astype(BF16)
+    down = ring_send(ring_add(chunk(1, -1), down, -1), -1)
+    red = (chunk(0, 1).astype(F32) + up.astype(F32) + down.astype(F32)).astype(BF16)
     whole_rows = over_t[:, :, :out_w].reshape(rows, out_w)
     grad_input = whole_rows[:, :width]
     output = (tokens.astype(F32) + dot(whole_rows[:, width:], decoder)).astype(BF16)
@@ -385,14 +409,8 @@
     here = lax.dynamic_index_in_dim(both, c, 0, keepdims=False)
     away = lax.dynamic_index_in_dim(both, 1 - c, 0, keepdims=False)
     away = lax.ppermute(away, "c", SWAP)
-    low = jnp.where(c == 0, here, away).astype(F32)
-    high = jnp.where(c == 0, away, here).astype(F32)
-    grads = [
-        jnp.concatenate(
-            [low[:, i * own : (i + 1) * own], high[:, i * own : (i + 1) * own]], axis=1
-        )
-        for i in range(4)
-    ]
+    grads = spread(core, here, away)
+
     return (
         output,
         grad_input,

time: 114 us -> 111 us (0.974)
  waiting for transfers between devices: 41.1 us -> 36.3 us
    all_to_all x1, waiting for transfers between devices: 9.12 us -> 3.93 us  [on_device(): small = lax.all_to_all(small, ('yh', 'z'), 0, 0, tiled=True)]
    ppermute x8, waiting for transfers between devices: 21.7 us -> 18.4 us  [ring_send(): return lax.ppermute(a, ('z', 'c'), pairs)]
    all_to_all x1, waiting for transfers between devices: 1.23 us -> 3.98 us  [on_device(): over_t = lax.all_to_all(both, TP, 0, 0, tiled=True)]
    ppermute x1, starting transfers between devices: 0.43 us -> 2.78 us  [on_device(): both = here.astype(F32) + lax.ppermute(away, 'yh', SWAP).astype(F32)]
    concatenate x6 -> x2, other arithmetic: 2.87 us -> 0.88 us  [ring_add(): return jnp.concatenate(parts, axis=0)]
    ppermute x1, waiting for transfers between devices: 2.89 us -> 4.78 us  [on_device(): both = here.astype(F32) + lax.ppermute(away, 'yh', SWAP).astype(F32)]
    convert_element_type x4, other arithmetic: 5.46 us -> 6.97 us  [the longest x3 5.69 us: ring_add(): return (local.astype(F32) + a.astype(F32)).astype(BF16)]
    pallas_call x0 -> x1, Pallas kernels: none -> 1.35 us  [spread(): pl.pallas_call(spread_kernel, in_specs=[pl.BlockSpec(memory_space=pltpu.S...]
  transfers between devices with their start and end apart: 16 -> 16, of which waited for: 13 -> 13; matrix products, arithmetic and copies ran while one was open for 12% -> 18% of each run, Pallas kernels for 0% -> 0%
where the time goes in v4:
time: 111 us; the launch traced here: 110 us
  waiting for transfers between devices  36.3 us (33%)
  starting transfers between devices  34.5 us (31%)
  Pallas kernels  16.7 us (15%)
  other arithmetic  16.5 us (15%)
  local copies, waits for them, and re-layouts  4.37 us (4%)
    ppermute x8, waiting for transfers between devices, ring_send(): return lax.ppermute(a, ('z', 'c'), pairs)  18.4 us
    pallas_call x1, Pallas kernels, run_block(): pl.pallas_call(block_kernel, in_specs=[pl.BlockSpec(memory_space=pltpu.SM...  15.4 us
    ppermute x8, starting transfers between devices, ring_send(): return lax.ppermute(a, ('z', 'c'), pairs)  11.3 us
    all_to_all x1, starting transfers between devices, on_device(): small = lax.all_to_all(small, ('yh', 'z'), 0, 0, tiled=True)  6.98 us
    convert_element_type x3, other arithmetic, ring_add(): return (local.astype(F32) + a.astype(F32)).astype(BF16)  5.69 us
    all_to_all x1, starting transfers between devices, on_device(): over_t = lax.all_to_all(both, TP, 0, 0, tiled=True)  5.05 us
    ppermute x1, waiting for transfers between devices, on_device(): both = here.astype(F32) + lax.ppermute(away, 'yh', SWAP).astype(F32)  4.78 us
    all_to_all x1, waiting for transfers between devices, on_device(): over_t = lax.all_to_all(both, TP, 0, 0, tiled=True)  3.98 us
  transfers between devices with their start and end apart: 16, of which 13 were waited for; matrix products, arithmetic and copies ran while one was open for 18% of the time, Pallas kernels for 0%

profile of v4, /device:TPU:1, one launch (start us, length us, event | category | flops | bytes accessed | tf_op | source)
XLA Modules:
  0.0 110.4 jit_solution(8931496497240391447)
XLA Ops:
  0.6 3.3 %collective-permute-start = (bf16[256,1024]{1,0:T(8,128)(2,1)}, bf16[256,1024]{1,0:T(8,128)(2,1)S(1)}, u32[]{:S(2)}, u32[]{:S(2)}) collective-permute-start(bf16[256,1024]{1,0:T(8,128)(2,1)} %tok_own_h.1), channel_id=1, source_target_pairs={{0,8},{8,0},{1,9},{9,1},{2,10},{10,2},{3,11},{11,3},{4,12},{12,4},... | collective-permute-start | bytes 1572872 | tf_op jit(solution)/shard_map/ppermute | solution.py:325
  4.1 0.6 pad_add_fusion.core_ref
  4.7 1.1 collective-permute-done.tok_oth_h
  5.7 0.7 collective-permute-done.1.cot_oth_h
  6.5 0.7 copy-done.5
  7.3 15.4 %shard_map.160 = (bf16[8,128,2048]{2,1,0:T(8,128)(2,1)}, bf16[8,32,2432]{2,1,0:T(8,128)(2,1)}, bf16[8,32,2432]{2,1,0:T(8,128)(2,1)}, bf16[64,2048]{1,0:T(8,128)(2,1)}, bf16[64,2048]{1,0:T(8,128)(2,1)}) custom-call(s32[2]{0:T(128)} %pad_add_fusion.core_ref, f32[1,1024]{1,0:T(1,128)} %bitcast.59, bf16[256,1024]{1,0:T(8,128)(2,1)} %tok_own_h.1, ...), custom_call_target="tpu_custom_call" | custom-call | flops 7500000256 | bytes 14000000 | tf_op jit(solution)/shard_map/pallas_call | solution.py:245
  22.6 0.4 collective-permute-start.3
  23.2 4.1 %collective-permute-start.2 = (bf16[64,2048]{1,0:T(8,128)(2,1)}, bf16[64,2048]{1,0:T(8,128)(2,1)S(1)}, u32[]{:S(2)}, u32[]{:S(2)}) collective-permute-start(bf16[64,2048]{1,0:T(8,128)(2,1)} %get-tuple-element.32), channel_id=1, source_target_pairs={{0,16},{8,120},{16,32},{24,8},{32,48},{40,24},{48,64},{56,40},{64,... | collective-permute-start | bytes 786440 | tf_op jit(solution)/shard_map/ppermute | solution.py:276
  27.3 1.1 dynamic-slice_bitcast_fusion.1
  28.4 2.6 %add_convert_fusion = bf16[8,32,2432]{2,1,0:T(8,128)(2,1)} fusion(bf16[8,32,2432]{2,1,0:T(8,128)(2,1)S(1)} %collective-permute-done.3, bf16[8,32,2432]{2,1,0:T(8,128)(2,1)} %get-tuple-element.33), kind=kLoop, calls=%fused_computation.1 | loop fusion | flops 2490368 | bytes 3735552 | tf_op jit(solution)/shard_map/convert_element_type | solution.py:344
  31.0 2.1 %collective-permute-done.2 = bf16[64,2048]{1,0:T(8,128)(2,1)S(1)} collective-permute-done((bf16[64,2048]{1,0:T(8,128)(2,1)}, bf16[64,2048]{1,0:T(8,128)(2,1)S(1)}, u32[]{:S(2)}, u32[]{:S(2)}) %collective-permute-start.2) | collective-permute-done | bytes 262176 | tf_op jit(solution)/shard_map/ppermute | solution.py:276
  33.1 1.0 fusion.9
  34.1 0.3 collective-permute-done.4
  34.4 3.1 %collective-permute-start.5 = (bf16[128,2048]{1,0:T(8,128)(2,1)S(1)}, bf16[128,2048]{1,0:T(8,128)(2,1)S(1)}, u32[]{:S(2)}, u32[]{:S(2)}) collective-permute-start(bf16[128,2048]{1,0:T(8,128)(2,1)S(1)} %pad_maximum_fusion), channel_id=1, source_target_pairs={{0,16},{8,120},{16,32},{24,8},{32,48},{40,24},{48,64},{56,40},{64,... | collective-permute-start | bytes 1572872 | tf_op jit(solution)/shard_map/ppermute | solution.py:276
  37.5 5.0 %all-to-all-start = ((bf16[8,32,2432]{2,1,0:T(8,128)(2,1)}), bf16[8,32,2432]{2,1,0:T(8,128)(2,1)S(1)}, u32[]{:S(2)}, u32[]{:S(2)}) async-start(bf16[8,32,2432]{2,1,0:T(8,128)(2,1)} %add_convert_fusion), calls=%async_computation | async-start | bytes 2490368 | tf_op jit(solution)/shard_map/all_to_all | solution.py:348
  42.6 1.0 fusion.8
  43.6 0.8 pad_maximum_fusion.1
  44.4 2.0 %fusion.6 = bf16[128,2048]{1,0:T(8,128)(2,1)} fusion(bf16[128,2048]{1,0:T(8,128)(2,1)S(1)} %collective-permute-done.5, bf16[8,128,2048]{2,1,0:T(8,128)(2,1)} %get-tuple-element.31, s32[]{:T(128)S(6)} %select_n.59), kind=kLoop, calls=%fused_computation.14 | loop fusion | flops 1048576 | bytes 1572868 | tf_op jit(solution)/shard_map/convert_element_type | solution.py:282
  46.4 7.6 %collective-permute-done.6 = bf16[128,2048]{1,0:T(8,128)(2,1)} collective-permute-done((bf16[128,2048]{1,0:T(8,128)(2,1)}, bf16[128,2048]{1,0:T(8,128)(2,1)}, u32[]{:S(2)}, u32[]{:S(2)}) %collective-permute-start.6) | collective-permute-done | bytes 524320 | tf_op jit(solution)/shard_map/ppermute | solution.py:276
  54.0 4.0 %all-to-all-done = bf16[8,32,2432]{2,1,0:T(8,128)(2,1)S(1)} async-done(((bf16[8,32,2432]{2,1,0:T(8,128)(2,1)}), bf16[8,32,2432]{2,1,0:T(8,128)(2,1)S(1)}, u32[]{:S(2)}, u32[]{:S(2)}) %all-to-all-start) | async-done | bytes 1245216 | tf_op jit(solution)/shard_map/all_to_all | solution.py:348
  58.0 0.2 convert_reduce_fusion
  58.2 0.7 pad_maximum_fusion.2
  58.9 7.0 %all-to-all-start.1 = ((bf16[16,8,384]{2,1,0:T(8,128)(2,1)}), bf16[16,8,384]{2,1,0:T(8,128)(2,1)S(1)}, u32[]{:S(2)}, u32[]{:S(2)}) async-start(bf16[16,8,384]{2,1,0:T(8,128)(2,1)} %pad_maximum_fusion.2), calls=%async_computation.1 | async-start | bytes 196608 | tf_op jit(solution)/shard_map/all_to_all | solution.py:368
  65.9 2.6 %fusion.4 = (bf16[128,2048]{1,0:T(8,128)(2,1)S(1)}, bf16[128,2048]{1,0:T(8,128)(2,1)}) fusion(bf16[128,2048]{1,0:T(8,128)(2,1)} %collective-permute-done.6, bf16[8,128,2048]{2,1,0:T(8,128)(2,1)} %get-tuple-element.31, s32[]{:T(128)S(6)} %select_n.62, bf16[128,2048]{1,0:T(8,128)(2,1)S(1)} %collective-permute-done.7, s32[]{:T(128)S(6)} %select_n.61), kind=kLoop, calls=%fused_computation.10 | loop fusion | flops 2097152 | bytes 3145736 | tf_op jit(solution)/shard_map/convert_element_type | solution.py:282
  68.4 1.4 %collective-permute-start.8 = (bf16[128,2048]{1,0:T(8,128)(2,1)S(1)}, bf16[128,2048]{1,0:T(8,128)(2,1)S(1)}, u32[]{:S(2)}, u32[]{:S(2)}) collective-permute-start(bf16[128,2048]{1,0:T(8,128)(2,1)S(1)} %get-tuple-element.53), channel_id=1, source_target_pairs={{0,112},{8,24},{16,0},{24,40},{32,16},{40,56},{48,32},{56,72},{64,... | collective-permute-start | bytes 1572872 | tf_op jit(solution)/shard_map/ppermute | solution.py:276
  69.8 0.2 fusion.13
  70.0 0.9 fusion.17
  71.0 3.9 %all-to-all-done.1 = bf16[16,8,384]{2,1,0:T(8,128)(2,1)S(1)} async-done(((bf16[16,8,384]{2,1,0:T(8,128)(2,1)}), bf16[16,8,384]{2,1,0:T(8,128)(2,1)S(1)}, u32[]{:S(2)}, u32[]{:S(2)}) %all-to-all-start.1) | async-done | bytes 98336 | tf_op jit(solution)/shard_map/all_to_all | solution.py:368
  74.9 3.5 %collective-permute-done.8 = bf16[128,2048]{1,0:T(8,128)(2,1)S(1)} collective-permute-done((bf16[128,2048]{1,0:T(8,128)(2,1)S(1)}, bf16[128,2048]{1,0:T(8,128)(2,1)S(1)}, u32[]{:S(2)}, u32[]{:S(2)}) %collective-permute-start.8) | collective-permute-done | bytes 524320 | tf_op jit(solution)/shard_map/ppermute | solution.py:276
  78.5 1.2 %fusion.1 = bf16[128,2048]{1,0:T(8,128)(2,1)S(1)} fusion(bf16[128,2048]{1,0:T(8,128)(2,1)S(1)} %collective-permute-done.8, bf16[8,128,2048]{2,1,0:T(8,128)(2,1)} %get-tuple-element.31, s32[]{:T(128)S(6)} %select_n.68), kind=kLoop, calls=%fused_computation.5 | loop fusion | flops 1048576 | bytes 1572868 | tf_op jit(solution)/shard_map/convert_element_type | solution.py:282
  79.6 0.3 collective-permute-start.10
  79.9 2.5 %collective-permute-start.9 = (bf16[128,2048]{1,0:T(8,128)(2,1)}, bf16[128,2048]{1,0:T(8,128)(2,1)S(1)}, u32[]{:S(2)}, u32[]{:S(2)}) collective-permute-start(bf16[128,2048]{1,0:T(8,128)(2,1)} %get-tuple-element.47), channel_id=1, source_target_pairs={{0,16},{8,120},{16,32},{24,8},{32,48},{40,24},{48,64},{56,40},{64,... | collective-permute-start | bytes 1572872 | tf_op jit(solution)/shard_map/ppermute | solution.py:276
  82.4 0.6 dynamic-slice_bitcast_fusion.7
  83.0 0.6 pad_maximum_fusion.3
  83.6 0.9 broadcast_in_dim.5
  84.5 3.5 %all-to-all-start.2 = ((bf16[8,32,1408]{2,1,0:T(8,128)(2,1)}), bf16[8,32,1408]{2,1,0:T(8,128)(2,1)S(1)}, u32[]{:S(2)}, u32[]{:S(2)}) async-start(bf16[8,32,1408]{2,1,0:T(8,128)(2,1)} %broadcast_in_dim.5), calls=%async_computation.2 | async-start | bytes 1441792 | tf_op jit(solution)/shard_map/all_to_all | solution.py:393
  88.1 1.4 %collective-permute-done.10 = bf16[128,2048]{1,0:T(8,128)(2,1)S(1)} collective-permute-done((bf16[128,2048]{1,0:T(8,128)(2,1)S(1)}, bf16[128,2048]{1,0:T(8,128)(2,1)S(1)}, u32[]{:S(2)}, u32[]{:S(2)}) %collective-permute-start.10) | collective-permute-done | bytes 524320 | tf_op jit(solution)/shard_map/ppermute | solution.py:276
  89.5 3.5 %collective-permute-done.9 = bf16[128,2048]{1,0:T(8,128)(2,1)S(1)} collective-permute-done((bf16[128,2048]{1,0:T(8,128)(2,1)}, bf16[128,2048]{1,0:T(8,128)(2,1)S(1)}, u32[]{:S(2)}, u32[]{:S(2)}) %collective-permute-start.9) | collective-permute-done | bytes 524320 | tf_op jit(solution)/shard_map/ppermute | solution.py:276
  93.1 1.3 %fusion.3 = bf16[128,2048]{1,0:T(8,128)(2,1)S(1)} fusion(bf16[128,2048]{1,0:T(8,128)(2,1)S(1)} %collective-permute-done.10, bf16[128,2048]{1,0:T(8,128)(2,1)S(1)} %collective-permute-done.9, bf16[8,128,2048]{2,1,0:T(8,128)(2,1)} %get-tuple-element.31, s32[]{:T(128)S(6)} %select_n.67), kind=kLoop, calls=%fused_computation.8 | loop fusion | flops 1572864 | bytes 2097156 | tf_op jit(solution)/shard_map/convert_element_type | solution.py:397
  94.4 2.8 %collective-permute-start.11 = (bf16[64,2048]{1,0:T(8,128)(2,1)S(1)}, bf16[64,2048]{1,0:T(8,128)(2,1)S(1)}, u32[]{:S(2)}, u32[]{:S(2)}) collective-permute-start(bf16[64,2048]{1,0:T(8,128)(2,1)S(1)} %dynamic-slice_bitcast_fusion.4), channel_id=1, source_target_pairs={{0,128},{128,0},{1,129},{129,1},{2,130},{130,2},{3,131},{131,3},{4... | collective-permute-start | bytes 786440 | tf_op jit(solution)/shard_map/ppermute | solution.py:407
  97.2 3.0 %all-to-all-done.2 = bf16[8,32,1408]{2,1,0:T(8,128)(2,1)S(1)} async-done(((bf16[8,32,1408]{2,1,0:T(8,128)(2,1)}), bf16[8,32,1408]{2,1,0:T(8,128)(2,1)S(1)}, u32[]{:S(2)}, u32[]{:S(2)}) %all-to-all-start.2) | async-done | bytes 720928 | tf_op jit(solution)/shard_map/all_to_all | solution.py:393
  100.3 0.9 slice.106
  101.1 1.1 fusion
  102.2 4.8 %collective-permute-done.11 = bf16[64,2048]{1,0:T(8,128)(2,1)S(1)} collective-permute-done((bf16[64,2048]{1,0:T(8,128)(2,1)S(1)}, bf16[64,2048]{1,0:T(8,128)(2,1)S(1)}, u32[]{:S(2)}, u32[]{:S(2)}) %collective-permute-start.11) | collective-permute-done | bytes 262176 | tf_op jit(solution)/shard_map/ppermute | solution.py:407
  107.1 1.0 collective-permute-start.12
  108.1 0.6 convert_bitcast_fusion
  108.7 0.4 collective-permute-done.12.away
  109.0 1.4 %shard_map.161 = (f32[32,1024]{1,0:T(8,128)}, f32[32,1024]{1,0:T(8,128)}, f32[32,1024]{1,0:T(8,128)}, f32[32,1024]{1,0:T(8,128)}) custom-call(s32[2]{0:T(128)S(1)} %copy-done, bf16[32,2048]{1,0:T(8,128)(2,1)S(1)} %get-tuple-element.58.here, bf16[32,2048]{1,0:T(8,128)(2,1)S(1)} %collective-permute-done.12.away), custom_call_target="tpu_custom_call" | custom-call | tf_op jit(solution)/shard_map/pallas_call | solution.py:305
  (35 shorter events, 0.6 us)
Async XLA Ops:
  0.6 5.1 %collective-permute-start = (bf16[256,1024]{1,0:T(8,128)(2,1)}, bf16[256,1024]{1,0:T(8,128)(2,1)S(1)}, u32[]{:S(2)}, u32[]{:S(2)}) collective-permute-start(bf16[256,1024]{1,0:T(8,128)(2,1)} %tok_own_h.1), channel_id=1, source_target_pairs={{0,8},{8,0},{1,9},{9,1},{2,10},{10,2},{3,11},{11,3},{4,12},{12,4},... | collective-permute-start | bytes 1572872 | tf_op jit(solution)/shard_map/ppermute | solution.py:325
  4.0 2.5 %collective-permute-start.1 = (bf16[256,1024]{1,0:T(8,128)(2,1)}, bf16[256,1024]{1,0:T(8,128)(2,1)S(1)}, u32[]{:S(2)}, u32[]{:S(2)}) collective-permute-start(bf16[256,1024]{1,0:T(8,128)(2,1)} %cot_own_h.1), channel_id=1, source_target_pairs={{0,8},{8,0},{1,9},{9,1},{2,10},{10,2},{3,11},{11,3},{4,12},{12,4},... | collective-permute-start | bytes 1572872 | tf_op jit(solution)/shard_map/ppermute | solution.py:326
  5.7 0.8 copy-start.4
  6.5 0.8 copy-start.5
  7.3 15.8 %copy-start.1 = (bf16[256,1024]{1,0:T(8,128)(2,1)S(1)}, bf16[256,1024]{1,0:T(8,128)(2,1)}, u32[]{:S(2)}) copy-start(bf16[256,1024]{1,0:T(8,128)(2,1)} %tok_own_h.1) | copy-start | bytes 1572868
  22.6 5.7 %collective-permute-start.3 = (bf16[8,32,2432]{2,1,0:T(8,128)(2,1)}, bf16[8,32,2432]{2,1,0:T(8,128)(2,1)S(1)}, u32[]{:S(2)}, u32[]{:S(2)}) collective-permute-start(bf16[8,32,2432]{2,1,0:T(8,128)(2,1)} %get-tuple-element.34), channel_id=1, source_target_pairs={{0,8},{8,0},{1,9},{9,1},{2,10},{10,2},{3,11},{11,3},{4,12},{12,4},... | collective-permute-start | bytes 3735560 | tf_op jit(solution)/shard_map/ppermute | solution.py:344
  23.2 9.9 %collective-permute-start.2 = (bf16[64,2048]{1,0:T(8,128)(2,1)}, bf16[64,2048]{1,0:T(8,128)(2,1)S(1)}, u32[]{:S(2)}, u32[]{:S(2)}) collective-permute-start(bf16[64,2048]{1,0:T(8,128)(2,1)} %get-tuple-element.32), channel_id=1, source_target_pairs={{0,16},{8,120},{16,32},{24,8},{32,48},{40,24},{48,64},{56,40},{64,... | collective-permute-start | bytes 786440 | tf_op jit(solution)/shard_map/ppermute | solution.py:276
  27.3 7.1 %collective-permute-start.4 = (bf16[64,2048]{1,0:T(8,128)(2,1)}, bf16[64,2048]{1,0:T(8,128)(2,1)S(1)}, u32[]{:S(2)}, u32[]{:S(2)}) collective-permute-start(bf16[64,2048]{1,0:T(8,128)(2,1)} %get-tuple-element.36), channel_id=1, source_target_pairs={{0,112},{8,24},{16,0},{24,40},{32,16},{40,56},{48,32},{56,72},{64,... | collective-permute-start | bytes 786440 | tf_op jit(solution)/shard_map/ppermute | solution.py:276
  34.4 10.0 %collective-permute-start.5 = (bf16[128,2048]{1,0:T(8,128)(2,1)S(1)}, bf16[128,2048]{1,0:T(8,128)(2,1)S(1)}, u32[]{:S(2)}, u32[]{:S(2)}) collective-permute-start(bf16[128,2048]{1,0:T(8,128)(2,1)S(1)} %pad_maximum_fusion), channel_id=1, source_target_pairs={{0,16},{8,120},{16,32},{24,8},{32,48},{40,24},{48,64},{56,40},{64,... | collective-permute-start | bytes 1572872 | tf_op jit(solution)/shard_map/ppermute | solution.py:276
  37.5 20.5 %all-to-all-start = ((bf16[8,32,2432]{2,1,0:T(8,128)(2,1)}), bf16[8,32,2432]{2,1,0:T(8,128)(2,1)S(1)}, u32[]{:S(2)}, u32[]{:S(2)}) async-start(bf16[8,32,2432]{2,1,0:T(8,128)(2,1)} %add_convert_fusion), calls=%async_computation | async-start | bytes 2490368 | tf_op jit(solution)/shard_map/all_to_all | solution.py:348
  44.4 9.6 %collective-permute-start.6 = (bf16[128,2048]{1,0:T(8,128)(2,1)}, bf16[128,2048]{1,0:T(8,128)(2,1)}, u32[]{:S(2)}, u32[]{:S(2)}) collective-permute-start(bf16[128,2048]{1,0:T(8,128)(2,1)} %pad_maximum_fusion.1), channel_id=1, source_target_pairs={{0,112},{8,24},{16,0},{24,40},{32,16},{40,56},{48,32},{56,72},{64,... | collective-permute-start | bytes 1572872 | tf_op jit(solution)/shard_map/ppermute | solution.py:276
  54.0 11.9 %collective-permute-start.7 = (bf16[128,2048]{1,0:T(8,128)(2,1)}, bf16[128,2048]{1,0:T(8,128)(2,1)S(1)}, u32[]{:S(2)}, u32[]{:S(2)}) collective-permute-start(bf16[128,2048]{1,0:T(8,128)(2,1)} %fusion.6), channel_id=1, source_target_pairs={{0,16},{8,120},{16,32},{24,8},{32,48},{40,24},{48,64},{56,40},{64,... | collective-permute-start | bytes 1572872 | tf_op jit(solution)/shard_map/ppermute | solution.py:276
  58.1 11.7 %copy-start.3 = (f32[1024]{0:T(1024)S(1)}, f32[1024]{0:T(1024)}, u32[]{:S(2)}) copy-start(f32[1024]{0:T(1024)} %param.10) | copy-start | bytes 12292
  58.9 16.0 %all-to-all-start.1 = ((bf16[16,8,384]{2,1,0:T(8,128)(2,1)}), bf16[16,8,384]{2,1,0:T(8,128)(2,1)S(1)}, u32[]{:S(2)}, u32[]{:S(2)}) async-start(bf16[16,8,384]{2,1,0:T(8,128)(2,1)} %pad_maximum_fusion.2), calls=%async_computation.1 | async-start | bytes 196608 | tf_op jit(solution)/shard_map/all_to_all | solution.py:368
  68.4 10.0 %collective-permute-start.8 = (bf16[128,2048]{1,0:T(8,128)(2,1)S(1)}, bf16[128,2048]{1,0:T(8,128)(2,1)S(1)}, u32[]{:S(2)}, u32[]{:S(2)}) collective-permute-start(bf16[128,2048]{1,0:T(8,128)(2,1)S(1)} %get-tuple-element.53), channel_id=1, source_target_pairs={{0,112},{8,24},{16,0},{24,40},{32,16},{40,56},{48,32},{56,72},{64,... | collective-permute-start | bytes 1572872 | tf_op jit(solution)/shard_map/ppermute | solution.py:276
  79.6 9.9 %collective-permute-start.10 = (bf16[128,2048]{1,0:T(8,128)(2,1)S(1)}, bf16[128,2048]{1,0:T(8,128)(2,1)S(1)}, u32[]{:S(2)}, u32[]{:S(2)}) collective-permute-start(bf16[128,2048]{1,0:T(8,128)(2,1)S(1)} %fusion.1), channel_id=1, source_target_pairs={{0,112},{8,24},{16,0},{24,40},{32,16},{40,56},{48,32},{56,72},{64,... | collective-permute-start | bytes 1572872 | tf_op jit(solution)/shard_map/ppermute | solution.py:276
  79.9 13.1 %collective-permute-start.9 = (bf16[128,2048]{1,0:T(8,128)(2,1)}, bf16[128,2048]{1,0:T(8,128)(2,1)S(1)}, u32[]{:S(2)}, u32[]{:S(2)}) collective-permute-start(bf16[128,2048]{1,0:T(8,128)(2,1)} %get-tuple-element.47), channel_id=1, source_target_pairs={{0,16},{8,120},{16,32},{24,8},{32,48},{40,24},{48,64},{56,40},{64,... | collective-permute-start | bytes 1572872 | tf_op jit(solution)/shard_map/ppermute | solution.py:276
  84.5 15.7 %all-to-all-start.2 = ((bf16[8,32,1408]{2,1,0:T(8,128)(2,1)}), bf16[8,32,1408]{2,1,0:T(8,128)(2,1)S(1)}, u32[]{:S(2)}, u32[]{:S(2)}) async-start(bf16[8,32,1408]{2,1,0:T(8,128)(2,1)} %broadcast_in_dim.5), calls=%async_computation.2 | async-start | bytes 1441792 | tf_op jit(solution)/shard_map/all_to_all | solution.py:393
  88.1 13.1 %copy-start.2 = (bf16[256,1024]{1,0:T(8,128)(2,1)S(1)}, bf16[256,1024]{1,0:T(8,128)(2,1)}, u32[]{:S(2)}) copy-start(bf16[256,1024]{1,0:T(8,128)(2,1)} %dec_h.1) | copy-start | bytes 1572868
  94.4 12.6 %collective-permute-start.11 = (bf16[64,2048]{1,0:T(8,128)(2,1)S(1)}, bf16[64,2048]{1,0:T(8,128)(2,1)S(1)}, u32[]{:S(2)}, u32[]{:S(2)}) collective-permute-start(bf16[64,2048]{1,0:T(8,128)(2,1)S(1)} %dynamic-slice_bitcast_fusion.4), channel_id=1, source_target_pairs={{0,128},{128,0},{1,129},{129,1},{2,130},{130,2},{3,131},{131,3},{4... | collective-permute-start | bytes 786440 | tf_op jit(solution)/shard_map/ppermute | solution.py:407
  100.2 8.8 %copy-start = (s32[2]{0:T(128)S(1)}, s32[2]{0:T(128)}, u32[]{:S(2)}) copy-start(s32[2]{0:T(128)} %pad_add_fusion.core_ref) | copy-start | bytes 28
  107.1 1.9 %collective-permute-start.12 = (bf16[32,2048]{1,0:T(8,128)(2,1)S(1)}, bf16[32,2048]{1,0:T(8,128)(2,1)S(1)}, u32[]{:S(2)}, u32[]{:S(2)}) collective-permute-start(bf16[32,2048]{1,0:T(8,128)(2,1)S(1)} %get-tuple-element.57), channel_id=1, source_target_pairs={{0,8},{8,0},{1,9},{9,1},{2,10},{10,2},{3,11},{11,3},{4,12},{12,4},... | collective-permute-start | bytes 393224 | tf_op jit(solution)/shard_map/ppermute | solution.py:411

commit v5 on v4

--- a/solution.py
+++ b/solution.py
@@ -342,15 +342,12 @@
     up = ring_send(first_up, 1)
     down = ring_send(first_down, -1)
     both = (keep.astype(F32) + lax.ppermute(send, "c", SWAP).astype(F32)).astype(BF16)
-    up, both = tie(up, both)
+    up, _ = tie(up, both)
     up = ring_add(chunk(3, 1), up, 1)
-    up, down, both = tie(up, down, both)
+    up, down = tie(up, down)
     over_t = lax.all_to_all(both, TP, 0, 0, tiled=True)
     up = ring_send(up, 1)
     down = ring_send(ring_add(chunk(3, -1), down, -1), -1)
-    up = ring_add(chunk(2, 1), up, 1)
-    up, down = tie(up, down)
-    up = ring_send(up, 1)
     total = jnp.sum(over_t.astype(F32), axis=0)
     piece = rows // NT
     out_w = width + code_w
@@ -364,8 +361,11 @@
     small = jnp.concatenate(
         [small, jnp.broadcast_to(gain_v[None], (YH * Z, *gain_v.shape))], axis=2
     ).astype(BF16)
-    small, down = tie(small, down)
+    small, up = tie(small, up)
     small = lax.all_to_all(small, ("yh", "z"), 0, 0, tiled=True)
+    up = ring_add(chunk(2, 1), up, 1)
+    up, down = tie(up, down)
+    up = ring_send(up, 1)
     down = ring_send(ring_add(chunk(2, -1), down, -1), -1)
     up = ring_add(chunk(1, 1), up, 1)
     up, down = tie(up, down)

time: 111 us -> 109 us (0.982)
  other arithmetic: 16.5 us -> 14.6 us
    ppermute x8, waiting for transfers between devices: 18.4 us -> 8.95 us  [ring_send(): return lax.ppermute(a, ('z', 'c'), pairs)]
    all_to_all x1, waiting for transfers between devices: 3.98 us -> 12.1 us  [on_device(): over_t = lax.all_to_all(both, TP, 0, 0, tiled=True)]
    all_to_all x1, starting transfers between devices: 6.98 us -> 4.97 us  [on_device(): small = lax.all_to_all(small, ('yh', 'z'), 0, 0, tiled=True)]
    ppermute x8, starting transfers between devices: 11.3 us -> 13 us  [ring_send(): return lax.ppermute(a, ('z', 'c'), pairs)]
    convert_element_type x1, other arithmetic: 2.65 us -> 1.38 us  [on_device(): (keep.astype(F32) + lax.ppermute(send, 'c', SWAP).astype(F32)).astype(BF16)]
  transfers between devices with their start and end apart: 16 -> 16, of which waited for: 13 -> 11; matrix products, arithmetic and copies ran while one was open for 18% -> 17% of each run, Pallas kernels for 0% -> 0%
where the time goes in v5:
time: 109 us; the launch traced here: 108 us
  starting transfers between devices  35.4 us (32%)
  waiting for transfers between devices  35.4 us (32%)
  Pallas kernels  16.7 us (15%)
  other arithmetic  14.6 us (13%)
  local copies, waits for them, and re-layouts  4.36 us (4%)
  matrix products  1.1 us (1%)
    pallas_call x1, Pallas kernels, run_block(): pl.pallas_call(block_kernel, in_specs=[pl.BlockSpec(memory_space=pltpu.SM...  15.4 us
    ppermute x8, starting transfers between devices, ring_send(): return lax.ppermute(a, ('z', 'c'), pairs)  13 us
    all_to_all x1, waiting for transfers between devices, on_device(): over_t = lax.all_to_all(both, TP, 0, 0, tiled=True)  12.1 us
    ppermute x8, waiting for transfers between devices, ring_send(): return lax.ppermute(a, ('z', 'c'), pairs)  8.95 us
    all_to_all x1, starting transfers between devices, on_device(): over_t = lax.all_to_all(both, TP, 0, 0, tiled=True)  5.04 us
    all_to_all x1, starting transfers between devices, on_device(): small = lax.all_to_all(small, ('yh', 'z'), 0, 0, tiled=True)  4.97 us
    convert_element_type x3, other arithmetic, ring_add(): return (local.astype(F32) + a.astype(F32)).astype(BF16)  4.87 us
    ppermute x1, waiting for transfers between devices, on_device(): both = here.astype(F32) + lax.ppermute(away, 'yh', SWAP).astype(F32)  4.52 us
  transfers between devices with their start and end apart: 16, of which 11 were waited for; matrix products, arithmetic and copies ran while one was open for 17% of the time, Pallas kernels for 0%

profile of v5, /device:TPU:1, one launch (start us, length us, event | category | flops | bytes accessed | tf_op | source)
XLA Modules:
  0.0 108.4 jit_solution(7394516412380993757)
XLA Ops:
  0.6 3.3 %collective-permute-start = (bf16[256,1024]{1,0:T(8,128)(2,1)}, bf16[256,1024]{1,0:T(8,128)(2,1)S(1)}, u32[]{:S(2)}, u32[]{:S(2)}) collective-permute-start(bf16[256,1024]{1,0:T(8,128)(2,1)} %tok_own_h.1), channel_id=1, source_target_pairs={{0,8},{8,0},{1,9},{9,1},{2,10},{10,2},{3,11},{11,3},{4,12},{12,4},... | collective-permute-start | bytes 1572872 | tf_op jit(solution)/shard_map/ppermute | solution.py:325
  4.0 0.1 collective-permute-start.1
  4.1 0.6 pad_add_fusion.core_ref
  4.7 1.1 collective-permute-done.tok_oth_h
  5.7 0.7 collective-permute-done.1.cot_oth_h
  6.5 0.7 copy-done.6
  7.3 15.4 %shard_map.160 = (bf16[8,128,2048]{2,1,0:T(8,128)(2,1)}, bf16[8,32,2432]{2,1,0:T(8,128)(2,1)}, bf16[8,32,2432]{2,1,0:T(8,128)(2,1)}, bf16[64,2048]{1,0:T(8,128)(2,1)}, bf16[64,2048]{1,0:T(8,128)(2,1)}) custom-call(s32[2]{0:T(128)} %pad_add_fusion.core_ref, f32[1,1024]{1,0:T(1,128)} %bitcast.59, bf16[256,1024]{1,0:T(8,128)(2,1)} %tok_own_h.1, ...), custom_call_target="tpu_custom_call" | custom-call | flops 7500000256 | bytes 14000000 | tf_op jit(solution)/shard_map/pallas_call | solution.py:245
  22.6 0.4 collective-permute-start.2
  23.1 0.1 fusion.18
  23.2 4.1 %collective-permute-start.3 = (bf16[64,2048]{1,0:T(8,128)(2,1)}, bf16[64,2048]{1,0:T(8,128)(2,1)}, u32[]{:S(2)}, u32[]{:S(2)}) collective-permute-start(bf16[64,2048]{1,0:T(8,128)(2,1)} %get-tuple-element.32), channel_id=1, source_target_pairs={{0,16},{8,120},{16,32},{24,8},{32,48},{40,24},{48,64},{56,40},{64,... | collective-permute-start | bytes 786440 | tf_op jit(solution)/shard_map/ppermute | solution.py:276
  27.3 1.1 dynamic-slice_bitcast_fusion.1
  28.4 1.4 %add_convert_fusion = bf16[8,32,2432]{2,1,0:T(8,128)(2,1)} fusion(bf16[8,32,2432]{2,1,0:T(8,128)(2,1)S(1)} %collective-permute-done.2, bf16[8,32,2432]{2,1,0:T(8,128)(2,1)S(1)} %copy-done.1), kind=kLoop, calls=%fused_computation.1 | loop fusion | flops 2490368 | bytes 3735552 | tf_op jit(solution)/shard_map/convert_element_type | solution.py:344
  29.8 5.0 %all-to-all-start = ((bf16[8,32,2432]{2,1,0:T(8,128)(2,1)}), bf16[8,32,2432]{2,1,0:T(8,128)(2,1)S(1)}, u32[]{:S(2)}, u32[]{:S(2)}) async-start(bf16[8,32,2432]{2,1,0:T(8,128)(2,1)} %add_convert_fusion), calls=%async_computation | async-start | bytes 2490368 | tf_op jit(solution)/shard_map/all_to_all | solution.py:348
  34.8 1.1 %fusion.9 = bf16[64,2048]{1,0:T(8,128)(2,1)S(1)} fusion(bf16[64,2048]{1,0:T(8,128)(2,1)} %collective-permute-done.3, bf16[8,128,2048]{2,1,0:T(8,128)(2,1)} %get-tuple-element.31, s32[]{:T(128)S(6)} %select_n.58), kind=kLoop, calls=%fused_computation.22 | loop fusion | flops 524288 | bytes 786436 | tf_op jit(solution)/shard_map/convert_element_type | solution.py:284
  36.0 2.7 %collective-permute-start.5 = (bf16[128,2048]{1,0:T(8,128)(2,1)S(1)}, bf16[128,2048]{1,0:T(8,128)(2,1)}, u32[]{:S(2)}, u32[]{:S(2)}) collective-permute-start(bf16[128,2048]{1,0:T(8,128)(2,1)S(1)} %pad_maximum_fusion), channel_id=1, source_target_pairs={{0,16},{8,120},{16,32},{24,8},{32,48},{40,24},{48,64},{56,40},{64,... | collective-permute-start | bytes 1572872 | tf_op jit(solution)/shard_map/ppermute | solution.py:276
  38.7 1.1 %fusion.8 = bf16[64,2048]{1,0:T(8,128)(2,1)S(1)} fusion(bf16[64,2048]{1,0:T(8,128)(2,1)} %collective-permute-done.4, bf16[8,128,2048]{2,1,0:T(8,128)(2,1)} %get-tuple-element.31, s32[]{:T(128)S(6)} %select_n.61, s32[]{:T(128)S(6)} %add.206), kind=kLoop, calls=%fused_computation.20 | loop fusion | flops 524288 | bytes 786440 | tf_op jit(solution)/shard_map/convert_element_type | solution.py:284
  39.8 0.8 pad_maximum_fusion.1
  40.6 12.1 %all-to-all-done = bf16[8,32,2432]{2,1,0:T(8,128)(2,1)S(1)} async-done(((bf16[8,32,2432]{2,1,0:T(8,128)(2,1)}), bf16[8,32,2432]{2,1,0:T(8,128)(2,1)S(1)}, u32[]{:S(2)}, u32[]{:S(2)}) %all-to-all-start) | async-done | bytes 1245216 | tf_op jit(solution)/shard_map/all_to_all | solution.py:348
  52.7 0.2 convert_reduce_fusion
  53.0 0.7 pad_maximum_fusion.2
  53.6 1.3 %fusion.5 = bf16[128,2048]{1,0:T(8,128)(2,1)S(1)} fusion(bf16[128,2048]{1,0:T(8,128)(2,1)} %collective-permute-done.5, bf16[8,128,2048]{2,1,0:T(8,128)(2,1)} %get-tuple-element.31, s32[]{:T(128)S(6)} %select_n.60), kind=kLoop, calls=%fused_computation.12 | loop fusion | flops 1048576 | bytes 1572868 | tf_op jit(solution)/shard_map/convert_element_type | solution.py:282
  55.0 2.9 %collective-permute-start.7 = (bf16[128,2048]{1,0:T(8,128)(2,1)S(1)}, bf16[128,2048]{1,0:T(8,128)(2,1)S(1)}, u32[]{:S(2)}, u32[]{:S(2)}) collective-permute-start(bf16[128,2048]{1,0:T(8,128)(2,1)S(1)} %fusion.5), channel_id=1, source_target_pairs={{0,16},{8,120},{16,32},{24,8},{32,48},{40,24},{48,64},{56,40},{64,... | collective-permute-start | bytes 1572872 | tf_op jit(solution)/shard_map/ppermute | solution.py:276
  57.9 5.0 %all-to-all-start.1 = ((bf16[16,8,384]{2,1,0:T(8,128)(2,1)}), bf16[16,8,384]{2,1,0:T(8,128)(2,1)S(1)}, u32[]{:S(2)}, u32[]{:S(2)}) async-start(bf16[16,8,384]{2,1,0:T(8,128)(2,1)} %pad_maximum_fusion.2), calls=%async_computation.1 | async-start | bytes 196608 | tf_op jit(solution)/shard_map/all_to_all | solution.py:365
  62.9 0.2 fusion.13
  63.1 0.9 collective-permute-done.7
  64.1 2.4 %fusion.4 = (bf16[128,2048]{1,0:T(8,128)(2,1)S(1)}, bf16[128,2048]{1,0:T(8,128)(2,1)}) fusion(bf16[128,2048]{1,0:T(8,128)(2,1)S(1)} %collective-permute-done.6, bf16[8,128,2048]{2,1,0:T(8,128)(2,1)} %get-tuple-element.31, s32[]{:T(128)S(6)} %select_n.62, bf16[128,2048]{1,0:T(8,128)(2,1)S(1)} %collective-permute-done.7, s32[]{:T(128)S(6)} %select_n.59), kind=kLoop, calls=%fused_computation.10 | loop fusion | flops 2097152 | bytes 3145736 | tf_op jit(solution)/shard_map/convert_element_type | solution.py:282
  66.4 0.5 collective-permute-start.8
  66.9 0.9 fusion.17
  67.8 4.1 %all-to-all-done.1 = bf16[16,8,384]{2,1,0:T(8,128)(2,1)S(1)} async-done(((bf16[16,8,384]{2,1,0:T(8,128)(2,1)}), bf16[16,8,384]{2,1,0:T(8,128)(2,1)S(1)}, u32[]{:S(2)}, u32[]{:S(2)}) %all-to-all-start.1) | async-done | bytes 98336 | tf_op jit(solution)/shard_map/all_to_all | solution.py:365
  72.0 4.3 %collective-permute-done.8 = bf16[128,2048]{1,0:T(8,128)(2,1)S(1)} collective-permute-done((bf16[128,2048]{1,0:T(8,128)(2,1)S(1)}, bf16[128,2048]{1,0:T(8,128)(2,1)S(1)}, u32[]{:S(2)}, u32[]{:S(2)}) %collective-permute-start.8) | collective-permute-done | bytes 524320 | tf_op jit(solution)/shard_map/ppermute | solution.py:276
  76.3 1.2 %fusion.1 = bf16[128,2048]{1,0:T(8,128)(2,1)S(1)} fusion(bf16[128,2048]{1,0:T(8,128)(2,1)S(1)} %collective-permute-done.8, bf16[8,128,2048]{2,1,0:T(8,128)(2,1)} %get-tuple-element.31, s32[]{:T(128)S(6)} %select_n.68), kind=kLoop, calls=%fused_computation.5 | loop fusion | flops 1048576 | bytes 1572868 | tf_op jit(solution)/shard_map/convert_element_type | solution.py:282
  77.5 2.7 %collective-permute-start.9 = (bf16[128,2048]{1,0:T(8,128)(2,1)}, bf16[128,2048]{1,0:T(8,128)(2,1)S(1)}, u32[]{:S(2)}, u32[]{:S(2)}) collective-permute-start(bf16[128,2048]{1,0:T(8,128)(2,1)} %get-tuple-element.43), channel_id=1, source_target_pairs={{0,16},{8,120},{16,32},{24,8},{32,48},{40,24},{48,64},{56,40},{64,... | collective-permute-start | bytes 1572872 | tf_op jit(solution)/shard_map/ppermute | solution.py:276
  80.2 0.6 dynamic-slice_bitcast_fusion.7
  80.8 0.6 pad_maximum_fusion.3
  81.4 0.9 broadcast_in_dim.5
  82.3 4.3 %all-to-all-start.2 = ((bf16[8,32,1408]{2,1,0:T(8,128)(2,1)}), bf16[8,32,1408]{2,1,0:T(8,128)(2,1)S(1)}, u32[]{:S(2)}, u32[]{:S(2)}) async-start(bf16[8,32,1408]{2,1,0:T(8,128)(2,1)} %broadcast_in_dim.5), calls=%async_computation.2 | async-start | bytes 1441792 | tf_op jit(solution)/shard_map/all_to_all | solution.py:393
  86.6 0.8 collective-permute-done.10
  87.4 3.0 %collective-permute-done.9 = bf16[128,2048]{1,0:T(8,128)(2,1)S(1)} collective-permute-done((bf16[128,2048]{1,0:T(8,128)(2,1)}, bf16[128,2048]{1,0:T(8,128)(2,1)S(1)}, u32[]{:S(2)}, u32[]{:S(2)}) %collective-permute-start.9) | collective-permute-done | bytes 524320 | tf_op jit(solution)/shard_map/ppermute | solution.py:276
  90.4 1.3 %fusion.3 = bf16[128,2048]{1,0:T(8,128)(2,1)S(1)} fusion(bf16[128,2048]{1,0:T(8,128)(2,1)S(1)} %collective-permute-done.10, bf16[128,2048]{1,0:T(8,128)(2,1)S(1)} %collective-permute-done.9, bf16[8,128,2048]{2,1,0:T(8,128)(2,1)} %get-tuple-element.31, s32[]{:T(128)S(6)} %select_n.67), kind=kLoop, calls=%fused_computation.8 | loop fusion | flops 1572864 | bytes 2097156 | tf_op jit(solution)/shard_map/convert_element_type | solution.py:397
  91.7 2.8 %collective-permute-start.11 = (bf16[64,2048]{1,0:T(8,128)(2,1)S(1)}, bf16[64,2048]{1,0:T(8,128)(2,1)S(1)}, u32[]{:S(2)}, u32[]{:S(2)}) collective-permute-start(bf16[64,2048]{1,0:T(8,128)(2,1)S(1)} %dynamic-slice_bitcast_fusion.4), channel_id=1, source_target_pairs={{0,128},{128,0},{1,129},{129,1},{2,130},{130,2},{3,131},{131,3},{4... | collective-permute-start | bytes 786440 | tf_op jit(solution)/shard_map/ppermute | solution.py:407
  94.5 3.5 %all-to-all-done.2 = bf16[8,32,1408]{2,1,0:T(8,128)(2,1)S(1)} async-done(((bf16[8,32,1408]{2,1,0:T(8,128)(2,1)}), bf16[8,32,1408]{2,1,0:T(8,128)(2,1)S(1)}, u32[]{:S(2)}, u32[]{:S(2)}) %all-to-all-start.2) | async-done | bytes 720928 | tf_op jit(solution)/shard_map/all_to_all | solution.py:393
  98.1 0.9 slice.106
  99.0 1.1 %fusion = bf16[256,1024]{1,0:T(8,128)(2,1)} fusion(bf16[256,1024]{1,0:T(8,128)(2,1)S(1)} %copy-done.3, bf16[256,1024]{1,0:T(8,128)(2,1)S(1)} %copy-done.2, bf16[256,1280]{1,0:T(8,128)(2,1)S(1)} %bitcast.55), kind=kOutput, calls=%fused_computation.3 | convolution fusion | flops 135004160 | bytes 1703936 | tf_op jit(solution)/shard_map/dot_general | solution.py:23
  100.1 4.5 %collective-permute-done.11 = bf16[64,2048]{1,0:T(8,128)(2,1)S(1)} collective-permute-done((bf16[64,2048]{1,0:T(8,128)(2,1)S(1)}, bf16[64,2048]{1,0:T(8,128)(2,1)S(1)}, u32[]{:S(2)}, u32[]{:S(2)}) %collective-permute-start.11) | collective-permute-done | bytes 262176 | tf_op jit(solution)/shard_map/ppermute | solution.py:407
  104.7 1.3 %collective-permute-start.12 = (bf16[32,2048]{1,0:T(8,128)(2,1)S(1)}, bf16[32,2048]{1,0:T(8,128)(2,1)S(1)}, u32[]{:S(2)}, u32[]{:S(2)}) collective-permute-start(bf16[32,2048]{1,0:T(8,128)(2,1)S(1)} %get-tuple-element.53), channel_id=1, source_target_pairs={{0,8},{8,0},{1,9},{9,1},{2,10},{10,2},{3,11},{11,3},{4,12},{12,4},... | collective-permute-start | bytes 393224 | tf_op jit(solution)/shard_map/ppermute | solution.py:411
  106.0 0.6 convert_bitcast_fusion
  106.7 0.4 collective-permute-done.12.away
  107.0 1.4 %shard_map.161 = (f32[32,1024]{1,0:T(8,128)}, f32[32,1024]{1,0:T(8,128)}, f32[32,1024]{1,0:T(8,128)}, f32[32,1024]{1,0:T(8,128)}) custom-call(s32[2]{0:T(128)S(1)} %copy-done, bf16[32,2048]{1,0:T(8,128)(2,1)S(1)} %get-tuple-element.54.here, bf16[32,2048]{1,0:T(8,128)(2,1)S(1)} %collective-permute-done.12.away), custom_call_target="tpu_custom_call" | custom-call | tf_op jit(solution)/shard_map/pallas_call | solution.py:305
  (37 shorter events, 0.5 us)
Async XLA Ops:
  0.6 5.1 %collective-permute-start = (bf16[256,1024]{1,0:T(8,128)(2,1)}, bf16[256,1024]{1,0:T(8,128)(2,1)S(1)}, u32[]{:S(2)}, u32[]{:S(2)}) collective-permute-start(bf16[256,1024]{1,0:T(8,128)(2,1)} %tok_own_h.1), channel_id=1, source_target_pairs={{0,8},{8,0},{1,9},{9,1},{2,10},{10,2},{3,11},{11,3},{4,12},{12,4},... | collective-permute-start | bytes 1572872 | tf_op jit(solution)/shard_map/ppermute | solution.py:325
  4.0 2.5 %collective-permute-start.1 = (bf16[256,1024]{1,0:T(8,128)(2,1)}, bf16[256,1024]{1,0:T(8,128)(2,1)S(1)}, u32[]{:S(2)}, u32[]{:S(2)}) collective-permute-start(bf16[256,1024]{1,0:T(8,128)(2,1)} %cot_own_h.1), channel_id=1, source_target_pairs={{0,8},{8,0},{1,9},{9,1},{2,10},{10,2},{3,11},{11,3},{4,12},{12,4},... | collective-permute-start | bytes 1572872 | tf_op jit(solution)/shard_map/ppermute | solution.py:326
  5.7 0.8 copy-start.5
  6.5 0.8 copy-start.6
  7.3 15.8 %copy-start.2 = (bf16[256,1024]{1,0:T(8,128)(2,1)S(1)}, bf16[256,1024]{1,0:T(8,128)(2,1)}, u32[]{:S(2)}) copy-start(bf16[256,1024]{1,0:T(8,128)(2,1)} %tok_own_h.1) | copy-start | bytes 1572868
  22.6 5.8 %copy-start.1 = (bf16[8,32,2432]{2,1,0:T(8,128)(2,1)S(1)}, bf16[8,32,2432]{2,1,0:T(8,128)(2,1)}, u32[]{:S(2)}) copy-start(bf16[8,32,2432]{2,1,0:T(8,128)(2,1)} %get-tuple-element.29) | copy-start | bytes 3735556
  22.6 5.7 %collective-permute-start.2 = (bf16[8,32,2432]{2,1,0:T(8,128)(2,1)}, bf16[8,32,2432]{2,1,0:T(8,128)(2,1)S(1)}, u32[]{:S(2)}, u32[]{:S(2)}) collective-permute-start(bf16[8,32,2432]{2,1,0:T(8,128)(2,1)} %get-tuple-element.30), channel_id=1, source_target_pairs={{0,8},{8,0},{1,9},{9,1},{2,10},{10,2},{3,11},{11,3},{4,12},{12,4},... | collective-permute-start | bytes 3735560 | tf_op jit(solution)/shard_map/ppermute | solution.py:344
  23.2 11.6 %collective-permute-start.3 = (bf16[64,2048]{1,0:T(8,128)(2,1)}, bf16[64,2048]{1,0:T(8,128)(2,1)}, u32[]{:S(2)}, u32[]{:S(2)}) collective-permute-start(bf16[64,2048]{1,0:T(8,128)(2,1)} %get-tuple-element.32), channel_id=1, source_target_pairs={{0,16},{8,120},{16,32},{24,8},{32,48},{40,24},{48,64},{56,40},{64,... | collective-permute-start | bytes 786440 | tf_op jit(solution)/shard_map/ppermute | solution.py:276
  27.3 8.7 %collective-permute-start.4 = (bf16[64,2048]{1,0:T(8,128)(2,1)}, bf16[64,2048]{1,0:T(8,128)(2,1)}, u32[]{:S(2)}, u32[]{:S(2)}) collective-permute-start(bf16[64,2048]{1,0:T(8,128)(2,1)} %get-tuple-element.34), channel_id=1, source_target_pairs={{0,112},{8,24},{16,0},{24,40},{32,16},{40,56},{48,32},{56,72},{64,... | collective-permute-start | bytes 786440 | tf_op jit(solution)/shard_map/ppermute | solution.py:276
  29.8 23.0 %all-to-all-start = ((bf16[8,32,2432]{2,1,0:T(8,128)(2,1)}), bf16[8,32,2432]{2,1,0:T(8,128)(2,1)S(1)}, u32[]{:S(2)}, u32[]{:S(2)}) async-start(bf16[8,32,2432]{2,1,0:T(8,128)(2,1)} %add_convert_fusion), calls=%async_computation | async-start | bytes 2490368 | tf_op jit(solution)/shard_map/all_to_all | solution.py:348
  36.0 17.7 %collective-permute-start.5 = (bf16[128,2048]{1,0:T(8,128)(2,1)S(1)}, bf16[128,2048]{1,0:T(8,128)(2,1)}, u32[]{:S(2)}, u32[]{:S(2)}) collective-permute-start(bf16[128,2048]{1,0:T(8,128)(2,1)S(1)} %pad_maximum_fusion), channel_id=1, source_target_pairs={{0,16},{8,120},{16,32},{24,8},{32,48},{40,24},{48,64},{56,40},{64,... | collective-permute-start | bytes 1572872 | tf_op jit(solution)/shard_map/ppermute | solution.py:276
  40.6 22.3 %copy-start.4 = (f32[1024]{0:T(1024)S(1)}, f32[1024]{0:T(1024)}, u32[]{:S(2)}) copy-start(f32[1024]{0:T(1024)} %param.10) | copy-start | bytes 12292
  40.6 14.3 %collective-permute-start.6 = (bf16[128,2048]{1,0:T(8,128)(2,1)}, bf16[128,2048]{1,0:T(8,128)(2,1)S(1)}, u32[]{:S(2)}, u32[]{:S(2)}) collective-permute-start(bf16[128,2048]{1,0:T(8,128)(2,1)} %pad_maximum_fusion.1), channel_id=1, source_target_pairs={{0,112},{8,24},{16,0},{24,40},{32,16},{40,56},{48,32},{56,72},{64,... | collective-permute-start | bytes 1572872 | tf_op jit(solution)/shard_map/ppermute | solution.py:276
  55.0 9.1 %collective-permute-start.7 = (bf16[128,2048]{1,0:T(8,128)(2,1)S(1)}, bf16[128,2048]{1,0:T(8,128)(2,1)S(1)}, u32[]{:S(2)}, u32[]{:S(2)}) collective-permute-start(bf16[128,2048]{1,0:T(8,128)(2,1)S(1)} %fusion.5), channel_id=1, source_target_pairs={{0,16},{8,120},{16,32},{24,8},{32,48},{40,24},{48,64},{56,40},{64,... | collective-permute-start | bytes 1572872 | tf_op jit(solution)/shard_map/ppermute | solution.py:276
  57.9 14.0 %all-to-all-start.1 = ((bf16[16,8,384]{2,1,0:T(8,128)(2,1)}), bf16[16,8,384]{2,1,0:T(8,128)(2,1)S(1)}, u32[]{:S(2)}, u32[]{:S(2)}) async-start(bf16[16,8,384]{2,1,0:T(8,128)(2,1)} %pad_maximum_fusion.2), calls=%async_computation.1 | async-start | bytes 196608 | tf_op jit(solution)/shard_map/all_to_all | solution.py:365
  66.4 9.8 %collective-permute-start.8 = (bf16[128,2048]{1,0:T(8,128)(2,1)S(1)}, bf16[128,2048]{1,0:T(8,128)(2,1)S(1)}, u32[]{:S(2)}, u32[]{:S(2)}) collective-permute-start(bf16[128,2048]{1,0:T(8,128)(2,1)S(1)} %get-tuple-element.49), channel_id=1, source_target_pairs={{0,112},{8,24},{16,0},{24,40},{32,16},{40,56},{48,32},{56,72},{64,... | collective-permute-start | bytes 1572872 | tf_op jit(solution)/shard_map/ppermute | solution.py:276
  77.4 10.0 %collective-permute-start.10 = (bf16[128,2048]{1,0:T(8,128)(2,1)S(1)}, bf16[128,2048]{1,0:T(8,128)(2,1)S(1)}, u32[]{:S(2)}, u32[]{:S(2)}) collective-permute-start(bf16[128,2048]{1,0:T(8,128)(2,1)S(1)} %fusion.1), channel_id=1, source_target_pairs={{0,112},{8,24},{16,0},{24,40},{32,16},{40,56},{48,32},{56,72},{64,... | collective-permute-start | bytes 1572872 | tf_op jit(solution)/shard_map/ppermute | solution.py:276
  77.5 12.8 %collective-permute-start.9 = (bf16[128,2048]{1,0:T(8,128)(2,1)}, bf16[128,2048]{1,0:T(8,128)(2,1)S(1)}, u32[]{:S(2)}, u32[]{:S(2)}) collective-permute-start(bf16[128,2048]{1,0:T(8,128)(2,1)} %get-tuple-element.43), channel_id=1, source_target_pairs={{0,16},{8,120},{16,32},{24,8},{32,48},{40,24},{48,64},{56,40},{64,... | collective-permute-start | bytes 1572872 | tf_op jit(solution)/shard_map/ppermute | solution.py:276
  82.3 15.8 %all-to-all-start.2 = ((bf16[8,32,1408]{2,1,0:T(8,128)(2,1)}), bf16[8,32,1408]{2,1,0:T(8,128)(2,1)S(1)}, u32[]{:S(2)}, u32[]{:S(2)}) async-start(bf16[8,32,1408]{2,1,0:T(8,128)(2,1)} %broadcast_in_dim.5), calls=%async_computation.2 | async-start | bytes 1441792 | tf_op jit(solution)/shard_map/all_to_all | solution.py:393
  86.6 12.4 %copy-start.3 = (bf16[256,1024]{1,0:T(8,128)(2,1)S(1)}, bf16[256,1024]{1,0:T(8,128)(2,1)}, u32[]{:S(2)}) copy-start(bf16[256,1024]{1,0:T(8,128)(2,1)} %dec_h.1) | copy-start | bytes 1572868
  91.7 12.9 %collective-permute-start.11 = (bf16[64,2048]{1,0:T(8,128)(2,1)S(1)}, bf16[64,2048]{1,0:T(8,128)(2,1)S(1)}, u32[]{:S(2)}, u32[]{:S(2)}) collective-permute-start(bf16[64,2048]{1,0:T(8,128)(2,1)S(1)} %dynamic-slice_bitcast_fusion.4), channel_id=1, source_target_pairs={{0,128},{128,0},{1,129},{129,1},{2,130},{130,2},{3,131},{131,3},{4... | collective-permute-start | bytes 786440 | tf_op jit(solution)/shard_map/ppermute | solution.py:407
  98.1 8.9 %copy-start = (s32[2]{0:T(128)S(1)}, s32[2]{0:T(128)}, u32[]{:S(2)}) copy-start(s32[2]{0:T(128)} %pad_add_fusion.core_ref) | copy-start | bytes 28
  104.7 2.3 %collective-permute-start.12 = (bf16[32,2048]{1,0:T(8,128)(2,1)S(1)}, bf16[32,2048]{1,0:T(8,128)(2,1)S(1)}, u32[]{:S(2)}, u32[]{:S(2)}) collective-permute-start(bf16[32,2048]{1,0:T(8,128)(2,1)S(1)} %get-tuple-element.53), channel_id=1, source_target_pairs={{0,8},{8,0},{1,9},{9,1},{2,10},{10,2},{3,11},{11,3},{4,12},{12,4},... | collective-permute-start | bytes 393224 | tf_op jit(solution)/shard_map/ppermute | solution.py:411

commit v6 on v5

--- a/solution.py
+++ b/solution.py
@@ -389,7 +389,6 @@
 
     dec_b = jnp.pad(small[:, :cols].astype(BF16), ((0, piece - dec_rows), (0, 0)))
     mine = jnp.concatenate([mine, dec_b], axis=1)
-    mine, down = tie(mine, down)
     over_t = lax.all_to_all(
         jnp.broadcast_to(mine[None], (NT, *mine.shape)), TP, 0, 0, tiled=True
     )

time: 109 us -> 106 us (0.972)
  waiting for transfers between devices: 35.4 us -> 30.9 us
  starting transfers between devices: 35.4 us -> 36.6 us
    ppermute x8, waiting for transfers between devices: 8.95 us -> 3.08 us  [ring_send(): return lax.ppermute(a, ('z', 'c'), pairs)]
    all_to_all x1, waiting for transfers between devices: 3.54 us -> 6.13 us  [on_device(): lax.all_to_all(jnp.broadcast_to(mine[None], (NT, *mine.shape)), TP, 0, 0,...]
    ppermute x1, starting transfers between devices: 1.34 us -> 3.74 us  [on_device(): away = lax.ppermute(away, 'c', SWAP)]
    ppermute x1, waiting for transfers between devices: 4.52 us -> 3.28 us  [on_device(): both = here.astype(F32) + lax.ppermute(away, 'yh', SWAP).astype(F32)]
  transfers between devices with their start and end apart: 16 -> 16, of which waited for: 11 -> 9; matrix products, arithmetic and copies ran while one was open for 17% -> 17% of each run, Pallas kernels for 0% -> 0%
where the time goes in v6:
time: 106 us; the launch traced here: 105 us
  starting transfers between devices  36.6 us (35%)
  waiting for transfers between devices  30.9 us (29%)
  Pallas kernels  16.7 us (16%)
  other arithmetic  14.6 us (14%)
  local copies, waits for them, and re-layouts  4.36 us (4%)
  matrix products  1.1 us (1%)
    pallas_call x1, Pallas kernels, run_block(): pl.pallas_call(block_kernel, in_specs=[pl.BlockSpec(memory_space=pltpu.SM...  15.4 us
    ppermute x8, starting transfers between devices, ring_send(): return lax.ppermute(a, ('z', 'c'), pairs)  13 us
    all_to_all x1, waiting for transfers between devices, on_device(): over_t = lax.all_to_all(both, TP, 0, 0, tiled=True)  12.1 us
    all_to_all x1, waiting for transfers between devices, on_device(): lax.all_to_all(jnp.broadcast_to(mine[None], (NT, *mine.shape)), TP, 0, 0,...  6.13 us
    all_to_all x1, starting transfers between devices, on_device(): over_t = lax.all_to_all(both, TP, 0, 0, tiled=True)  5.04 us
    all_to_all x1, starting transfers between devices, on_device(): small = lax.all_to_all(small, ('yh', 'z'), 0, 0, tiled=True)  4.97 us
    convert_element_type x3, other arithmetic, ring_add(): return (local.astype(F32) + a.astype(F32)).astype(BF16)  4.88 us
    all_to_all x1, waiting for transfers between devices, on_device(): small = lax.all_to_all(small, ('yh', 'z'), 0, 0, tiled=True)  4.09 us
  transfers between devices with their start and end apart: 16, of which 9 were waited for; matrix products, arithmetic and copies ran while one was open for 17% of the time, Pallas kernels for 0%

profile of v6, /device:TPU:1, one launch (start us, length us, event | category | flops | bytes accessed | tf_op | source)
XLA Modules:
  0.0 105.1 jit_solution(6294532429202380636)
XLA Ops:
  0.6 3.3 %collective-permute-start = (bf16[256,1024]{1,0:T(8,128)(2,1)}, bf16[256,1024]{1,0:T(8,128)(2,1)S(1)}, u32[]{:S(2)}, u32[]{:S(2)}) collective-permute-start(bf16[256,1024]{1,0:T(8,128)(2,1)} %tok_own_h.1), channel_id=1, source_target_pairs={{0,8},{8,0},{1,9},{9,1},{2,10},{10,2},{3,11},{11,3},{4,12},{12,4},... | collective-permute-start | bytes 1572872 | tf_op jit(solution)/shard_map/ppermute | solution.py:325
  4.0 0.1 collective-permute-start.1
  4.1 0.6 pad_add_fusion.core_ref
  4.7 1.1 %collective-permute-done.tok_oth_h = bf16[256,1024]{1,0:T(8,128)(2,1)S(1)} collective-permute-done((bf16[256,1024]{1,0:T(8,128)(2,1)}, bf16[256,1024]{1,0:T(8,128)(2,1)S(1)}, u32[]{:S(2)}, u32[]{:S(2)}) %collective-permute-start) | collective-permute-done | bytes 524320 | tf_op jit(solution)/shard_map/ppermute | solution.py:325
  5.7 0.7 collective-permute-done.1.cot_oth_h
  6.5 0.7 copy-done.6
  7.3 15.4 %shard_map.160 = (bf16[8,128,2048]{2,1,0:T(8,128)(2,1)}, bf16[8,32,2432]{2,1,0:T(8,128)(2,1)}, bf16[8,32,2432]{2,1,0:T(8,128)(2,1)}, bf16[64,2048]{1,0:T(8,128)(2,1)}, bf16[64,2048]{1,0:T(8,128)(2,1)}) custom-call(s32[2]{0:T(128)} %pad_add_fusion.core_ref, f32[1,1024]{1,0:T(1,128)} %bitcast.59, bf16[256,1024]{1,0:T(8,128)(2,1)} %tok_own_h.1, ...), custom_call_target="tpu_custom_call" | custom-call | flops 7500000256 | bytes 14000000 | tf_op jit(solution)/shard_map/pallas_call | solution.py:245
  22.6 0.4 collective-permute-start.2
  23.1 0.1 fusion.18
  23.2 4.1 %collective-permute-start.3 = (bf16[64,2048]{1,0:T(8,128)(2,1)}, bf16[64,2048]{1,0:T(8,128)(2,1)}, u32[]{:S(2)}, u32[]{:S(2)}) collective-permute-start(bf16[64,2048]{1,0:T(8,128)(2,1)} %get-tuple-element.30), channel_id=1, source_target_pairs={{0,16},{8,120},{16,32},{24,8},{32,48},{40,24},{48,64},{56,40},{64,... | collective-permute-start | bytes 786440 | tf_op jit(solution)/shard_map/ppermute | solution.py:276
  27.3 1.1 %dynamic-slice_bitcast_fusion.1 = (bf16[64,2048]{1,0:T(8,128)(2,1)S(1)}, bf16[64,2048]{1,0:T(8,128)(2,1)S(1)}) fusion(bf16[8,128,2048]{2,1,0:T(8,128)(2,1)} %get-tuple-element.29, s32[]{:T(128)S(6)} %select_n.66, s32[]{:T(128)S(6)} %select_n.58, s32[]{:T(128)S(6)} %add.206), kind=kLoop, calls=%fused_computation.24 | loop fusion | bytes 1048588 | tf_op jit(solution)/shard_map/slice | solution.py:285
  28.4 1.4 %add_convert_fusion = bf16[8,32,2432]{2,1,0:T(8,128)(2,1)} fusion(bf16[8,32,2432]{2,1,0:T(8,128)(2,1)S(1)} %collective-permute-done.2, bf16[8,32,2432]{2,1,0:T(8,128)(2,1)S(1)} %copy-done.1), kind=kLoop, calls=%fused_computation.1 | loop fusion | flops 2490368 | bytes 3735552 | tf_op jit(solution)/shard_map/convert_element_type | solution.py:344
  29.8 5.0 %all-to-all-start = ((bf16[8,32,2432]{2,1,0:T(8,128)(2,1)}), bf16[8,32,2432]{2,1,0:T(8,128)(2,1)S(1)}, u32[]{:S(2)}, u32[]{:S(2)}) async-start(bf16[8,32,2432]{2,1,0:T(8,128)(2,1)} %add_convert_fusion), calls=%async_computation | async-start | bytes 2490368 | tf_op jit(solution)/shard_map/all_to_all | solution.py:348
  34.8 1.1 %fusion.9 = bf16[64,2048]{1,0:T(8,128)(2,1)S(1)} fusion(bf16[64,2048]{1,0:T(8,128)(2,1)} %collective-permute-done.3, bf16[8,128,2048]{2,1,0:T(8,128)(2,1)} %get-tuple-element.29, s32[]{:T(128)S(6)} %select_n.58), kind=kLoop, calls=%fused_computation.22 | loop fusion | flops 524288 | bytes 786436 | tf_op jit(solution)/shard_map/convert_element_type | solution.py:284
  36.0 2.7 %collective-permute-start.5 = (bf16[128,2048]{1,0:T(8,128)(2,1)S(1)}, bf16[128,2048]{1,0:T(8,128)(2,1)}, u32[]{:S(2)}, u32[]{:S(2)}) collective-permute-start(bf16[128,2048]{1,0:T(8,128)(2,1)S(1)} %pad_maximum_fusion), channel_id=1, source_target_pairs={{0,16},{8,120},{16,32},{24,8},{32,48},{40,24},{48,64},{56,40},{64,... | collective-permute-start | bytes 1572872 | tf_op jit(solution)/shard_map/ppermute | solution.py:276
  38.7 1.1 %fusion.8 = bf16[64,2048]{1,0:T(8,128)(2,1)S(1)} fusion(bf16[64,2048]{1,0:T(8,128)(2,1)} %collective-permute-done.4, bf16[8,128,2048]{2,1,0:T(8,128)(2,1)} %get-tuple-element.29, s32[]{:T(128)S(6)} %select_n.66, s32[]{:T(128)S(6)} %add.206), kind=kLoop, calls=%fused_computation.20 | loop fusion | flops 524288 | bytes 786440 | tf_op jit(solution)/shard_map/convert_element_type | solution.py:284
  39.8 0.8 pad_maximum_fusion.1
  40.6 12.1 %all-to-all-done = bf16[8,32,2432]{2,1,0:T(8,128)(2,1)S(1)} async-done(((bf16[8,32,2432]{2,1,0:T(8,128)(2,1)}), bf16[8,32,2432]{2,1,0:T(8,128)(2,1)S(1)}, u32[]{:S(2)}, u32[]{:S(2)}) %all-to-all-start) | async-done | bytes 1245216 | tf_op jit(solution)/shard_map/all_to_all | solution.py:348
  52.7 0.2 convert_reduce_fusion
  53.0 0.7 pad_maximum_fusion.2
  53.6 1.3 %fusion.3 = bf16[128,2048]{1,0:T(8,128)(2,1)S(1)} fusion(bf16[128,2048]{1,0:T(8,128)(2,1)} %collective-permute-done.5, bf16[8,128,2048]{2,1,0:T(8,128)(2,1)} %get-tuple-element.29, s32[]{:T(128)S(6)} %select_n.65), kind=kLoop, calls=%fused_computation.9 | loop fusion | flops 1048576 | bytes 1572868 | tf_op jit(solution)/shard_map/convert_element_type | solution.py:282
  55.0 2.9 %collective-permute-start.7 = (bf16[128,2048]{1,0:T(8,128)(2,1)S(1)}, bf16[128,2048]{1,0:T(8,128)(2,1)S(1)}, u32[]{:S(2)}, u32[]{:S(2)}) collective-permute-start(bf16[128,2048]{1,0:T(8,128)(2,1)S(1)} %fusion.3), channel_id=1, source_target_pairs={{0,16},{8,120},{16,32},{24,8},{32,48},{40,24},{48,64},{56,40},{64,... | collective-permute-start | bytes 1572872 | tf_op jit(solution)/shard_map/ppermute | solution.py:276
  57.9 5.0 %all-to-all-start.1 = ((bf16[16,8,384]{2,1,0:T(8,128)(2,1)}), bf16[16,8,384]{2,1,0:T(8,128)(2,1)S(1)}, u32[]{:S(2)}, u32[]{:S(2)}) async-start(bf16[16,8,384]{2,1,0:T(8,128)(2,1)} %pad_maximum_fusion.2), calls=%async_computation.1 | async-start | bytes 196608 | tf_op jit(solution)/shard_map/all_to_all | solution.py:365
  62.9 0.2 fusion.13
  63.1 0.9 collective-permute-done.7
  64.1 2.4 %fusion.2 = (bf16[128,2048]{1,0:T(8,128)(2,1)S(1)}, bf16[128,2048]{1,0:T(8,128)(2,1)}) fusion(bf16[128,2048]{1,0:T(8,128)(2,1)S(1)} %collective-permute-done.6, bf16[8,128,2048]{2,1,0:T(8,128)(2,1)} %get-tuple-element.29, s32[]{:T(128)S(6)} %select_n.67, bf16[128,2048]{1,0:T(8,128)(2,1)S(1)} %collective-permute-done.7, s32[]{:T(128)S(6)} %select_n.64), kind=kLoop, calls=%fused_computation.7 | loop fusion | flops 2097152 | bytes 3145736 | tf_op jit(solution)/shard_map/convert_element_type | solution.py:282
  66.4 0.5 collective-permute-start.8
  66.9 0.9 fusion.17
  67.8 4.1 %all-to-all-done.1 = bf16[16,8,384]{2,1,0:T(8,128)(2,1)S(1)} async-done(((bf16[16,8,384]{2,1,0:T(8,128)(2,1)}), bf16[16,8,384]{2,1,0:T(8,128)(2,1)S(1)}, u32[]{:S(2)}, u32[]{:S(2)}) %all-to-all-start.1) | async-done | bytes 98336 | tf_op jit(solution)/shard_map/all_to_all | solution.py:365
  72.0 0.9 broadcast_in_dim.5
  72.9 3.5 %all-to-all-start.2 = ((bf16[8,32,1408]{2,1,0:T(8,128)(2,1)}), bf16[8,32,1408]{2,1,0:T(8,128)(2,1)S(1)}, u32[]{:S(2)}, u32[]{:S(2)}) async-start(bf16[8,32,1408]{2,1,0:T(8,128)(2,1)} %broadcast_in_dim.5), calls=%async_computation.2 | async-start | bytes 1441792 | tf_op jit(solution)/shard_map/all_to_all | solution.py:392
  76.5 1.2 %fusion.1 = bf16[128,2048]{1,0:T(8,128)(2,1)S(1)} fusion(bf16[128,2048]{1,0:T(8,128)(2,1)S(1)} %collective-permute-done.8, bf16[8,128,2048]{2,1,0:T(8,128)(2,1)} %get-tuple-element.29, s32[]{:T(128)S(6)} %select_n.68), kind=kLoop, calls=%fused_computation.5 | loop fusion | flops 1048576 | bytes 1572868 | tf_op jit(solution)/shard_map/convert_element_type | solution.py:282
  77.6 0.8 collective-permute-start.10
  78.4 2.0 %collective-permute-start.9 = (bf16[128,2048]{1,0:T(8,128)(2,1)}, bf16[128,2048]{1,0:T(8,128)(2,1)S(1)}, u32[]{:S(2)}, u32[]{:S(2)}) collective-permute-start(bf16[128,2048]{1,0:T(8,128)(2,1)} %get-tuple-element.39), channel_id=1, source_target_pairs={{0,16},{8,120},{16,32},{24,8},{32,48},{40,24},{48,64},{56,40},{64,... | collective-permute-start | bytes 1572872 | tf_op jit(solution)/shard_map/ppermute | solution.py:276
  80.4 0.6 dynamic-slice_bitcast_fusion.7
  81.0 0.6 pad_maximum_fusion.3
  81.6 6.1 %all-to-all-done.2 = bf16[8,32,1408]{2,1,0:T(8,128)(2,1)S(1)} async-done(((bf16[8,32,1408]{2,1,0:T(8,128)(2,1)}), bf16[8,32,1408]{2,1,0:T(8,128)(2,1)S(1)}, u32[]{:S(2)}, u32[]{:S(2)}) %all-to-all-start.2) | async-done | bytes 720928 | tf_op jit(solution)/shard_map/all_to_all | solution.py:392
  87.8 0.9 slice.106
  88.6 2.1 %collective-permute-done.9 = bf16[128,2048]{1,0:T(8,128)(2,1)S(1)} collective-permute-done((bf16[128,2048]{1,0:T(8,128)(2,1)}, bf16[128,2048]{1,0:T(8,128)(2,1)S(1)}, u32[]{:S(2)}, u32[]{:S(2)}) %collective-permute-start.9) | collective-permute-done | bytes 524320 | tf_op jit(solution)/shard_map/ppermute | solution.py:276
  90.8 1.3 %fusion.6 = bf16[128,2048]{1,0:T(8,128)(2,1)S(1)} fusion(bf16[128,2048]{1,0:T(8,128)(2,1)S(1)} %collective-permute-done.10, bf16[128,2048]{1,0:T(8,128)(2,1)S(1)} %collective-permute-done.9, bf16[8,128,2048]{2,1,0:T(8,128)(2,1)} %get-tuple-element.29, s32[]{:T(128)S(6)} %select_n.63), kind=kLoop, calls=%fused_computation.14 | loop fusion | flops 1572864 | bytes 2097156 | tf_op jit(solution)/shard_map/convert_element_type | solution.py:396
  92.1 2.4 %collective-permute-start.11 = (bf16[64,2048]{1,0:T(8,128)(2,1)S(1)}, bf16[64,2048]{1,0:T(8,128)(2,1)S(1)}, u32[]{:S(2)}, u32[]{:S(2)}) collective-permute-start(bf16[64,2048]{1,0:T(8,128)(2,1)S(1)} %dynamic-slice_bitcast_fusion.4), channel_id=1, source_target_pairs={{0,128},{128,0},{1,129},{129,1},{2,130},{130,2},{3,131},{131,3},{4... | collective-permute-start | bytes 786440 | tf_op jit(solution)/shard_map/ppermute | solution.py:406
  94.5 1.1 %fusion = bf16[256,1024]{1,0:T(8,128)(2,1)} fusion(bf16[256,1024]{1,0:T(8,128)(2,1)S(1)} %copy-done.3, bf16[256,1024]{1,0:T(8,128)(2,1)S(1)} %copy-done.2, bf16[256,1280]{1,0:T(8,128)(2,1)S(1)} %bitcast.55), kind=kOutput, calls=%fused_computation.3 | convolution fusion | flops 135004160 | bytes 1703936 | tf_op jit(solution)/shard_map/dot_general | solution.py:23
  95.6 3.3 %collective-permute-done.11 = bf16[64,2048]{1,0:T(8,128)(2,1)S(1)} collective-permute-done((bf16[64,2048]{1,0:T(8,128)(2,1)S(1)}, bf16[64,2048]{1,0:T(8,128)(2,1)S(1)}, u32[]{:S(2)}, u32[]{:S(2)}) %collective-permute-start.11) | collective-permute-done | bytes 262176 | tf_op jit(solution)/shard_map/ppermute | solution.py:406
  98.9 0.1 fusion.7
  99.0 3.7 %collective-permute-start.12 = (bf16[32,2048]{1,0:T(8,128)(2,1)S(1)}, bf16[32,2048]{1,0:T(8,128)(2,1)S(1)}, u32[]{:S(2)}, u32[]{:S(2)}) collective-permute-start(bf16[32,2048]{1,0:T(8,128)(2,1)S(1)} %get-tuple-element.49), channel_id=1, source_target_pairs={{0,8},{8,0},{1,9},{9,1},{2,10},{10,2},{3,11},{11,3},{4,12},{12,4},... | collective-permute-start | bytes 393224 | tf_op jit(solution)/shard_map/ppermute | solution.py:410
  102.7 0.6 convert_bitcast_fusion
  103.4 0.4 collective-permute-done.12.away
  103.7 1.4 %shard_map.161 = (f32[32,1024]{1,0:T(8,128)}, f32[32,1024]{1,0:T(8,128)}, f32[32,1024]{1,0:T(8,128)}, f32[32,1024]{1,0:T(8,128)}) custom-call(s32[2]{0:T(128)S(1)} %copy-done, bf16[32,2048]{1,0:T(8,128)(2,1)S(1)} %get-tuple-element.50.here, bf16[32,2048]{1,0:T(8,128)(2,1)S(1)} %collective-permute-done.12.away), custom_call_target="tpu_custom_call" | custom-call | tf_op jit(solution)/shard_map/pallas_call | solution.py:305
  (37 shorter events, 0.3 us)
Async XLA Ops:
  0.6 5.1 %collective-permute-start = (bf16[256,1024]{1,0:T(8,128)(2,1)}, bf16[256,1024]{1,0:T(8,128)(2,1)S(1)}, u32[]{:S(2)}, u32[]{:S(2)}) collective-permute-start(bf16[256,1024]{1,0:T(8,128)(2,1)} %tok_own_h.1), channel_id=1, source_target_pairs={{0,8},{8,0},{1,9},{9,1},{2,10},{10,2},{3,11},{11,3},{4,12},{12,4},... | collective-permute-start | bytes 1572872 | tf_op jit(solution)/shard_map/ppermute | solution.py:325
  4.0 2.5 %collective-permute-start.1 = (bf16[256,1024]{1,0:T(8,128)(2,1)}, bf16[256,1024]{1,0:T(8,128)(2,1)S(1)}, u32[]{:S(2)}, u32[]{:S(2)}) collective-permute-start(bf16[256,1024]{1,0:T(8,128)(2,1)} %cot_own_h.1), channel_id=1, source_target_pairs={{0,8},{8,0},{1,9},{9,1},{2,10},{10,2},{3,11},{11,3},{4,12},{12,4},... | collective-permute-start | bytes 1572872 | tf_op jit(solution)/shard_map/ppermute | solution.py:326
  5.7 0.8 copy-start.5
  6.5 0.8 copy-start.6
  7.3 15.8 %copy-start.2 = (bf16[256,1024]{1,0:T(8,128)(2,1)S(1)}, bf16[256,1024]{1,0:T(8,128)(2,1)}, u32[]{:S(2)}) copy-start(bf16[256,1024]{1,0:T(8,128)(2,1)} %tok_own_h.1) | copy-start | bytes 1572868
  22.6 5.8 %copy-start.1 = (bf16[8,32,2432]{2,1,0:T(8,128)(2,1)S(1)}, bf16[8,32,2432]{2,1,0:T(8,128)(2,1)}, u32[]{:S(2)}) copy-start(bf16[8,32,2432]{2,1,0:T(8,128)(2,1)} %get-tuple-element.27) | copy-start | bytes 3735556
  22.6 5.7 %collective-permute-start.2 = (bf16[8,32,2432]{2,1,0:T(8,128)(2,1)}, bf16[8,32,2432]{2,1,0:T(8,128)(2,1)S(1)}, u32[]{:S(2)}, u32[]{:S(2)}) collective-permute-start(bf16[8,32,2432]{2,1,0:T(8,128)(2,1)} %get-tuple-element.28), channel_id=1, source_target_pairs={{0,8},{8,0},{1,9},{9,1},{2,10},{10,2},{3,11},{11,3},{4,12},{12,4},... | collective-permute-start | bytes 3735560 | tf_op jit(solution)/shard_map/ppermute | solution.py:344
  23.2 11.6 %collective-permute-start.3 = (bf16[64,2048]{1,0:T(8,128)(2,1)}, bf16[64,2048]{1,0:T(8,128)(2,1)}, u32[]{:S(2)}, u32[]{:S(2)}) collective-permute-start(bf16[64,2048]{1,0:T(8,128)(2,1)} %get-tuple-element.30), channel_id=1, source_target_pairs={{0,16},{8,120},{16,32},{24,8},{32,48},{40,24},{48,64},{56,40},{64,... | collective-permute-start | bytes 786440 | tf_op jit(solution)/shard_map/ppermute | solution.py:276
  27.3 8.7 %collective-permute-start.4 = (bf16[64,2048]{1,0:T(8,128)(2,1)}, bf16[64,2048]{1,0:T(8,128)(2,1)}, u32[]{:S(2)}, u32[]{:S(2)}) collective-permute-start(bf16[64,2048]{1,0:T(8,128)(2,1)} %get-tuple-element.32), channel_id=1, source_target_pairs={{0,112},{8,24},{16,0},{24,40},{32,16},{40,56},{48,32},{56,72},{64,... | collective-permute-start | bytes 786440 | tf_op jit(solution)/shard_map/ppermute | solution.py:276
  29.8 23.0 %all-to-all-start = ((bf16[8,32,2432]{2,1,0:T(8,128)(2,1)}), bf16[8,32,2432]{2,1,0:T(8,128)(2,1)S(1)}, u32[]{:S(2)}, u32[]{:S(2)}) async-start(bf16[8,32,2432]{2,1,0:T(8,128)(2,1)} %add_convert_fusion), calls=%async_computation | async-start | bytes 2490368 | tf_op jit(solution)/shard_map/all_to_all | solution.py:348
  36.0 17.7 %collective-permute-start.5 = (bf16[128,2048]{1,0:T(8,128)(2,1)S(1)}, bf16[128,2048]{1,0:T(8,128)(2,1)}, u32[]{:S(2)}, u32[]{:S(2)}) collective-permute-start(bf16[128,2048]{1,0:T(8,128)(2,1)S(1)} %pad_maximum_fusion), channel_id=1, source_target_pairs={{0,16},{8,120},{16,32},{24,8},{32,48},{40,24},{48,64},{56,40},{64,... | collective-permute-start | bytes 1572872 | tf_op jit(solution)/shard_map/ppermute | solution.py:276
  40.6 22.3 %copy-start.4 = (f32[1024]{0:T(1024)S(1)}, f32[1024]{0:T(1024)}, u32[]{:S(2)}) copy-start(f32[1024]{0:T(1024)} %param.10) | copy-start | bytes 12292
  40.6 14.3 %collective-permute-start.6 = (bf16[128,2048]{1,0:T(8,128)(2,1)}, bf16[128,2048]{1,0:T(8,128)(2,1)S(1)}, u32[]{:S(2)}, u32[]{:S(2)}) collective-permute-start(bf16[128,2048]{1,0:T(8,128)(2,1)} %pad_maximum_fusion.1), channel_id=1, source_target_pairs={{0,112},{8,24},{16,0},{24,40},{32,16},{40,56},{48,32},{56,72},{64,... | collective-permute-start | bytes 1572872 | tf_op jit(solution)/shard_map/ppermute | solution.py:276
  55.0 9.1 %collective-permute-start.7 = (bf16[128,2048]{1,0:T(8,128)(2,1)S(1)}, bf16[128,2048]{1,0:T(8,128)(2,1)S(1)}, u32[]{:S(2)}, u32[]{:S(2)}) collective-permute-start(bf16[128,2048]{1,0:T(8,128)(2,1)S(1)} %fusion.3), channel_id=1, source_target_pairs={{0,16},{8,120},{16,32},{24,8},{32,48},{40,24},{48,64},{56,40},{64,... | collective-permute-start | bytes 1572872 | tf_op jit(solution)/shard_map/ppermute | solution.py:276
  57.9 14.0 %all-to-all-start.1 = ((bf16[16,8,384]{2,1,0:T(8,128)(2,1)}), bf16[16,8,384]{2,1,0:T(8,128)(2,1)S(1)}, u32[]{:S(2)}, u32[]{:S(2)}) async-start(bf16[16,8,384]{2,1,0:T(8,128)(2,1)} %pad_maximum_fusion.2), calls=%async_computation.1 | async-start | bytes 196608 | tf_op jit(solution)/shard_map/all_to_all | solution.py:365
  66.4 10.0 %collective-permute-start.8 = (bf16[128,2048]{1,0:T(8,128)(2,1)S(1)}, bf16[128,2048]{1,0:T(8,128)(2,1)S(1)}, u32[]{:S(2)}, u32[]{:S(2)}) collective-permute-start(bf16[128,2048]{1,0:T(8,128)(2,1)S(1)} %get-tuple-element.45), channel_id=1, source_target_pairs={{0,112},{8,24},{16,0},{24,40},{32,16},{40,56},{48,32},{56,72},{64,... | collective-permute-start | bytes 1572872 | tf_op jit(solution)/shard_map/ppermute | solution.py:276
  72.9 14.8 %all-to-all-start.2 = ((bf16[8,32,1408]{2,1,0:T(8,128)(2,1)}), bf16[8,32,1408]{2,1,0:T(8,128)(2,1)S(1)}, u32[]{:S(2)}, u32[]{:S(2)}) async-start(bf16[8,32,1408]{2,1,0:T(8,128)(2,1)} %broadcast_in_dim.5), calls=%async_computation.2 | async-start | bytes 1441792 | tf_op jit(solution)/shard_map/all_to_all | solution.py:392
  77.6 11.0 %collective-permute-start.10 = (bf16[128,2048]{1,0:T(8,128)(2,1)S(1)}, bf16[128,2048]{1,0:T(8,128)(2,1)S(1)}, u32[]{:S(2)}, u32[]{:S(2)}) collective-permute-start(bf16[128,2048]{1,0:T(8,128)(2,1)S(1)} %fusion.1), channel_id=1, source_target_pairs={{0,112},{8,24},{16,0},{24,40},{32,16},{40,56},{48,32},{56,72},{64,... | collective-permute-start | bytes 1572872 | tf_op jit(solution)/shard_map/ppermute | solution.py:276
  78.4 12.3 %collective-permute-start.9 = (bf16[128,2048]{1,0:T(8,128)(2,1)}, bf16[128,2048]{1,0:T(8,128)(2,1)S(1)}, u32[]{:S(2)}, u32[]{:S(2)}) collective-permute-start(bf16[128,2048]{1,0:T(8,128)(2,1)} %get-tuple-element.39), channel_id=1, source_target_pairs={{0,16},{8,120},{16,32},{24,8},{32,48},{40,24},{48,64},{56,40},{64,... | collective-permute-start | bytes 1572872 | tf_op jit(solution)/shard_map/ppermute | solution.py:276
  87.8 6.8 %copy-start.3 = (bf16[256,1024]{1,0:T(8,128)(2,1)S(1)}, bf16[256,1024]{1,0:T(8,128)(2,1)}, u32[]{:S(2)}) copy-start(bf16[256,1024]{1,0:T(8,128)(2,1)} %dec_h.1) | copy-start | bytes 1572868
  92.0 11.7 %copy-start = (s32[2]{0:T(128)S(1)}, s32[2]{0:T(128)}, u32[]{:S(2)}) copy-start(s32[2]{0:T(128)} %pad_add_fusion.core_ref) | copy-start | bytes 28
  92.1 6.8 %collective-permute-start.11 = (bf16[64,2048]{1,0:T(8,128)(2,1)S(1)}, bf16[64,2048]{1,0:T(8,128)(2,1)S(1)}, u32[]{:S(2)}, u32[]{:S(2)}) collective-permute-start(bf16[64,2048]{1,0:T(8,128)(2,1)S(1)} %dynamic-slice_bitcast_fusion.4), channel_id=1, source_target_pairs={{0,128},{128,0},{1,129},{129,1},{2,130},{130,2},{3,131},{131,3},{4... | collective-permute-start | bytes 786440 | tf_op jit(solution)/shard_map/ppermute | solution.py:406
  99.0 4.7 %collective-permute-start.12 = (bf16[32,2048]{1,0:T(8,128)(2,1)S(1)}, bf16[32,2048]{1,0:T(8,128)(2,1)S(1)}, u32[]{:S(2)}, u32[]{:S(2)}) collective-permute-start(bf16[32,2048]{1,0:T(8,128)(2,1)S(1)} %get-tuple-element.49), channel_id=1, source_target_pairs={{0,8},{8,0},{1,9},{9,1},{2,10},{10,2},{3,11},{11,3},{4,12},{12,4},... | collective-permute-start | bytes 393224 | tf_op jit(solution)/shard_map/ppermute | solution.py:410

commit v7 on v6

--- a/solution.py
+++ b/solution.py
@@ -342,7 +342,6 @@
     up = ring_send(first_up, 1)
     down = ring_send(first_down, -1)
     both = (keep.astype(F32) + lax.ppermute(send, "c", SWAP).astype(F32)).astype(BF16)
-    up, _ = tie(up, both)
     up = ring_add(chunk(3, 1), up, 1)
     up, down = tie(up, down)
     over_t = lax.all_to_all(both, TP, 0, 0, tiled=True)

time: 106 us -> 106 us (level)
  no operation moved by 1% of the time
where the time goes in v7:
time: 106 us; the launch traced here: 105 us
  starting transfers between devices  36.6 us (35%)
  waiting for transfers between devices  30.9 us (29%)
  Pallas kernels  16.7 us (16%)
  other arithmetic  14.6 us (14%)
  local copies, waits for them, and re-layouts  4.36 us (4%)
  matrix products  1.1 us (1%)
    pallas_call x1, Pallas kernels, run_block(): pl.pallas_call(block_kernel, in_specs=[pl.BlockSpec(memory_space=pltpu.SM...  15.4 us
    ppermute x8, starting transfers between devices, ring_send(): return lax.ppermute(a, ('z', 'c'), pairs)  13 us
    all_to_all x1, waiting for transfers between devices, on_device(): over_t = lax.all_to_all(both, TP, 0, 0, tiled=True)  12.1 us
    all_to_all x1, waiting for transfers between devices, on_device(): lax.all_to_all(jnp.broadcast_to(mine[None], (NT, *mine.shape)), TP, 0, 0,...  6.13 us
    all_to_all x1, starting transfers between devices, on_device(): over_t = lax.all_to_all(both, TP, 0, 0, tiled=True)  5.04 us
    all_to_all x1, starting transfers between devices, on_device(): small = lax.all_to_all(small, ('yh', 'z'), 0, 0, tiled=True)  4.97 us
    convert_element_type x3, other arithmetic, ring_add(): return (local.astype(F32) + a.astype(F32)).astype(BF16)  4.88 us
    all_to_all x1, waiting for transfers between devices, on_device(): small = lax.all_to_all(small, ('yh', 'z'), 0, 0, tiled=True)  4.09 us
  transfers between devices with their start and end apart: 16, of which 9 were waited for; matrix products, arithmetic and copies ran while one was open for 17% of the time, Pallas kernels for 0%

profile of v7, /device:TPU:1, one launch (start us, length us, event | category | flops | bytes accessed | tf_op | source)
XLA Modules:
  0.0 105.1 jit_solution(6294532429202380636)
XLA Ops:
  0.6 3.3 %collective-permute-start = (bf16[256,1024]{1,0:T(8,128)(2,1)}, bf16[256,1024]{1,0:T(8,128)(2,1)S(1)}, u32[]{:S(2)}, u32[]{:S(2)}) collective-permute-start(bf16[256,1024]{1,0:T(8,128)(2,1)} %tok_own_h.1), channel_id=1, source_target_pairs={{0,8},{8,0},{1,9},{9,1},{2,10},{10,2},{3,11},{11,3},{4,12},{12,4},... | collective-permute-start | bytes 1572872 | tf_op jit(solution)/shard_map/ppermute | solution.py:325
  4.0 0.1 collective-permute-start.1
  4.1 0.6 pad_add_fusion.core_ref
  4.7 1.1 %collective-permute-done.tok_oth_h = bf16[256,1024]{1,0:T(8,128)(2,1)S(1)} collective-permute-done((bf16[256,1024]{1,0:T(8,128)(2,1)}, bf16[256,1024]{1,0:T(8,128)(2,1)S(1)}, u32[]{:S(2)}, u32[]{:S(2)}) %collective-permute-start) | collective-permute-done | bytes 524320 | tf_op jit(solution)/shard_map/ppermute | solution.py:325
  5.7 0.7 collective-permute-done.1.cot_oth_h
  6.5 0.7 copy-done.6
  7.3 15.4 %shard_map.160 = (bf16[8,128,2048]{2,1,0:T(8,128)(2,1)}, bf16[8,32,2432]{2,1,0:T(8,128)(2,1)}, bf16[8,32,2432]{2,1,0:T(8,128)(2,1)}, bf16[64,2048]{1,0:T(8,128)(2,1)}, bf16[64,2048]{1,0:T(8,128)(2,1)}) custom-call(s32[2]{0:T(128)} %pad_add_fusion.core_ref, f32[1,1024]{1,0:T(1,128)} %bitcast.59, bf16[256,1024]{1,0:T(8,128)(2,1)} %tok_own_h.1, ...), custom_call_target="tpu_custom_call" | custom-call | flops 7500000256 | bytes 14000000 | tf_op jit(solution)/shard_map/pallas_call | solution.py:245
  22.6 0.4 collective-permute-start.2
  23.1 0.1 fusion.18
  23.2 4.1 %collective-permute-start.3 = (bf16[64,2048]{1,0:T(8,128)(2,1)}, bf16[64,2048]{1,0:T(8,128)(2,1)}, u32[]{:S(2)}, u32[]{:S(2)}) collective-permute-start(bf16[64,2048]{1,0:T(8,128)(2,1)} %get-tuple-element.29), channel_id=1, source_target_pairs={{0,16},{8,120},{16,32},{24,8},{32,48},{40,24},{48,64},{56,40},{64,... | collective-permute-start | bytes 786440 | tf_op jit(solution)/shard_map/ppermute | solution.py:276
  27.3 1.1 %dynamic-slice_bitcast_fusion.1 = (bf16[64,2048]{1,0:T(8,128)(2,1)S(1)}, bf16[64,2048]{1,0:T(8,128)(2,1)S(1)}) fusion(bf16[8,128,2048]{2,1,0:T(8,128)(2,1)} %get-tuple-element.28, s32[]{:T(128)S(6)} %select_n.66, s32[]{:T(128)S(6)} %select_n.58, s32[]{:T(128)S(6)} %add.206), kind=kLoop, calls=%fused_computation.24 | loop fusion | bytes 1048588 | tf_op jit(solution)/shard_map/slice | solution.py:285
  28.4 1.4 %add_convert_fusion = bf16[8,32,2432]{2,1,0:T(8,128)(2,1)} fusion(bf16[8,32,2432]{2,1,0:T(8,128)(2,1)S(1)} %collective-permute-done.2, bf16[8,32,2432]{2,1,0:T(8,128)(2,1)S(1)} %copy-done.1), kind=kLoop, calls=%fused_computation.1 | loop fusion | flops 2490368 | bytes 3735552 | tf_op jit(solution)/shard_map/convert_element_type | solution.py:344
  29.8 5.0 %all-to-all-start = ((bf16[8,32,2432]{2,1,0:T(8,128)(2,1)}), bf16[8,32,2432]{2,1,0:T(8,128)(2,1)S(1)}, u32[]{:S(2)}, u32[]{:S(2)}) async-start(bf16[8,32,2432]{2,1,0:T(8,128)(2,1)} %add_convert_fusion), calls=%async_computation | async-start | bytes 2490368 | tf_op jit(solution)/shard_map/all_to_all | solution.py:347
  34.8 1.1 %fusion.9 = bf16[64,2048]{1,0:T(8,128)(2,1)S(1)} fusion(bf16[64,2048]{1,0:T(8,128)(2,1)} %collective-permute-done.3, bf16[8,128,2048]{2,1,0:T(8,128)(2,1)} %get-tuple-element.28, s32[]{:T(128)S(6)} %select_n.58), kind=kLoop, calls=%fused_computation.22 | loop fusion | flops 524288 | bytes 786436 | tf_op jit(solution)/shard_map/convert_element_type | solution.py:284
  36.0 2.7 %collective-permute-start.5 = (bf16[128,2048]{1,0:T(8,128)(2,1)S(1)}, bf16[128,2048]{1,0:T(8,128)(2,1)}, u32[]{:S(2)}, u32[]{:S(2)}) collective-permute-start(bf16[128,2048]{1,0:T(8,128)(2,1)S(1)} %pad_maximum_fusion), channel_id=1, source_target_pairs={{0,16},{8,120},{16,32},{24,8},{32,48},{40,24},{48,64},{56,40},{64,... | collective-permute-start | bytes 1572872 | tf_op jit(solution)/shard_map/ppermute | solution.py:276
  38.7 1.1 %fusion.8 = bf16[64,2048]{1,0:T(8,128)(2,1)S(1)} fusion(bf16[64,2048]{1,0:T(8,128)(2,1)} %collective-permute-done.4, bf16[8,128,2048]{2,1,0:T(8,128)(2,1)} %get-tuple-element.28, s32[]{:T(128)S(6)} %select_n.66, s32[]{:T(128)S(6)} %add.206), kind=kLoop, calls=%fused_computation.20 | loop fusion | flops 524288 | bytes 786440 | tf_op jit(solution)/shard_map/convert_element_type | solution.py:284
  39.8 0.8 pad_maximum_fusion.1
  40.6 12.1 %all-to-all-done = bf16[8,32,2432]{2,1,0:T(8,128)(2,1)S(1)} async-done(((bf16[8,32,2432]{2,1,0:T(8,128)(2,1)}), bf16[8,32,2432]{2,1,0:T(8,128)(2,1)S(1)}, u32[]{:S(2)}, u32[]{:S(2)}) %all-to-all-start) | async-done | bytes 1245216 | tf_op jit(solution)/shard_map/all_to_all | solution.py:347
  52.7 0.2 convert_reduce_fusion
  53.0 0.7 pad_maximum_fusion.2
  53.6 1.3 %fusion.3 = bf16[128,2048]{1,0:T(8,128)(2,1)S(1)} fusion(bf16[128,2048]{1,0:T(8,128)(2,1)} %collective-permute-done.5, bf16[8,128,2048]{2,1,0:T(8,128)(2,1)} %get-tuple-element.28, s32[]{:T(128)S(6)} %select_n.65), kind=kLoop, calls=%fused_computation.9 | loop fusion | flops 1048576 | bytes 1572868 | tf_op jit(solution)/shard_map/convert_element_type | solution.py:282
  55.0 2.9 %collective-permute-start.7 = (bf16[128,2048]{1,0:T(8,128)(2,1)S(1)}, bf16[128,2048]{1,0:T(8,128)(2,1)S(1)}, u32[]{:S(2)}, u32[]{:S(2)}) collective-permute-start(bf16[128,2048]{1,0:T(8,128)(2,1)S(1)} %fusion.3), channel_id=1, source_target_pairs={{0,16},{8,120},{16,32},{24,8},{32,48},{40,24},{48,64},{56,40},{64,... | collective-permute-start | bytes 1572872 | tf_op jit(solution)/shard_map/ppermute | solution.py:276
  57.9 5.0 %all-to-all-start.1 = ((bf16[16,8,384]{2,1,0:T(8,128)(2,1)}), bf16[16,8,384]{2,1,0:T(8,128)(2,1)S(1)}, u32[]{:S(2)}, u32[]{:S(2)}) async-start(bf16[16,8,384]{2,1,0:T(8,128)(2,1)} %pad_maximum_fusion.2), calls=%async_computation.1 | async-start | bytes 196608 | tf_op jit(solution)/shard_map/all_to_all | solution.py:364
  62.9 0.2 fusion.13
  63.1 0.9 collective-permute-done.7
  64.1 2.4 %fusion.2 = (bf16[128,2048]{1,0:T(8,128)(2,1)S(1)}, bf16[128,2048]{1,0:T(8,128)(2,1)}) fusion(bf16[128,2048]{1,0:T(8,128)(2,1)S(1)} %collective-permute-done.6, bf16[8,128,2048]{2,1,0:T(8,128)(2,1)} %get-tuple-element.28, s32[]{:T(128)S(6)} %select_n.67, bf16[128,2048]{1,0:T(8,128)(2,1)S(1)} %collective-permute-done.7, s32[]{:T(128)S(6)} %select_n.64), kind=kLoop, calls=%fused_computation.7 | loop fusion | flops 2097152 | bytes 3145736 | tf_op jit(solution)/shard_map/convert_element_type | solution.py:282
  66.4 0.5 collective-permute-start.8
  66.9 0.9 fusion.17
  67.8 4.1 %all-to-all-done.1 = bf16[16,8,384]{2,1,0:T(8,128)(2,1)S(1)} async-done(((bf16[16,8,384]{2,1,0:T(8,128)(2,1)}), bf16[16,8,384]{2,1,0:T(8,128)(2,1)S(1)}, u32[]{:S(2)}, u32[]{:S(2)}) %all-to-all-start.1) | async-done | bytes 98336 | tf_op jit(solution)/shard_map/all_to_all | solution.py:364
  72.0 0.9 broadcast_in_dim.5
  72.9 3.5 %all-to-all-start.2 = ((bf16[8,32,1408]{2,1,0:T(8,128)(2,1)}), bf16[8,32,1408]{2,1,0:T(8,128)(2,1)S(1)}, u32[]{:S(2)}, u32[]{:S(2)}) async-start(bf16[8,32,1408]{2,1,0:T(8,128)(2,1)} %broadcast_in_dim.5), calls=%async_computation.2 | async-start | bytes 1441792 | tf_op jit(solution)/shard_map/all_to_all | solution.py:391
  76.5 1.2 %fusion.1 = bf16[128,2048]{1,0:T(8,128)(2,1)S(1)} fusion(bf16[128,2048]{1,0:T(8,128)(2,1)S(1)} %collective-permute-done.8, bf16[8,128,2048]{2,1,0:T(8,128)(2,1)} %get-tuple-element.28, s32[]{:T(128)S(6)} %select_n.68), kind=kLoop, calls=%fused_computation.5 | loop fusion | flops 1048576 | bytes 1572868 | tf_op jit(solution)/shard_map/convert_element_type | solution.py:282
  77.6 0.8 collective-permute-start.10
  78.4 2.0 %collective-permute-start.9 = (bf16[128,2048]{1,0:T(8,128)(2,1)}, bf16[128,2048]{1,0:T(8,128)(2,1)S(1)}, u32[]{:S(2)}, u32[]{:S(2)}) collective-permute-start(bf16[128,2048]{1,0:T(8,128)(2,1)} %get-tuple-element.37), channel_id=1, source_target_pairs={{0,16},{8,120},{16,32},{24,8},{32,48},{40,24},{48,64},{56,40},{64,... | collective-permute-start | bytes 1572872 | tf_op jit(solution)/shard_map/ppermute | solution.py:276
  80.4 0.6 dynamic-slice_bitcast_fusion.7
  81.0 0.6 pad_maximum_fusion.3
  81.6 6.1 %all-to-all-done.2 = bf16[8,32,1408]{2,1,0:T(8,128)(2,1)S(1)} async-done(((bf16[8,32,1408]{2,1,0:T(8,128)(2,1)}), bf16[8,32,1408]{2,1,0:T(8,128)(2,1)S(1)}, u32[]{:S(2)}, u32[]{:S(2)}) %all-to-all-start.2) | async-done | bytes 720928 | tf_op jit(solution)/shard_map/all_to_all | solution.py:391
  87.8 0.9 slice.106
  88.6 2.1 %collective-permute-done.9 = bf16[128,2048]{1,0:T(8,128)(2,1)S(1)} collective-permute-done((bf16[128,2048]{1,0:T(8,128)(2,1)}, bf16[128,2048]{1,0:T(8,128)(2,1)S(1)}, u32[]{:S(2)}, u32[]{:S(2)}) %collective-permute-start.9) | collective-permute-done | bytes 524320 | tf_op jit(solution)/shard_map/ppermute | solution.py:276
  90.8 1.3 %fusion.6 = bf16[128,2048]{1,0:T(8,128)(2,1)S(1)} fusion(bf16[128,2048]{1,0:T(8,128)(2,1)S(1)} %collective-permute-done.10, bf16[128,2048]{1,0:T(8,128)(2,1)S(1)} %collective-permute-done.9, bf16[8,128,2048]{2,1,0:T(8,128)(2,1)} %get-tuple-element.28, s32[]{:T(128)S(6)} %select_n.63), kind=kLoop, calls=%fused_computation.14 | loop fusion | flops 1572864 | bytes 2097156 | tf_op jit(solution)/shard_map/convert_element_type | solution.py:395
  92.1 2.4 %collective-permute-start.11 = (bf16[64,2048]{1,0:T(8,128)(2,1)S(1)}, bf16[64,2048]{1,0:T(8,128)(2,1)S(1)}, u32[]{:S(2)}, u32[]{:S(2)}) collective-permute-start(bf16[64,2048]{1,0:T(8,128)(2,1)S(1)} %dynamic-slice_bitcast_fusion.4), channel_id=1, source_target_pairs={{0,128},{128,0},{1,129},{129,1},{2,130},{130,2},{3,131},{131,3},{4... | collective-permute-start | bytes 786440 | tf_op jit(solution)/shard_map/ppermute | solution.py:405
  94.5 1.1 %fusion = bf16[256,1024]{1,0:T(8,128)(2,1)} fusion(bf16[256,1024]{1,0:T(8,128)(2,1)S(1)} %copy-done.3, bf16[256,1024]{1,0:T(8,128)(2,1)S(1)} %copy-done.2, bf16[256,1280]{1,0:T(8,128)(2,1)S(1)} %bitcast.55), kind=kOutput, calls=%fused_computation.3 | convolution fusion | flops 135004160 | bytes 1703936 | tf_op jit(solution)/shard_map/dot_general | solution.py:23
  95.6 3.3 %collective-permute-done.11 = bf16[64,2048]{1,0:T(8,128)(2,1)S(1)} collective-permute-done((bf16[64,2048]{1,0:T(8,128)(2,1)S(1)}, bf16[64,2048]{1,0:T(8,128)(2,1)S(1)}, u32[]{:S(2)}, u32[]{:S(2)}) %collective-permute-start.11) | collective-permute-done | bytes 262176 | tf_op jit(solution)/shard_map/ppermute | solution.py:405
  98.9 0.1 fusion.7
  99.0 3.7 %collective-permute-start.12 = (bf16[32,2048]{1,0:T(8,128)(2,1)S(1)}, bf16[32,2048]{1,0:T(8,128)(2,1)S(1)}, u32[]{:S(2)}, u32[]{:S(2)}) collective-permute-start(bf16[32,2048]{1,0:T(8,128)(2,1)S(1)} %get-tuple-element.47), channel_id=1, source_target_pairs={{0,8},{8,0},{1,9},{9,1},{2,10},{10,2},{3,11},{11,3},{4,12},{12,4},... | collective-permute-start | bytes 393224 | tf_op jit(solution)/shard_map/ppermute | solution.py:409
  102.7 0.6 convert_bitcast_fusion
  103.4 0.4 collective-permute-done.12.away
  103.7 1.4 %shard_map.161 = (f32[32,1024]{1,0:T(8,128)}, f32[32,1024]{1,0:T(8,128)}, f32[32,1024]{1,0:T(8,128)}, f32[32,1024]{1,0:T(8,128)}) custom-call(s32[2]{0:T(128)S(1)} %copy-done, bf16[32,2048]{1,0:T(8,128)(2,1)S(1)} %get-tuple-element.48.here, bf16[32,2048]{1,0:T(8,128)(2,1)S(1)} %collective-permute-done.12.away), custom_call_target="tpu_custom_call" | custom-call | tf_op jit(solution)/shard_map/pallas_call | solution.py:305
  (37 shorter events, 0.3 us)
Async XLA Ops:
  0.6 5.1 %collective-permute-start = (bf16[256,1024]{1,0:T(8,128)(2,1)}, bf16[256,1024]{1,0:T(8,128)(2,1)S(1)}, u32[]{:S(2)}, u32[]{:S(2)}) collective-permute-start(bf16[256,1024]{1,0:T(8,128)(2,1)} %tok_own_h.1), channel_id=1, source_target_pairs={{0,8},{8,0},{1,9},{9,1},{2,10},{10,2},{3,11},{11,3},{4,12},{12,4},... | collective-permute-start | bytes 1572872 | tf_op jit(solution)/shard_map/ppermute | solution.py:325
  4.0 2.5 %collective-permute-start.1 = (bf16[256,1024]{1,0:T(8,128)(2,1)}, bf16[256,1024]{1,0:T(8,128)(2,1)S(1)}, u32[]{:S(2)}, u32[]{:S(2)}) collective-permute-start(bf16[256,1024]{1,0:T(8,128)(2,1)} %cot_own_h.1), channel_id=1, source_target_pairs={{0,8},{8,0},{1,9},{9,1},{2,10},{10,2},{3,11},{11,3},{4,12},{12,4},... | collective-permute-start | bytes 1572872 | tf_op jit(solution)/shard_map/ppermute | solution.py:326
  5.7 0.8 copy-start.5
  6.5 0.8 copy-start.6
  7.3 15.8 %copy-start.2 = (bf16[256,1024]{1,0:T(8,128)(2,1)S(1)}, bf16[256,1024]{1,0:T(8,128)(2,1)}, u32[]{:S(2)}) copy-start(bf16[256,1024]{1,0:T(8,128)(2,1)} %tok_own_h.1) | copy-start | bytes 1572868
  22.6 5.8 %copy-start.1 = (bf16[8,32,2432]{2,1,0:T(8,128)(2,1)S(1)}, bf16[8,32,2432]{2,1,0:T(8,128)(2,1)}, u32[]{:S(2)}) copy-start(bf16[8,32,2432]{2,1,0:T(8,128)(2,1)} %get-tuple-element.26) | copy-start | bytes 3735556
  22.6 5.7 %collective-permute-start.2 = (bf16[8,32,2432]{2,1,0:T(8,128)(2,1)}, bf16[8,32,2432]{2,1,0:T(8,128)(2,1)S(1)}, u32[]{:S(2)}, u32[]{:S(2)}) collective-permute-start(bf16[8,32,2432]{2,1,0:T(8,128)(2,1)} %get-tuple-element.27), channel_id=1, source_target_pairs={{0,8},{8,0},{1,9},{9,1},{2,10},{10,2},{3,11},{11,3},{4,12},{12,4},... | collective-permute-start | bytes 3735560 | tf_op jit(solution)/shard_map/ppermute | solution.py:344
  23.2 11.6 %collective-permute-start.3 = (bf16[64,2048]{1,0:T(8,128)(2,1)}, bf16[64,2048]{1,0:T(8,128)(2,1)}, u32[]{:S(2)}, u32[]{:S(2)}) collective-permute-start(bf16[64,2048]{1,0:T(8,128)(2,1)} %get-tuple-element.29), channel_id=1, source_target_pairs={{0,16},{8,120},{16,32},{24,8},{32,48},{40,24},{48,64},{56,40},{64,... | collective-permute-start | bytes 786440 | tf_op jit(solution)/shard_map/ppermute | solution.py:276
  27.3 8.7 %collective-permute-start.4 = (bf16[64,2048]{1,0:T(8,128)(2,1)}, bf16[64,2048]{1,0:T(8,128)(2,1)}, u32[]{:S(2)}, u32[]{:S(2)}) collective-permute-start(bf16[64,2048]{1,0:T(8,128)(2,1)} %get-tuple-element.30), channel_id=1, source_target_pairs={{0,112},{8,24},{16,0},{24,40},{32,16},{40,56},{48,32},{56,72},{64,... | collective-permute-start | bytes 786440 | tf_op jit(solution)/shard_map/ppermute | solution.py:276
  29.8 23.0 %all-to-all-start = ((bf16[8,32,2432]{2,1,0:T(8,128)(2,1)}), bf16[8,32,2432]{2,1,0:T(8,128)(2,1)S(1)}, u32[]{:S(2)}, u32[]{:S(2)}) async-start(bf16[8,32,2432]{2,1,0:T(8,128)(2,1)} %add_convert_fusion), calls=%async_computation | async-start | bytes 2490368 | tf_op jit(solution)/shard_map/all_to_all | solution.py:347
  36.0 17.7 %collective-permute-start.5 = (bf16[128,2048]{1,0:T(8,128)(2,1)S(1)}, bf16[128,2048]{1,0:T(8,128)(2,1)}, u32[]{:S(2)}, u32[]{:S(2)}) collective-permute-start(bf16[128,2048]{1,0:T(8,128)(2,1)S(1)} %pad_maximum_fusion), channel_id=1, source_target_pairs={{0,16},{8,120},{16,32},{24,8},{32,48},{40,24},{48,64},{56,40},{64,... | collective-permute-start | bytes 1572872 | tf_op jit(solution)/shard_map/ppermute | solution.py:276
  40.6 22.3 %copy-start.4 = (f32[1024]{0:T(1024)S(1)}, f32[1024]{0:T(1024)}, u32[]{:S(2)}) copy-start(f32[1024]{0:T(1024)} %param.10) | copy-start | bytes 12292
  40.6 14.3 %collective-permute-start.6 = (bf16[128,2048]{1,0:T(8,128)(2,1)}, bf16[128,2048]{1,0:T(8,128)(2,1)S(1)}, u32[]{:S(2)}, u32[]{:S(2)}) collective-permute-start(bf16[128,2048]{1,0:T(8,128)(2,1)} %pad_maximum_fusion.1), channel_id=1, source_target_pairs={{0,112},{8,24},{16,0},{24,40},{32,16},{40,56},{48,32},{56,72},{64,... | collective-permute-start | bytes 1572872 | tf_op jit(solution)/shard_map/ppermute | solution.py:276
  55.0 9.1 %collective-permute-start.7 = (bf16[128,2048]{1,0:T(8,128)(2,1)S(1)}, bf16[128,2048]{1,0:T(8,128)(2,1)S(1)}, u32[]{:S(2)}, u32[]{:S(2)}) collective-permute-start(bf16[128,2048]{1,0:T(8,128)(2,1)S(1)} %fusion.3), channel_id=1, source_target_pairs={{0,16},{8,120},{16,32},{24,8},{32,48},{40,24},{48,64},{56,40},{64,... | collective-permute-start | bytes 1572872 | tf_op jit(solution)/shard_map/ppermute | solution.py:276
  57.9 14.0 %all-to-all-start.1 = ((bf16[16,8,384]{2,1,0:T(8,128)(2,1)}), bf16[16,8,384]{2,1,0:T(8,128)(2,1)S(1)}, u32[]{:S(2)}, u32[]{:S(2)}) async-start(bf16[16,8,384]{2,1,0:T(8,128)(2,1)} %pad_maximum_fusion.2), calls=%async_computation.1 | async-start | bytes 196608 | tf_op jit(solution)/shard_map/all_to_all | solution.py:364
  66.4 10.0 %collective-permute-start.8 = (bf16[128,2048]{1,0:T(8,128)(2,1)S(1)}, bf16[128,2048]{1,0:T(8,128)(2,1)S(1)}, u32[]{:S(2)}, u32[]{:S(2)}) collective-permute-start(bf16[128,2048]{1,0:T(8,128)(2,1)S(1)} %get-tuple-element.43), channel_id=1, source_target_pairs={{0,112},{8,24},{16,0},{24,40},{32,16},{40,56},{48,32},{56,72},{64,... | collective-permute-start | bytes 1572872 | tf_op jit(solution)/shard_map/ppermute | solution.py:276
  72.9 14.8 %all-to-all-start.2 = ((bf16[8,32,1408]{2,1,0:T(8,128)(2,1)}), bf16[8,32,1408]{2,1,0:T(8,128)(2,1)S(1)}, u32[]{:S(2)}, u32[]{:S(2)}) async-start(bf16[8,32,1408]{2,1,0:T(8,128)(2,1)} %broadcast_in_dim.5), calls=%async_computation.2 | async-start | bytes 1441792 | tf_op jit(solution)/shard_map/all_to_all | solution.py:391
  77.6 11.0 %collective-permute-start.10 = (bf16[128,2048]{1,0:T(8,128)(2,1)S(1)}, bf16[128,2048]{1,0:T(8,128)(2,1)S(1)}, u32[]{:S(2)}, u32[]{:S(2)}) collective-permute-start(bf16[128,2048]{1,0:T(8,128)(2,1)S(1)} %fusion.1), channel_id=1, source_target_pairs={{0,112},{8,24},{16,0},{24,40},{32,16},{40,56},{48,32},{56,72},{64,... | collective-permute-start | bytes 1572872 | tf_op jit(solution)/shard_map/ppermute | solution.py:276
  78.4 12.3 %collective-permute-start.9 = (bf16[128,2048]{1,0:T(8,128)(2,1)}, bf16[128,2048]{1,0:T(8,128)(2,1)S(1)}, u32[]{:S(2)}, u32[]{:S(2)}) collective-permute-start(bf16[128,2048]{1,0:T(8,128)(2,1)} %get-tuple-element.37), channel_id=1, source_target_pairs={{0,16},{8,120},{16,32},{24,8},{32,48},{40,24},{48,64},{56,40},{64,... | collective-permute-start | bytes 1572872 | tf_op jit(solution)/shard_map/ppermute | solution.py:276
  87.8 6.8 %copy-start.3 = (bf16[256,1024]{1,0:T(8,128)(2,1)S(1)}, bf16[256,1024]{1,0:T(8,128)(2,1)}, u32[]{:S(2)}) copy-start(bf16[256,1024]{1,0:T(8,128)(2,1)} %dec_h.1) | copy-start | bytes 1572868
  92.0 11.7 %copy-start = (s32[2]{0:T(128)S(1)}, s32[2]{0:T(128)}, u32[]{:S(2)}) copy-start(s32[2]{0:T(128)} %pad_add_fusion.core_ref) | copy-start | bytes 28
  92.1 6.8 %collective-permute-start.11 = (bf16[64,2048]{1,0:T(8,128)(2,1)S(1)}, bf16[64,2048]{1,0:T(8,128)(2,1)S(1)}, u32[]{:S(2)}, u32[]{:S(2)}) collective-permute-start(bf16[64,2048]{1,0:T(8,128)(2,1)S(1)} %dynamic-slice_bitcast_fusion.4), channel_id=1, source_target_pairs={{0,128},{128,0},{1,129},{129,1},{2,130},{130,2},{3,131},{131,3},{4... | collective-permute-start | bytes 786440 | tf_op jit(solution)/shard_map/ppermute | solution.py:405
  99.0 4.7 %collective-permute-start.12 = (bf16[32,2048]{1,0:T(8,128)(2,1)S(1)}, bf16[32,2048]{1,0:T(8,128)(2,1)S(1)}, u32[]{:S(2)}, u32[]{:S(2)}) collective-permute-start(bf16[32,2048]{1,0:T(8,128)(2,1)S(1)} %get-tuple-element.47), channel_id=1, source_target_pairs={{0,8},{8,0},{1,9},{9,1},{2,10},{10,2},{3,11},{11,3},{4,12},{12,4},... | collective-permute-start | bytes 393224 | tf_op jit(solution)/shard_map/ppermute | solution.py:409
